TPU v7x, 128 devices: a whole 4x4x4 slice. The times are simulated.
128 devices in a mesh: dp: 8 (over z_hi, y), tp: 16 (over x, z_lo, core).
Axes of the slice: x: 4, y: 4, z: 4 (z_hi: 2, z_lo: 2; z = z_hi * 2 + z_lo), core: 2. Of those that a mesh axis runs over, the one named last changes fastest.
Arguments:
- residual: bfloat16 [2, 1024, 7168], P(None, ('dp', 'tp')), may hold values from -3 to 3
- queries: bfloat16 [2, 1024, 64, 576], P(None, ('dp', 'tp')), may hold values from -28 to 28
- latent_cache: bfloat16 [2, 1024, 256, 576], P(None, ('dp', 'tp')), may hold values from -6 to 6
- new_latent: bfloat16 [2, 1024, 576], P(None, ('dp', 'tp')), may hold values from -6 to 6
- lengths: int32 [2, 1024], P(None, ('dp', 'tp')), may hold values from 1 to 256, as said below
- positions: int32 [2, 1024], P(None, ('dp', 'tp')), may hold values from 0 to 8191
- latent_value_weight: bfloat16 [64, 512, 128], P('tp'), may hold values from -3 to 3
- w_out: bfloat16 [8192, 7168], P('tp'), may hold values from -0.0625 to 0.0625
- norm_gain: bfloat16 [7168], replicated, may hold values from 0.099609375 to 1.8984375
- gate_weight: bfloat16 [7168, 10240], P(None, 'tp'), may hold values from -0.0625 to 0.0625
- up_weight: bfloat16 [7168, 10240], P(None, 'tp'), may hold values from -0.0625 to 0.0625
Outputs:
- after_attention: bfloat16 [2, 1024, 7168], P(None, ('dp', 'tp'))
- activation: bfloat16 [2, 1024, 10240], P(None, 'dp', 'tp')
Inputs may be any that keep to these rules, and one draw needn't show every extreme that they name: `lengths`: in each micro-batch one row holds exactly 256 cached tokens and another exactly 1.
All inputs are finite; a program needn't handle non-finite values.
Results may differ from a plain program's by a relative error of at most 0.039.
Values may be sent and summed in bfloat16 or wider, within the bound.
No kernel may reach another device: no remote copies, remote signals or barrier semaphores. Data moves between devices by JAX's collectives and lax.ppermute only.
A program may use at most 128 MiB of HBM per device.

v0:
```python
import jax
import jax.numpy as jnp
from jax import lax
from jax.sharding import PartitionSpec as P

score_scale = 192.0 ** (-0.5)
neg_large = -1e30


def rotary(values, position):
    half_width = values.shape[-1] // 2
    exponent = jnp.arange(half_width, dtype=jnp.float32) * (2.0 / values.shape[-1])
    frequency = 10000.0 ** (-exponent)
    angles = position.astype(jnp.float32)[..., None] * frequency
    cosine = jnp.cos(angles)
    sine_part = jnp.sin(angles)
    leading = values[..., :half_width]
    trailing = values[..., half_width:]
    return jnp.concatenate(
        [leading * cosine - trailing * sine_part, leading * sine_part + trailing * cosine], axis=-1
    )


def attend_span(query_rows, key_rows, valid_len, block_len, latent):
    batch_rows, head_count = (query_rows.shape[0], query_rows.shape[1])
    blocks_due = (jnp.max(valid_len) + block_len - 1) // block_len

    def block_step(number, carried):
        running, totals, context = carried
        offset = number * block_len
        key_block = lax.dynamic_slice_in_dim(key_rows, offset, block_len, 1)
        scores = (
            jnp.einsum("bhk,btk->bht", query_rows, key_block, preferred_element_type=jnp.float32)
            * score_scale
        )
        visible = (offset + jnp.arange(block_len))[None, None, :] < valid_len[:, None, None]
        scores = jnp.where(visible, scores, neg_large)
        updated = jnp.maximum(running, jnp.max(scores, axis=-1))
        weights = jnp.where(visible, jnp.exp(scores - updated[..., None]), 0.0)
        factor = jnp.exp(running - updated)
        totals = totals * factor + jnp.sum(weights, axis=-1)
        context = context * factor[..., None] + jnp.einsum(
            "bht,btk->bhk",
            weights.astype(jnp.bfloat16),
            key_block[..., :latent],
            preferred_element_type=jnp.float32,
        )
        return (updated, totals, context)

    start_state = (
        jnp.full((batch_rows, head_count), neg_large, jnp.float32),
        jnp.zeros((batch_rows, head_count), jnp.float32),
        jnp.zeros((batch_rows, head_count, latent), jnp.float32),
    )
    return lax.fori_loop(0, blocks_due, block_step, start_state)


def join_parts(first_part, second_part):
    top_first, sum_first, context_first = first_part
    top_second, sum_second, context_second = second_part
    joined = jnp.maximum(top_first, top_second)
    scale_first = jnp.exp(top_first - joined)
    scale_second = jnp.exp(top_second - joined)
    return (
        joined,
        sum_first * scale_first + sum_second * scale_second,
        context_first * scale_first[..., None] + context_second * scale_second[..., None],
    )


def shards(
    residual,
    queries,
    latent_cache,
    new_latent,
    lengths,
    positions,
    latent_value_weight,
    w_out,
    norm_gain,
    gate_weight,
    up_weight,
):
    latent = latent_value_weight.shape[1]
    query_rope = rotary(queries[..., latent:].astype(jnp.float32), positions[..., None]).astype(
        jnp.bfloat16
    )
    query_all = jnp.concatenate([queries[..., :latent], query_rope], axis=-1)
    key_rope = rotary(new_latent[..., latent:].astype(jnp.float32), positions).astype(jnp.bfloat16)
    new_key = jnp.concatenate([new_latent[..., :latent], key_rope], axis=-1)
    flat_query = query_all.reshape((-1,) + query_all.shape[2:])
    flat_cache = latent_cache.reshape((-1,) + latent_cache.shape[2:])
    flat_new = new_key.reshape(-1, new_key.shape[-1])
    flat_len = lengths.reshape(-1)
    cache_len = latent_cache.shape[2]
    half_len = cache_len // 2
    span_part = attend_span(flat_query, flat_cache, flat_len, half_len, latent)
    own_score = (
        jnp.einsum("bhk,bk->bh", flat_query, flat_new, preferred_element_type=jnp.float32)
        * score_scale
    )
    new_part = (
        own_score,
        jnp.ones_like(own_score),
        jnp.broadcast_to(
            flat_new[:, None, :latent].astype(jnp.float32), own_score.shape + (latent,)
        ),
    )
    running, totals, context = join_parts(span_part, new_part)
    attended_latent = (
        (context / totals[..., None]).astype(jnp.bfloat16).reshape(queries.shape[:3] + (latent,))
    )
    value_matrix_rows = jnp.einsum(
        "sqwy,wyd->sqwd",
        lax.all_to_all(attended_latent, "tp", split_axis=2, concat_axis=1, tiled=True),
        latent_value_weight,
        preferred_element_type=jnp.float32,
    ).astype(jnp.bfloat16)
    flat_value = value_matrix_rows.reshape(value_matrix_rows.shape[:2] + (-1,))
    head_terms = jnp.einsum("mrj,jd->mrd", flat_value, w_out, preferred_element_type=jnp.float32)
    gain_row = norm_gain.astype(jnp.float32)
    summed = lax.psum_scatter(
        head_terms.astype(jnp.bfloat16), "tp", scatter_dimension=1, tiled=True
    ).astype(jnp.float32)
    after_attention = (residual.astype(jnp.float32) + summed).astype(jnp.bfloat16)
    widened = after_attention.astype(jnp.float32)
    mean_square = jnp.mean(widened * widened, axis=-1, keepdims=True)
    row_group_block = lax.all_gather(
        (widened * lax.rsqrt(mean_square + 1e-06) * gain_row).astype(jnp.bfloat16),
        "tp",
        axis=1,
        tiled=True,
    )
    gate_activation = jnp.einsum(
        "nqb,bj->nqj", row_group_block, gate_weight, preferred_element_type=jnp.float32
    )
    up_projected = jnp.einsum(
        "nqb,bj->nqj", row_group_block, up_weight, preferred_element_type=jnp.float32
    )
    activation = (jax.nn.silu(gate_activation) * up_projected).astype(jnp.bfloat16)
    return (after_attention, activation)


def solution(mesh):
    return jax.shard_map(
        shards,
        mesh=mesh,
        in_specs=(
            P(None, ("dp", "tp"), None),
            P(None, ("dp", "tp"), None, None),
            P(None, ("dp", "tp"), None, None),
            P(None, ("dp", "tp"), None),
            P(None, ("dp", "tp")),
            P(None, ("dp", "tp")),
            P("tp", None, None),
            P("tp", None),
            P(),
            P(None, "tp"),
            P(None, "tp"),
        ),
        out_specs=(P(None, ("dp", "tp"), None), P(None, "dp", "tp")),
        check_vma=False,
    )
```

profile of v0, /device:TPU:1, one launch (start us, length us, event | category | flops | bytes accessed | tf_op | source)
XLA Modules:
  0.0 189.5 jit_solution(17757839697886193860)
XLA Ops:
  7.3 1.4 reduce_max.18
  9.4 1.0 slice_convert_fusion
  10.4 0.1 lt.29
  10.5 0.1 subtract_convert_fusion.1
  10.6 0.2 subtract_convert_fusion
  10.9 1.3 pad_maximum_fusion
  12.2 0.2 broadcast_in_dim.50
  12.5 11.9 %while.15 = (s32[]{:T(128)}, f32[16,64]{1,0:T(8,128)S(1)}, f32[16,64]{1,0:T(8,128)S(1)}, f32[16,64,512]{2,1,0:T(8,128)S(1)}, s32[]{:T(128)}, /*index=5*/s32[2,8]...) while((s32[]{:T(128)}, f32[16,64]{1,0:T(8,128)S(1)}, ...), condition=%wide.wide.region_4.5_spmd, body=%wide.wide.region_1.4_spmd.sunk | while | flops 287445120 | bytes 11609335 | solution.py:55
  12.6 2.8 %fusion.69 = (f32[16,64]{1,0:T(8,128)S(1)}, f32[16,64,128]{2,1,0:T(8,128)S(1)}) fusion(bf16[16,64,576]{2,1,0:T(8,128)(2,1)} %get-tuple-element.217, bf16[16,256,576]{1,2,0:T(8,128)(2,1)} %get-tuple-element.216, s32[]{:T(128)S(6)} %select_n.36, pred[16,128]{1,0:T(8,128)(4,1)S(1)} %broadcast_compare_fusion.3), kind=kOutput, calls=%fused_computation.63.clone.clone.1 | convolution fusion | flops 151387136 | bytes 4200452 | tf_op jit(solution)/shard_map/while/body/bhk,btk->bht/dot_general | solution.py:33
  15.4 0.4 fusion.70
  15.8 2.6 %multiply_add_fusion.8 = f32[16,64,512]{2,1,0:T(8,128)S(1)} fusion(f32[16,64,512]{2,1,0:T(8,128)S(1)} %get-tuple-element.200, bf16[16,256,576]{1,2,0:T(8,128)(2,1)} %get-tuple-element.216, s32[]{:T(128)S(6)} %select_n.36, f32[16,64]{1,0:T(8,128)S(1)} %get-tuple-element.183, f32[16,64,128]{2,1,0:T(8,128)S(1)} %get-tuple-element.181, ...), kind=kOutput, calls=%fused_computation.4.clone.clone.1 | convolution fusion | flops 135659520 | bytes 6825988 | tf_op jit(solution)/shard_map/while/body/bht,btk->bhk/dot_general | solution.py:42
  18.6 2.8 %fusion.69 = (f32[16,64]{1,0:T(8,128)S(1)}, f32[16,64,128]{2,1,0:T(8,128)S(1)}) fusion(bf16[16,64,576]{2,1,0:T(8,128)(2,1)} %get-tuple-element.217, bf16[16,256,576]{1,2,0:T(8,128)(2,1)} %get-tuple-element.216, s32[]{:T(128)S(6)} %select_n.36, pred[16,128]{1,0:T(8,128)(4,1)S(1)} %broadcast_compare_fusion.3), kind=kOutput, calls=%fused_computation.63.clone.clone.1 | convolution fusion | flops 151387136 | bytes 4200452 | tf_op jit(solution)/shard_map/while/body/bhk,btk->bht/dot_general | solution.py:33
  21.4 0.4 fusion.70
  21.8 2.6 %multiply_add_fusion.8 = f32[16,64,512]{2,1,0:T(8,128)S(1)} fusion(f32[16,64,512]{2,1,0:T(8,128)S(1)} %get-tuple-element.200, bf16[16,256,576]{1,2,0:T(8,128)(2,1)} %get-tuple-element.216, s32[]{:T(128)S(6)} %select_n.36, f32[16,64]{1,0:T(8,128)S(1)} %get-tuple-element.183, f32[16,64,128]{2,1,0:T(8,128)S(1)} %get-tuple-element.181, ...), kind=kOutput, calls=%fused_computation.4.clone.clone.1 | convolution fusion | flops 135659520 | bytes 6825988 | tf_op jit(solution)/shard_map/while/body/bht,btk->bhk/dot_general | solution.py:42
  24.4 0.1 fusion.47
  24.5 1.8 fusion.42
  26.4 0.5 divide_convert_fusion
  26.9 0.6 copy.27
  27.5 22.2 %all_to_all.18 = bf16[2,8,64,512]{3,1,0,2:T(8,128)(2,1)S(1)} all-to-all(bf16[2,8,64,512]{3,1,0,2:T(8,128)(2,1)S(1)} %copy.27), channel_id=1, replica_groups=mesh['dp'=8,'tp'=16] {'tp'}, dimensions={2} | all-to-all | bytes 2097152 | tf_op jit(solution)/shard_map/all_to_all | solution.py:115
  49.7 0.5 fusion.35
  50.3 5.2 %convolution_convert_fusion = bf16[2,128,7168]{2,1,0:T(8,128)(2,1)S(1)} fusion(bf16[2,128,512]{1,2,0:T(8,128)(2,1)S(1)} %bitcast.56, bf16[512,7168]{1,0:T(8,128)(2,1)} %param.20), kind=kOutput, calls=%fused_computation.25 | convolution fusion | flops 1880883200 | bytes 11272192 | tf_op jit(solution)/shard_map/mrj,jd->mrd/dot_general | solution.py:120
  55.4 3.8 %copy.41 = bf16[2,128,7168]{2,0,1:T(2,128)(2,1)S(1)} copy(bf16[2,128,7168]{2,1,0:T(8,128)(2,1)S(1)} %convolution_convert_fusion) | data formatting | bytes 7340032
  59.2 2.7 %copy.43 = bf16[16,8,2,7168]{3,1,2,0:T(8,128)(2,1)} copy(bf16[16,8,2,7168]{3,2,1,0:T(2,128)(2,1)S(1)} %bitcast.54) | data formatting | bytes 7340032
  61.9 0.2 all-gather.2.cloned.1.call-start
  62.2 0.5 copy-done.4
  62.6 63.2 %reduce-scatter.4.cloned.1.call-done = bf16[8,14336]{1,0:T(8,128)(2,1)} async-done(((bf16[128,14336]{1,0:T(8,128)(2,1)}), bf16[8,14336]{1,0:T(8,128)(2,1)}) %reduce-scatter.4.cloned.1.call-update) | async-done | bytes 229392
  125.8 1.1 reshape.110
  127.0 0.2 fusion.39
  127.2 0.8 fusion.41
  128.0 39.4 %all-gather.2.cloned.1.call-done = bf16[2,128,7168]{2,1,0:T(8,128)(2,1)} async-done(((bf16[2,8,7168]{2,1,0:T(8,128)(2,1)}), bf16[2,128,7168]{2,1,0:T(8,128)(2,1)}) %all-gather.2.cloned.1.call-update) | async-done | bytes 3670032 | tf_op jit(solution)/shard_map/all_gather | solution.py:128
  167.4 7.9 %fusion.26 = f32[2,128,640]{2,1,0:T(8,128)S(1)} fusion(bf16[2,128,7168]{2,1,0:T(8,128)(2,1)} %all-gather.2.cloned.1.call-done, bf16[7168,640]{1,0:T(8,128)(2,1)} %param.22), kind=kOutput, calls=%fused_computation.23 | convolution fusion | flops 2348810240 | bytes 13500416 | tf_op jit(solution)/shard_map/nqb,bj->nqj/dot_general | solution.py:134
  175.3 7.4 %fusion.32 = bf16[2,128,640]{2,1,0:T(8,128)(2,1)} fusion(bf16[2,128,7168]{2,1,0:T(8,128)(2,1)S(1)} %copy-done.7, bf16[7168,640]{1,0:T(8,128)(2,1)} %param.23, f32[2,128,640]{2,1,0:T(8,128)S(1)} %fusion.26), kind=kOutput, calls=%fused_computation.30 | convolution fusion | flops 2349793280 | bytes 13828096 | tf_op jit(solution)/shard_map/nqb,bj->nqj/dot_general | solution.py:137
  (42 shorter events, 0.4 us)
Async XLA Ops:
  7.2 42.6 %copy-start = (bf16[4,512,128]{2,1,0:T(8,128)(2,1)S(1)}, bf16[4,512,128]{2,1,0:T(8,128)(2,1)}, u32[]{:S(2)}) copy-start(bf16[4,512,128]{2,1,0:T(8,128)(2,1)} %param.19) | copy-start | bytes 1572868
  7.2 3.2 %copy-start.6 = (s32[2,8]{1,0:T(2,128)S(1)}, s32[2,8]{1,0:T(2,128)}, u32[]{:S(2)}) copy-start(s32[2,8]{1,0:T(2,128)} %param.17) | copy-start | bytes 196
  7.2 3.7 %slice-start = ((bf16[2,8,64,576]{3,2,1,0:T(8,128)(2,1)}), bf16[2,8,64,512]{3,2,1,0:T(8,128)(2,1)S(1)}, s32[]{:S(2)}) async-start(bf16[2,8,64,576]{3,2,1,0:T(8,128)(2,1)} %param.14), calls=%async_computation.4 | async-start | bytes 2097152 | tf_op jit(solution)/shard_map/slice | solution.py:88
  7.2 3.3 %copy-start.3 = (bf16[2,8,576]{2,1,0:T(8,128)(2,1)S(1)}, bf16[2,8,576]{2,1,0:T(8,128)(2,1)}, u32[]{:S(2)}) copy-start(bf16[2,8,576]{2,1,0:T(8,128)(2,1)} %param.16) | copy-start | bytes 55300
  7.2 3.3 %copy-start.5 = (s32[2,8]{1,0:T(2,128)S(1)}, s32[2,8]{1,0:T(2,128)}, u32[]{:S(2)}) copy-start(s32[2,8]{1,0:T(2,128)} %param.18) | copy-start | bytes 196
  7.2 118.6 %reduce-scatter.4.cloned.1.call-start = ((), (), s32[]{:S(2)}) async-start(), calls=%async_computation.3 | async-start | bytes 3899392
  12.5 12.0 %slice-start.1 = ((bf16[2,8,576]{2,1,0:T(8,128)(2,1)}), bf16[2,8,512]{2,1,0:T(8,128)(2,1)S(1)}, s32[]{:S(2)}) async-start(bf16[2,8,576]{2,1,0:T(8,128)(2,1)} %param.16), calls=%async_computation.5 | async-start | bytes 32768 | tf_op jit(solution)/shard_map/slice | solution.py:90
  61.9 0.7 copy-start.4
  61.9 65.0 %copy-start.2 = (bf16[2,8,7168]{2,1,0:T(8,128)(2,1)S(1)}, bf16[2,8,7168]{2,1,0:T(8,128)(2,1)}, u32[]{:S(2)}) copy-start(bf16[2,8,7168]{2,1,0:T(8,128)(2,1)} %param.13) | copy-start | bytes 688132
  61.9 105.5 %all-gather.2.cloned.1.call-start = ((), (), s32[]{:S(2)}) async-start(), calls=%async_computation.2 | async-start | bytes 3899392 | tf_op jit(solution)/shard_map/all_gather | solution.py:128
  127.2 48.1 %copy-start.1 = (bf16[2,8,7168]{2,1,0:T(8,128)(2,1)}, bf16[2,8,7168]{2,1,0:T(8,128)(2,1)S(1)}, u32[]{:S(2)}) copy-start(bf16[2,8,7168]{2,1,0:T(8,128)(2,1)S(1)} %get-tuple-element.69) | copy-start | bytes 688132
  167.4 7.9 %copy-start.7 = (bf16[2,128,7168]{2,1,0:T(8,128)(2,1)S(1)}, bf16[2,128,7168]{2,1,0:T(8,128)(2,1)}, u32[]{:S(2)}) copy-start(bf16[2,128,7168]{2,1,0:T(8,128)(2,1)} %all-gather.2.cloned.1.call-done) | copy-start | bytes 11010052
Sparse Core Ops, SparseCore 0:
  62.1 63.7 reduce-scatter.3
  128.1 39.2 all-gather.1
where the time goes:
time: 190 us
  waiting for transfers between devices  103 us (54%)
  matrix products  33.5 us (18%)
  blocking collectives  22.2 us (12%)
  between operations  14.9 us (8%)
  local copies, waits for them, and re-layouts  9.02 us (5%)
  other arithmetic  6.76 us (4%)
    unnamed x3, waiting for transfers between devices  63.2 us
    all_gather x1, waiting for transfers between devices, shards(): lax.all_gather((widened * lax.rsqrt(mean_square + 1e-06) * gain_row).asty...  39.4 us
    all_to_all x1, blocking collectives, shards(): lax.all_to_all(attended_latent, 'tp', split_axis=2, concat_axis=1, tiled=...  22.2 us
    unnamed x19, local copies, waits for them, and re-layouts  8.07 us
    dot_general x1, matrix products, shards(): jnp.einsum('nqb,bj->nqj', row_group_block, gate_weight, preferred_element...  7.87 us
    dot_general x1, matrix products, shards(): jnp.einsum('nqb,bj->nqj', row_group_block, up_weight, preferred_element_t...  7.35 us
    dot_general x2, matrix products, block_step(): jnp.einsum('bhk,btk->bht', query_rows, key_block, preferred_element_type=...  5.56 us
    dot_general x2, matrix products, block_step(): jnp.einsum('bht,btk->bhk', weights.astype(jnp.bfloat16), key_block[..., :...  5.23 us
  transfers between devices with their start and end apart: 2, of which 2 were waited for; matrix products, arithmetic and copies ran while one was open for 0% of the time, Pallas kernels for 0%

commit v1 on v0

v1 whole, which is shorter than its diff:
```python
import functools

import jax
import jax.numpy as jnp
import numpy as np
from jax import lax
from jax.experimental import pallas as pl
from jax.experimental.pallas import tpu as pltpu
from jax.sharding import PartitionSpec as P

score_scale = 192.0 ** (-0.5)
neg_large = -1e30
f32 = jnp.float32
bf16 = jnp.bfloat16
vmem_limit = 48 * 1024 * 1024
x_size, z_size, core_size = 4, 2, 2
tp_size = x_size * z_size * core_size


def tp_perm(dx=0, dz=0, dc=0):
    pairs = []
    for i in range(tp_size):
        x, z, c = i // 4, (i // 2) % 2, i % 2
        pairs.append((i, ((x + dx) % 4) * 4 + (z ^ dz) * 2 + (c ^ dc)))
    return pairs


def send(value, dx=0, dz=0, dc=0):
    return lax.ppermute(value, "tp", tp_perm(dx, dz, dc))


def rotary_tables(positions, rope):
    half = rope // 2
    exponent = jnp.arange(half, dtype=f32) * (2.0 / rope)
    angles = positions.astype(f32)[..., None] * (10000.0 ** (-exponent))
    cosine, sine = jnp.cos(angles), jnp.sin(angles)
    return jnp.concatenate([cosine, cosine, -sine, sine], axis=-1)


def attention_kernel(rows, latent, len_ref, q_ref, c_ref, n_ref, t_ref, out_ref, held):
    step = pl.program_id(0)
    rope = q_ref.shape[-1] - latent
    slots = c_ref.shape[1]
    half = rope // 2

    def turn(values, cosine, sine):
        swapped = jnp.concatenate([values[:, half:], values[:, :half]], axis=-1)
        return (values * cosine + swapped * sine).astype(bf16)

    for r in range(rows):
        row = step * rows + r
        length = len_ref[row]
        table = t_ref[r : r + 1, :]
        cosine, sine = table[:, :rope], table[:, rope:]
        q_lat = q_ref[r, :, :latent]
        q_rope = turn(q_ref[r, :, latent:].astype(f32), cosine, sine)
        n_lat = n_ref[r : r + 1, :latent].astype(f32)
        n_rope = turn(n_ref[r : r + 1, latent:].astype(f32), cosine, sine).astype(f32)
        dims = (((1,), (1,)), ((), ()))
        scores = lax.dot_general(q_lat, c_ref[r, :, :latent], dims, preferred_element_type=f32)
        scores += lax.dot_general(q_rope, c_ref[r, :, latent:], dims, preferred_element_type=f32)
        own = jnp.sum(q_lat.astype(f32) * n_lat, axis=-1, keepdims=True)
        own += jnp.sum(q_rope.astype(f32) * n_rope, axis=-1, keepdims=True)
        own = own * score_scale
        visible = lax.broadcasted_iota(jnp.int32, scores.shape, 1) < length
        scores = jnp.where(visible, scores * score_scale, neg_large)
        top = jnp.maximum(jnp.max(scores, axis=-1, keepdims=True), own)
        weights = jnp.where(visible, jnp.exp(scores - top), 0.0)
        own_weight = jnp.exp(own - top)
        total = jnp.sum(weights, axis=-1, keepdims=True) + own_weight
        context = jnp.dot(weights.astype(bf16), c_ref[r, :, :latent], preferred_element_type=f32)
        context += own_weight.astype(bf16).astype(f32) * n_lat
        held[:, row, :] = context * (1.0 / total)

    @pl.when(step == pl.num_programs(0) - 1)
    def _():
        out_ref[...] = held[...].astype(bf16)


def attention(queries, cache, new_latent, lengths, tables, latent):
    count, heads, width = queries.shape
    slots = cache.shape[1]
    rows = 8
    return pl.pallas_call(
        functools.partial(attention_kernel, rows, latent),
        grid_spec=pltpu.PrefetchScalarGridSpec(
            num_scalar_prefetch=1,
            grid=(count // rows,),
            in_specs=[
                pl.BlockSpec((rows, heads, width), lambda i, n: (i, 0, 0)),
                pl.BlockSpec((rows, slots, width), lambda i, n: (i, 0, 0)),
                pl.BlockSpec((rows, width), lambda i, n: (i, 0)),
                pl.BlockSpec((rows, tables.shape[1]), lambda i, n: (i, 0)),
            ],
            out_specs=pl.BlockSpec((heads, count, latent), lambda i, n: (0, 0, 0)),
            scratch_shapes=[pltpu.VMEM((heads, count, latent), f32)],
        ),
        out_shape=jax.ShapeDtypeStruct((heads, count, latent), bf16),
        compiler_params=pltpu.CompilerParams(vmem_limit_bytes=vmem_limit),
        cost_estimate=pl.CostEstimate(
            flops=4 * count * heads * width * slots,
            bytes_accessed=2 * count * width * (heads + slots),
            transcendentals=count * heads * slots,
        ),
        name="attention",
    )(lengths, queries, cache, new_latent, tables)


def value_kernel(block, order_ref, a_ref, v_ref, w_ref, send_ref, keep_ref, value_ref, gathered):
    step = pl.program_id(0)
    heads, width = v_ref.shape[0], v_ref.shape[2]

    @pl.when(step == 0)
    def _():
        for p in range(tp_size):
            gathered[:, p * block : (p + 1) * block, :] = a_ref[order_ref[p]]
        for h in range(heads):
            value_ref[:, h * width : (h + 1) * width] = jnp.dot(
                gathered[h], v_ref[h], preferred_element_type=f32
            ).astype(bf16)

    project(value_ref[...], w_ref, send_ref, keep_ref, block, True)


def project(values, w_ref, send_ref, keep_ref, block, x_major):
    half = values.shape[0] // 2
    if x_major:
        parts = []
        for c in range(core_size):
            for px in range(x_size):
                for pz in range(z_size):
                    at = ((c * z_size + pz) * x_size + px) * block
                    parts.append(values[at : at + block])
        values = jnp.concatenate(parts, axis=0)
    result = jnp.dot(values, w_ref[...], preferred_element_type=f32).astype(bf16)
    keep_ref[...] = result[:half]
    send_ref[...] = result[half:]


def out_kernel(block, v_ref, w_ref, send_ref, keep_ref):
    project(v_ref[...], w_ref, send_ref, keep_ref, block, False)


def value_and_out(order, arrived, value_weight, w_out, columns, tile):
    sources, heads, block, latent = arrived.shape
    rows = sources * block
    depth = w_out.shape[0]
    return pl.pallas_call(
        functools.partial(value_kernel, block),
        grid_spec=pltpu.PrefetchScalarGridSpec(
            num_scalar_prefetch=1,
            grid=(columns // tile,),
            in_specs=[
                pl.BlockSpec(arrived.shape, lambda i, o: (0, 0, 0, 0)),
                pl.BlockSpec(value_weight.shape, lambda i, o: (0, 0, 0)),
                pl.BlockSpec((depth, tile), lambda i, o: (0, i)),
            ],
            out_specs=[
                pl.BlockSpec((rows // 2, tile), lambda i, o: (0, i)),
                pl.BlockSpec((rows // 2, tile), lambda i, o: (0, i)),
                pl.BlockSpec((rows, depth), lambda i, o: (0, 0)),
            ],
            scratch_shapes=[pltpu.VMEM((heads, rows, latent), bf16)],
        ),
        out_shape=[
            jax.ShapeDtypeStruct((rows // 2, columns), bf16),
            jax.ShapeDtypeStruct((rows // 2, columns), bf16),
            jax.ShapeDtypeStruct((rows, depth), bf16),
        ],
        compiler_params=pltpu.CompilerParams(vmem_limit_bytes=vmem_limit),
        cost_estimate=pl.CostEstimate(
            flops=2 * rows * depth * (columns + latent),
            bytes_accessed=2 * depth * columns,
            transcendentals=0,
        ),
        name="value_out",
    )(order, arrived, value_weight, w_out)


def out_only(values, w_out, block, start, columns, tile):
    rows, depth = values.shape
    first = start // tile
    return pl.pallas_call(
        functools.partial(out_kernel, block),
        grid=(columns // tile,),
        in_specs=[
            pl.BlockSpec((rows, depth), lambda i: (0, 0)),
            pl.BlockSpec((depth, tile), lambda i: (0, first + i)),
        ],
        out_specs=[
            pl.BlockSpec((rows // 2, tile), lambda i: (0, i)),
            pl.BlockSpec((rows // 2, tile), lambda i: (0, i)),
        ],
        out_shape=[
            jax.ShapeDtypeStruct((rows // 2, columns), bf16),
            jax.ShapeDtypeStruct((rows // 2, columns), bf16),
        ],
        compiler_params=pltpu.CompilerParams(vmem_limit_bytes=vmem_limit),
        cost_estimate=pl.CostEstimate(
            flops=2 * rows * depth * columns, bytes_accessed=2 * depth * columns, transcendentals=0
        ),
        name="out_proj",
    )(values, w_out)


def gated_kernel(layout, first, last, width, *refs):
    pieces = 1 + max(p for p, _ in layout)
    refs = list(refs)
    order_ref = refs.pop(0)
    x_refs = [refs.pop(0) for _ in range(pieces)]
    gain_ref, gate_ref, up_ref = refs.pop(0), refs.pop(0), refs.pop(0)
    if not first:
        acc_in, square_in = refs.pop(0), refs.pop(0)
    if last:
        out_ref, acc_ref, square_ref, ordered = refs
    else:
        acc_ref, square_ref = refs
    step = pl.program_id(0)
    block = 16

    @pl.when(step == 0)
    def _():
        if first:
            acc_ref[...] = jnp.zeros_like(acc_ref)
            square_ref[...] = jnp.zeros_like(square_ref)
        else:
            acc_ref[...] = acc_in[...]
            square_ref[...] = square_in[...]

    wide = jnp.concatenate([x_refs[p][at : at + block] for p, at in layout], axis=0).astype(f32)
    squares = wide * wide
    lanes = square_ref.shape[1]
    total = square_ref[...]
    for k in range(0, wide.shape[1], lanes):
        total += squares[:, k : k + lanes]
    square_ref[...] = total
    scaled = (wide * gain_ref[...].astype(f32)).astype(bf16)
    weights = jnp.concatenate([gate_ref[...], up_ref[...]], axis=1)
    acc_ref[...] += jnp.dot(scaled, weights, preferred_element_type=f32)

    if last:

        @pl.when(step == pl.num_programs(0) - 1)
        def _():
            hidden = out_ref.shape[2]
            mean = jnp.sum(square_ref[...], axis=-1, keepdims=True) * (1.0 / width)
            scale = lax.rsqrt(mean + 1e-06)
            gate = acc_ref[:, :hidden] * scale
            up = acc_ref[:, hidden:] * scale
            active = gate / (1.0 + jnp.exp(-gate)) * up
            for p in range(tp_size):
                at = pl.multiple_of(order_ref[p] * 8, 8)
                for m in range(2):
                    begin = p * block + m * 8
                    ordered[m, pl.ds(at, 8), :] = active[begin : begin + 8]
            out_ref[...] = ordered[...].astype(bf16)


def gated(order, pieces, layout, gain, gate, up, start, tile, carried, width):
    first = carried is None
    last = not first
    columns = pieces[0].shape[1]
    hidden = gate.shape[1]
    rows = sum(p.shape[0] for p in pieces)
    base = start // tile
    in_specs = [pl.BlockSpec((p.shape[0], tile), lambda i, o: (0, i)) for p in pieces]
    in_specs += [
        pl.BlockSpec((1, tile), lambda i, o: (0, base + i)),
        pl.BlockSpec((tile, hidden), lambda i, o: (base + i, 0)),
        pl.BlockSpec((tile, hidden), lambda i, o: (base + i, 0)),
    ]
    args = list(pieces) + [gain, gate, up]
    acc_shape, square_shape = (rows, 2 * hidden), (rows, 128)
    whole = lambda i, o: (0, 0)
    if not first:
        in_specs += [pl.BlockSpec(acc_shape, whole), pl.BlockSpec(square_shape, whole)]
        args += list(carried)
    if last:
        out_dims = (2, rows // 2, hidden)
        out_specs = pl.BlockSpec(out_dims, lambda i, o: (0, 0, 0))
        out_shape = jax.ShapeDtypeStruct(out_dims, bf16)
        scratch = [
            pltpu.VMEM(acc_shape, f32),
            pltpu.VMEM(square_shape, f32),
            pltpu.VMEM(out_dims, f32),
        ]
    else:
        out_specs = [pl.BlockSpec(acc_shape, whole), pl.BlockSpec(square_shape, whole)]
        out_shape = [jax.ShapeDtypeStruct(acc_shape, f32), jax.ShapeDtypeStruct(square_shape, f32)]
        scratch = []
    return pl.pallas_call(
        functools.partial(gated_kernel, layout, first, last, width),
        grid_spec=pltpu.PrefetchScalarGridSpec(
            num_scalar_prefetch=1,
            grid=(columns // tile,),
            in_specs=in_specs,
            out_specs=out_specs,
            scratch_shapes=scratch,
        ),
        out_shape=out_shape,
        compiler_params=pltpu.CompilerParams(vmem_limit_bytes=vmem_limit),
        cost_estimate=pl.CostEstimate(
            flops=4 * rows * columns * hidden,
            bytes_accessed=4 * columns * hidden,
            transcendentals=0,
        ),
        name="gated_pair",
    )(order, *args)


def shards(
    residual,
    queries,
    latent_cache,
    new_latent,
    lengths,
    positions,
    latent_value_weight,
    w_out,
    norm_gain,
    gate_weight,
    up_weight,
):
    latent = latent_value_weight.shape[1]
    micro, own_rows, width = residual.shape
    block = micro * own_rows
    heads = queries.shape[2]
    me = lax.axis_index("tp")
    my_x, my_z, my_c = me // 4, (me // 2) % 2, me % 2
    order = jnp.stack(
        [
            ((my_x + px) % 4) * 4 + (my_z ^ pz) * 2 + (my_c ^ pc)
            for pc in range(core_size)
            for pz in range(z_size)
            for px in range(x_size)
        ]
    ).astype(jnp.int32)
    tables = rotary_tables(positions.reshape(-1), queries.shape[3] - latent)
    attended = attention(
        queries.reshape((block,) + queries.shape[2:]),
        latent_cache.reshape((block,) + latent_cache.shape[2:]),
        new_latent.reshape(block, -1),
        lengths.reshape(-1),
        tables,
        latent,
    )
    arrived = lax.all_to_all(
        attended.reshape(tp_size, heads // tp_size, block, latent),
        "tp",
        split_axis=0,
        concat_axis=0,
        tiled=True,
    )
    tile = 1792
    cut = 3584
    send_a, keep_a, values = value_and_out(order, arrived, latent_value_weight, w_out, cut, tile)
    send_b, keep_b = out_only(values, w_out, block, cut, width - cut, tile)
    flat_residual = residual.reshape(block, width).astype(f32)

    def add(*parts):
        total = parts[0].astype(f32)
        for part in parts[1:]:
            total = total + part.astype(f32)
        return total

    def x_sum(value, rows):
        own = value[:rows]
        right = send(value[rows : 2 * rows], dx=1)
        left = send(value[3 * rows : 4 * rows], dx=3)
        across = send(value[2 * rows : 3 * rows], dx=2)
        return own, right, left, across

    pair_a = add(keep_a, send(send_a, dc=1)).astype(bf16)
    pair_b = add(keep_b, send(send_b, dc=1)).astype(bf16)
    line_a = add(*x_sum(pair_a, 2 * block)).astype(bf16)
    line_b = add(pair_b[: 4 * block], send(pair_b[4 * block :], dz=1)).astype(bf16)
    after_a = add(
        flat_residual[:, :cut], line_a[:block], send(line_a[block:], dz=1)
    ).astype(bf16)
    after_b = add(flat_residual[:, cut:], *x_sum(line_b, block)).astype(bf16)

    def x_gather(value):
        return [value, send(value, dx=3), send(value, dx=2), send(value, dx=1)]

    near_a = jnp.concatenate(x_gather(after_a), axis=0)
    far_a = send(near_a, dz=1)
    pieces_a = [near_a, far_a, send(near_a, dc=1), send(far_a, dc=1)]
    both_b = jnp.concatenate([after_b, send(after_b, dz=1)], axis=0)
    gathered_b = x_gather(both_b)
    pieces_b = gathered_b + [send(g, dc=1) for g in gathered_b]

    canonical = [
        (pc, pz, px) for pc in range(core_size) for pz in range(z_size) for px in range(x_size)
    ]
    layout_a = [(pc * 2 + pz, px * block) for pc, pz, px in canonical]
    layout_b = [(pc * 4 + px, pz * block) for pc, pz, px in canonical]
    gain_row = norm_gain.reshape(1, width)
    k_tile = 512
    carried = gated(
        order, pieces_a, layout_a, gain_row, gate_weight, up_weight, 0, k_tile, None, width
    )
    activation = gated(
        order, pieces_b, layout_b, gain_row, gate_weight, up_weight, cut, k_tile, carried, width
    )
    after_attention = jnp.concatenate([after_a, after_b], axis=1).reshape(residual.shape)
    return (after_attention, activation)


def solution(mesh):
    return jax.shard_map(
        shards,
        mesh=mesh,
        in_specs=(
            P(None, ("dp", "tp"), None),
            P(None, ("dp", "tp"), None, None),
            P(None, ("dp", "tp"), None, None),
            P(None, ("dp", "tp"), None),
            P(None, ("dp", "tp")),
            P(None, ("dp", "tp")),
            P("tp", None, None),
            P("tp", None),
            P(),
            P(None, "tp"),
            P(None, "tp"),
        ),
        out_specs=(P(None, ("dp", "tp"), None), P(None, "dp", "tp")),
        check_vma=False,
    )
```

time: 190 us -> 123 us (0.65)
  waiting for transfers between devices: 103 us -> 38.6 us
  starting transfers between devices: 0.26 us -> 37.1 us
  Pallas kernels: 0 us -> 35.1 us
  matrix products: 33.5 us -> 0 us
  blocking collectives: 22.2 us -> 0 us
  between operations: 14.9 us -> 0.83 us
  other arithmetic: 6.76 us -> 2.41 us
    unnamed x3 -> x0, waiting for transfers between devices: 63.2 us -> none
    all_gather x1 -> x0, waiting for transfers between devices: 39.4 us -> none  [shards(): lax.all_gather((widened * lax.rsqrt(mean_square + 1e-06) * gain_row).asty...]
    pallas_call x0 -> x5, Pallas kernels: none -> 35.1 us  [the longest x2 17.4 us: gated(): pl.pallas_call(functools.partial(gated_kernel, layout, first, last, width...]
    dot_general x9 -> x0, matrix products: 33.5 us -> none  [the longest x1 7.87 us: shards(): jnp.einsum('nqb,bj->nqj', row_group_block, gate_weight, preferred_element...]
    ppermute x0 -> x24, starting transfers between devices: none -> 29.8 us  [send(): return lax.ppermute(value, 'tp', tp_perm(dx, dz, dc))]
    ppermute x0 -> x24, waiting for transfers between devices: none -> 23 us  [send(): return lax.ppermute(value, 'tp', tp_perm(dx, dz, dc))]
    all_to_all x1 -> x0, blocking collectives: 22.2 us -> none  [shards(): lax.all_to_all(attended_latent, 'tp', split_axis=2, concat_axis=1, tiled=...]
    all_to_all x0 -> x1, waiting for transfers between devices: none -> 15.6 us  [shards(): lax.all_to_all(attended.reshape(tp_size, heads // tp_size, block, latent)...]
  transfers between devices with their start and end apart: 2 -> 25, of which waited for: 2 -> 12; matrix products, arithmetic and copies ran while one was open for 0% -> 1% of each run, Pallas kernels for 0% -> 9%
where the time goes in v1:
time: 123 us; the launch traced here: 122 us
  waiting for transfers between devices  38.6 us (31%)
  starting transfers between devices  37.1 us (30%)
  Pallas kernels  35.1 us (29%)
  local copies, waits for them, and re-layouts  8.2 us (7%)
  other arithmetic  2.41 us (2%)
    ppermute x24, starting transfers between devices, send(): return lax.ppermute(value, 'tp', tp_perm(dx, dz, dc))  29.8 us
    ppermute x24, waiting for transfers between devices, send(): return lax.ppermute(value, 'tp', tp_perm(dx, dz, dc))  23 us
    pallas_call x2, Pallas kernels, gated(): pl.pallas_call(functools.partial(gated_kernel, layout, first, last, width...  17.4 us
    all_to_all x1, waiting for transfers between devices, shards(): lax.all_to_all(attended.reshape(tp_size, heads // tp_size, block, latent)...  15.6 us
    pallas_call x1, Pallas kernels, attention(): pl.pallas_call(functools.partial(attention_kernel, rows, latent), grid_sp...  10.8 us
    unnamed x13, local copies, waits for them, and re-layouts  7.82 us
    all_to_all x1, starting transfers between devices, shards(): lax.all_to_all(attended.reshape(tp_size, heads // tp_size, block, latent)...  7.3 us
    pallas_call x1, Pallas kernels, value_and_out(): pl.pallas_call(functools.partial(value_kernel, block), grid_spec=pltpu.Pr...  3.95 us
  transfers between devices with their start and end apart: 25, of which 12 were waited for; matrix products, arithmetic and copies ran while one was open for 1% of the time, Pallas kernels for 9%

profile of v1, /device:TPU:1, one launch (start us, length us, event | category | flops | bytes accessed | tf_op | source)
XLA Modules:
  0.0 122.3 jit_solution(12275330268943997236)
XLA Ops:
  1.4 7.8 %copy.13 = bf16[2,8,256,576]{3,2,1,0:T(8,128)(2,1)} copy(bf16[2,8,256,576]{2,3,1,0:T(8,128)(2,1)} %param.13) | data formatting | bytes 9437184 | tf_op args[2]
  9.5 10.8 %attention.1 = bf16[64,16,512]{2,1,0:T(8,128)(2,1)} custom-call(s32[16]{0:T(128)S(1)} %reshape.41.len_ref, bf16[16,64,576]{2,1,0:T(8,128)(2,1)S(1)} %bitcast.25, bf16[16,256,576]{2,1,0:T(8,128)(2,1)} %bitcast.27, bf16[16,576]{1,0:T(8,128)(2,1)S(1)} %bitcast.26, f32[16,128]{1,0:T(8,128)S(1)} %pad_maximum_fusion.2.t_ref), custom_call_target="tpu_custom_call" | custom-call | flops 603979776 | bytes 5898240 | tf_op jit(solution)/shard_map/attention/pallas_call | solution.py:84
  20.3 7.3 %all-to-all-start = ((bf16[16,4,16,512]{3,2,1,0:T(8,128)(2,1)}), bf16[16,4,16,512]{3,2,1,0:T(8,128)(2,1)S(1)}, u32[]{:S(2)}, u32[]{:S(2)}) async-start(bf16[16,4,16,512]{3,2,1,0:T(8,128)(2,1)} %bitcast.20), calls=%async_computation | async-start | bytes 2097152 | tf_op jit(solution)/shard_map/all_to_all | solution.py:347
  27.7 15.6 %all-to-all-done.a_ref = bf16[16,4,16,512]{3,2,1,0:T(8,128)(2,1)S(1)} async-done(((bf16[16,4,16,512]{3,2,1,0:T(8,128)(2,1)}), bf16[16,4,16,512]{3,2,1,0:T(8,128)(2,1)S(1)}, u32[]{:S(2)}, u32[]{:S(2)}) %all-to-all-start) | async-done | bytes 1048608 | tf_op jit(solution)/shard_map/all_to_all | solution.py:347
  43.3 3.9 %value_out.1 = (bf16[128,3584]{1,0:T(8,128)(2,1)S(1)}, bf16[128,3584]{1,0:T(8,128)(2,1)S(1)}, bf16[256,512]{1,0:T(8,128)(2,1)S(1)}) custom-call(s32[16]{0:T(128)S(1)} %stack.67.order_ref.refs_0_, bf16[16,4,16,512]{3,2,1,0:T(8,128)(2,1)S(1)} %all-to-all-done.a_ref, bf16[4,512,128]{2,1,0:T(8,128)(2,1)S(1)} %copy-done.1, bf16[512,7168]{1,0:T(8,128)(2,1)} %w_ref.3), custom_call_target="tpu_custom_call" | custom-call | flops 1073741824 | bytes 3670016 | tf_op jit(solution)/shard_map/value_out/pallas_call | solution.py:148
  47.3 1.0 collective-permute-start
  48.2 2.9 %out_proj.1 = (bf16[128,3584]{1,0:T(8,128)(2,1)S(1)}, bf16[128,3584]{1,0:T(8,128)(2,1)S(1)}) custom-call(bf16[256,512]{1,0:T(8,128)(2,1)S(1)} %get-tuple-element.11.v_ref, bf16[512,7168]{1,0:T(8,128)(2,1)} %w_ref.3), custom_call_target="tpu_custom_call" | custom-call | flops 939524096 | bytes 3670016 | tf_op jit(solution)/shard_map/out_proj/pallas_call | solution.py:183
  51.6 2.7 %collective-permute-start.2 = (bf16[32,3584]{1,0:T(8,128)(2,1)S(1)}, bf16[32,3584]{1,0:T(8,128)(2,1)S(1)}, u32[]{:S(2)}, u32[]{:S(2)}) collective-permute-start(bf16[32,3584]{1,0:T(8,128)(2,1)S(1)} %get-tuple-element.18), channel_id=1, source_target_pairs={{0,12},{1,13},{2,14},{3,15},{4,0},{5,1},{6,2},{7,3},{8,4},{9,5},{1... | collective-permute-start | bytes 688136 | tf_op jit(solution)/shard_map/ppermute | solution.py:29
  54.6 1.0 collective-permute-start.6
  55.6 4.7 %collective-permute-done.1 = bf16[32,3584]{1,0:T(8,128)(2,1)S(1)} collective-permute-done((bf16[32,3584]{1,0:T(8,128)(2,1)S(1)}, bf16[32,3584]{1,0:T(8,128)(2,1)S(1)}, u32[]{:S(2)}, u32[]{:S(2)}) %collective-permute-start.1) | collective-permute-done | bytes 229408 | tf_op jit(solution)/shard_map/ppermute | solution.py:29
  60.3 3.3 %collective-permute-done.3 = bf16[32,3584]{1,0:T(8,128)(2,1)S(1)} collective-permute-done((bf16[32,3584]{1,0:T(8,128)(2,1)S(1)}, bf16[32,3584]{1,0:T(8,128)(2,1)S(1)}, u32[]{:S(2)}, u32[]{:S(2)}) %collective-permute-start.3) | collective-permute-done | bytes 229408 | tf_op jit(solution)/shard_map/ppermute | solution.py:29
  63.8 1.6 %collective-permute-start.4 = (bf16[16,3584]{1,0:T(8,128)(2,1)S(1)}, bf16[16,3584]{1,0:T(8,128)(2,1)S(1)}, u32[]{:S(2)}, u32[]{:S(2)}) collective-permute-start(bf16[16,3584]{1,0:T(8,128)(2,1)S(1)} %slice.62), channel_id=1, source_target_pairs={{0,2},{1,3},{2,0},{3,1},{4,6},{5,7},{6,4},{7,5},{8,10},{9,11},{10,... | collective-permute-start | bytes 344072 | tf_op jit(solution)/shard_map/ppermute | solution.py:29
  66.4 2.1 %collective-permute-start.8 = (bf16[16,3584]{1,0:T(8,128)(2,1)S(1)}, bf16[16,3584]{1,0:T(8,128)(2,1)S(1)}, u32[]{:S(2)}, u32[]{:S(2)}) collective-permute-start(bf16[16,3584]{1,0:T(8,128)(2,1)S(1)} %get-tuple-element.23), channel_id=1, source_target_pairs={{0,12},{1,13},{2,14},{3,15},{4,0},{5,1},{6,2},{7,3},{8,4},{9,5},{1... | collective-permute-start | bytes 344072 | tf_op jit(solution)/shard_map/ppermute | solution.py:29
  68.5 1.5 %collective-permute-start.9 = (bf16[16,3584]{1,0:T(8,128)(2,1)S(1)}, bf16[16,3584]{1,0:T(8,128)(2,1)S(1)}, u32[]{:S(2)}, u32[]{:S(2)}) collective-permute-start(bf16[16,3584]{1,0:T(8,128)(2,1)S(1)} %get-tuple-element.22), channel_id=1, source_target_pairs={{0,8},{1,9},{2,10},{3,11},{4,12},{5,13},{6,14},{7,15},{8,0},{9,1},... | collective-permute-start | bytes 344072 | tf_op jit(solution)/shard_map/ppermute | solution.py:29
  70.7 3.5 %collective-permute-done.9 = bf16[16,3584]{1,0:T(8,128)(2,1)S(1)} collective-permute-done((bf16[16,3584]{1,0:T(8,128)(2,1)S(1)}, bf16[16,3584]{1,0:T(8,128)(2,1)S(1)}, u32[]{:S(2)}, u32[]{:S(2)}) %collective-permute-start.9) | collective-permute-done | bytes 114720 | tf_op jit(solution)/shard_map/ppermute | solution.py:29
  74.7 0.8 collective-permute-start.19
  75.5 0.8 collective-permute-start.20
  76.3 1.0 collective-permute-start.10
  78.0 2.0 %collective-permute-done.19 = bf16[16,3584]{1,0:T(8,128)(2,1)S(1)} collective-permute-done((bf16[16,3584]{1,0:T(8,128)(2,1)S(1)}, bf16[16,3584]{1,0:T(8,128)(2,1)S(1)}, u32[]{:S(2)}, u32[]{:S(2)}) %collective-permute-start.19) | collective-permute-done | bytes 114720 | tf_op jit(solution)/shard_map/ppermute | solution.py:29
  80.0 1.2 collective-permute-done.20
  81.2 1.2 %collective-permute-start.21 = (bf16[64,3584]{1,0:T(8,128)(2,1)S(1)}, bf16[64,3584]{1,0:T(8,128)(2,1)S(1)}, u32[]{:S(2)}, u32[]{:S(2)}) collective-permute-start(bf16[64,3584]{1,0:T(8,128)(2,1)S(1)} %pad_maximum_fusion.refs_1_), channel_id=1, source_target_pairs={{0,2},{1,3},{2,0},{3,1},{4,6},{5,7},{6,4},{7,5},{8,10},{9,11},{10,... | collective-permute-start | bytes 1376264 | tf_op jit(solution)/shard_map/ppermute | solution.py:29
  82.4 5.4 %collective-permute-start.22 = (bf16[64,3584]{1,0:T(8,128)(2,1)S(1)}, bf16[64,3584]{1,0:T(8,128)(2,1)S(1)}, u32[]{:S(2)}, u32[]{:S(2)}) collective-permute-start(bf16[64,3584]{1,0:T(8,128)(2,1)S(1)} %pad_maximum_fusion.refs_1_), channel_id=1, source_target_pairs={{0,1},{1,0},{2,3},{3,2},{4,5},{5,4},{6,7},{7,6},{8,9},{9,8},{10,11... | collective-permute-start | bytes 1376264 | tf_op jit(solution)/shard_map/ppermute | solution.py:29
  88.3 1.1 collective-permute-start.12
  90.0 4.3 %collective-permute-done.11.refs_2_ = bf16[32,3584]{1,0:T(8,128)(2,1)S(1)} collective-permute-done((bf16[32,3584]{1,0:T(8,128)(2,1)S(1)}, bf16[32,3584]{1,0:T(8,128)(2,1)S(1)}, u32[]{:S(2)}, u32[]{:S(2)}) %collective-permute-start.11) | collective-permute-done | bytes 229408 | tf_op jit(solution)/shard_map/ppermute | solution.py:29
  94.3 2.7 %collective-permute-start.14 = (bf16[32,3584]{1,0:T(8,128)(2,1)S(1)}, bf16[32,3584]{1,0:T(8,128)(2,1)S(1)}, u32[]{:S(2)}, u32[]{:S(2)}) collective-permute-start(bf16[32,3584]{1,0:T(8,128)(2,1)S(1)} %pad_maximum_fusion.1.refs_1_), channel_id=1, source_target_pairs={{0,1},{1,0},{2,3},{3,2},{4,5},{5,4},{6,7},{7,6},{8,9},{9,8},{10,11... | collective-permute-start | bytes 688136 | tf_op jit(solution)/shard_map/ppermute | solution.py:29
  97.1 3.2 %collective-permute-start.15 = (bf16[32,3584]{1,0:T(8,128)(2,1)S(1)}, bf16[32,3584]{1,0:T(8,128)(2,1)S(1)}, u32[]{:S(2)}, u32[]{:S(2)}) collective-permute-start(bf16[32,3584]{1,0:T(8,128)(2,1)S(1)} %collective-permute-done.11.refs_2_), channel_id=1, source_target_pairs={{0,1},{1,0},{2,3},{3,2},{4,5},{5,4},{6,7},{7,6},{8,9},{9,8},{10,11... | collective-permute-start | bytes 688136 | tf_op jit(solution)/shard_map/ppermute | solution.py:29
  100.3 1.5 %collective-permute-done.13.refs_4_ = bf16[32,3584]{1,0:T(8,128)(2,1)S(1)} collective-permute-done((bf16[32,3584]{1,0:T(8,128)(2,1)S(1)}, bf16[32,3584]{1,0:T(8,128)(2,1)S(1)}, u32[]{:S(2)}, u32[]{:S(2)}) %collective-permute-start.13) | collective-permute-done | bytes 229408 | tf_op jit(solution)/shard_map/ppermute | solution.py:29
  101.8 0.9 collective-permute-start.16
  103.2 0.7 maximum_bitcast_fusion
  103.9 0.9 collective-permute-done.23.refs_4_
  104.9 8.1 %gated_pair.2 = (f32[256,1280]{1,0:T(8,128)S(1)}, f32[256,128]{1,0:T(8,128)S(1)}) custom-call(s32[16]{0:T(128)S(1)} %stack.67.order_ref.refs_0_, bf16[64,3584]{1,0:T(8,128)(2,1)S(1)} %pad_maximum_fusion.refs_1_, bf16[64,3584]{1,0:T(8,128)(2,1)S(1)} %collective-permute-done.21.refs_2_, bf16[64,3584]{1,0:T(8,128)(2,1)S(1)} %collective-permute-done.22.refs_3_, ...), custom_call_target="tpu_custom_call" | custom-call | flops 2348810240 | bytes 9175040 | tf_op jit(solution)/shard_map/gated_pair/pallas_call | solution.py:291
  113.0 9.3 %gated_pair.3 = bf16[2,128,640]{2,1,0:T(8,128)(2,1)} custom-call(s32[16]{0:T(128)S(1)} %stack.67.order_ref.refs_0_, bf16[32,3584]{1,0:T(8,128)(2,1)S(1)} %pad_maximum_fusion.1.refs_1_, bf16[32,3584]{1,0:T(8,128)(2,1)S(1)} %collective-permute-done.11.refs_2_, bf16[32,3584]{1,0:T(8,128)(2,1)S(1)} %collective-permute-done.12.refs_3_, ...), custom_call_target="tpu_custom_call" | custom-call | flops 2348810240 | bytes 9175040 | tf_op jit(solution)/shard_map/gated_pair/pallas_call | solution.py:291
  (57 shorter events, 6.5 us)
Async XLA Ops:
  1.4 7.8 %copy-start.5 = (s32[2,8]{1,0:T(2,128)S(1)}, s32[2,8]{1,0:T(2,128)}, u32[]{:S(2)}) copy-start(s32[2,8]{1,0:T(2,128)} %param.15) | copy-start | bytes 196
  1.4 8.1 %copy-start = (bf16[2,8,64,576]{3,2,1,0:T(8,128)(2,1)S(1)}, bf16[2,8,64,576]{3,2,1,0:T(8,128)(2,1)}, u32[]{:S(2)}) copy-start(bf16[2,8,64,576]{3,2,1,0:T(8,128)(2,1)} %param.12) | copy-start | bytes 3538948
  1.4 8.1 %copy-start.2 = (bf16[2,8,576]{2,1,0:T(8,128)(2,1)S(1)}, bf16[2,8,576]{2,1,0:T(8,128)(2,1)}, u32[]{:S(2)}) copy-start(bf16[2,8,576]{2,1,0:T(8,128)(2,1)} %param.14) | copy-start | bytes 55300
  20.3 23.0 %copy-start.1 = (bf16[4,512,128]{2,1,0:T(8,128)(2,1)S(1)}, bf16[4,512,128]{2,1,0:T(8,128)(2,1)}, u32[]{:S(2)}) copy-start(bf16[4,512,128]{2,1,0:T(8,128)(2,1)} %v_ref.1) | copy-start | bytes 1572868
  20.3 23.0 %all-to-all-start = ((bf16[16,4,16,512]{3,2,1,0:T(8,128)(2,1)}), bf16[16,4,16,512]{3,2,1,0:T(8,128)(2,1)S(1)}, u32[]{:S(2)}, u32[]{:S(2)}) async-start(bf16[16,4,16,512]{3,2,1,0:T(8,128)(2,1)} %bitcast.20), calls=%async_computation | async-start | bytes 2097152 | tf_op jit(solution)/shard_map/all_to_all | solution.py:347
  47.3 4.0 %collective-permute-start = (bf16[128,3584]{1,0:T(8,128)(2,1)S(1)}, bf16[128,3584]{1,0:T(8,128)(2,1)S(1)}, u32[]{:S(2)}, u32[]{:S(2)}) collective-permute-start(bf16[128,3584]{1,0:T(8,128)(2,1)S(1)} %get-tuple-element.10), channel_id=1, source_target_pairs={{0,1},{1,0},{2,3},{3,2},{4,5},{5,4},{6,7},{7,6},{8,9},{9,8},{10,11... | collective-permute-start | bytes 2752520 | tf_op jit(solution)/shard_map/ppermute | solution.py:29
  51.2 3.1 %collective-permute-start.5 = (bf16[128,3584]{1,0:T(8,128)(2,1)S(1)}, bf16[128,3584]{1,0:T(8,128)(2,1)S(1)}, u32[]{:S(2)}, u32[]{:S(2)}) collective-permute-start(bf16[128,3584]{1,0:T(8,128)(2,1)S(1)} %get-tuple-element.13), channel_id=1, source_target_pairs={{0,1},{1,0},{2,3},{3,2},{4,5},{5,4},{6,7},{7,6},{8,9},{9,8},{10,11... | collective-permute-start | bytes 2752520 | tf_op jit(solution)/shard_map/ppermute | solution.py:29
  51.5 8.8 %collective-permute-start.1 = (bf16[32,3584]{1,0:T(8,128)(2,1)S(1)}, bf16[32,3584]{1,0:T(8,128)(2,1)S(1)}, u32[]{:S(2)}, u32[]{:S(2)}) collective-permute-start(bf16[32,3584]{1,0:T(8,128)(2,1)S(1)} %get-tuple-element.16), channel_id=1, source_target_pairs={{0,4},{1,5},{2,6},{3,7},{4,8},{5,9},{6,10},{7,11},{8,12},{9,13},{1... | collective-permute-start | bytes 688136 | tf_op jit(solution)/shard_map/ppermute | solution.py:29
  51.6 8.7 %collective-permute-start.2 = (bf16[32,3584]{1,0:T(8,128)(2,1)S(1)}, bf16[32,3584]{1,0:T(8,128)(2,1)S(1)}, u32[]{:S(2)}, u32[]{:S(2)}) collective-permute-start(bf16[32,3584]{1,0:T(8,128)(2,1)S(1)} %get-tuple-element.18), channel_id=1, source_target_pairs={{0,12},{1,13},{2,14},{3,15},{4,0},{5,1},{6,2},{7,3},{8,4},{9,5},{1... | collective-permute-start | bytes 688136 | tf_op jit(solution)/shard_map/ppermute | solution.py:29
  54.3 9.4 %collective-permute-start.3 = (bf16[32,3584]{1,0:T(8,128)(2,1)S(1)}, bf16[32,3584]{1,0:T(8,128)(2,1)S(1)}, u32[]{:S(2)}, u32[]{:S(2)}) collective-permute-start(bf16[32,3584]{1,0:T(8,128)(2,1)S(1)} %get-tuple-element.17), channel_id=1, source_target_pairs={{0,8},{1,9},{2,10},{3,11},{4,12},{5,13},{6,14},{7,15},{8,0},{9,1},... | collective-permute-start | bytes 688136 | tf_op jit(solution)/shard_map/ppermute | solution.py:29
  54.6 15.4 %copy-start.3 = (bf16[2,8,7168]{2,1,0:T(8,128)(2,1)S(1)}, bf16[2,8,7168]{2,1,0:T(8,128)(2,1)}, u32[]{:S(2)}) copy-start(bf16[2,8,7168]{2,1,0:T(8,128)(2,1)} %param.11) | copy-start | bytes 688132
  54.6 11.0 %collective-permute-start.6 = (bf16[64,3584]{1,0:T(8,128)(2,1)S(1)}, bf16[64,3584]{1,0:T(8,128)(2,1)S(1)}, u32[]{:S(2)}, u32[]{:S(2)}) collective-permute-start(bf16[64,3584]{1,0:T(8,128)(2,1)S(1)} %slice.65), channel_id=1, source_target_pairs={{0,2},{1,3},{2,0},{3,1},{4,6},{5,7},{6,4},{7,5},{8,10},{9,11},{10,... | collective-permute-start | bytes 1376264 | tf_op jit(solution)/shard_map/ppermute | solution.py:29
  63.8 6.2 %collective-permute-start.4 = (bf16[16,3584]{1,0:T(8,128)(2,1)S(1)}, bf16[16,3584]{1,0:T(8,128)(2,1)S(1)}, u32[]{:S(2)}, u32[]{:S(2)}) collective-permute-start(bf16[16,3584]{1,0:T(8,128)(2,1)S(1)} %slice.62), channel_id=1, source_target_pairs={{0,2},{1,3},{2,0},{3,1},{4,6},{5,7},{6,4},{7,5},{8,10},{9,11},{10,... | collective-permute-start | bytes 344072 | tf_op jit(solution)/shard_map/ppermute | solution.py:29
  65.7 24.3 %copy-start.4 = (bf16[7168]{0:T(1024)(128)(2,1)S(1)}, bf16[7168]{0:T(1024)(128)(2,1)}, u32[]{:S(2)}) copy-start(bf16[7168]{0:T(1024)(128)(2,1)} %param.19) | copy-start | bytes 43012
  65.7 4.9 %collective-permute-start.7 = (bf16[16,3584]{1,0:T(8,128)(2,1)S(1)}, bf16[16,3584]{1,0:T(8,128)(2,1)S(1)}, u32[]{:S(2)}, u32[]{:S(2)}) collective-permute-start(bf16[16,3584]{1,0:T(8,128)(2,1)S(1)} %get-tuple-element.21), channel_id=1, source_target_pairs={{0,4},{1,5},{2,6},{3,7},{4,8},{5,9},{6,10},{7,11},{8,12},{9,13},{1... | collective-permute-start | bytes 344072 | tf_op jit(solution)/shard_map/ppermute | solution.py:29
  66.4 4.3 %collective-permute-start.8 = (bf16[16,3584]{1,0:T(8,128)(2,1)S(1)}, bf16[16,3584]{1,0:T(8,128)(2,1)S(1)}, u32[]{:S(2)}, u32[]{:S(2)}) collective-permute-start(bf16[16,3584]{1,0:T(8,128)(2,1)S(1)} %get-tuple-element.23), channel_id=1, source_target_pairs={{0,12},{1,13},{2,14},{3,15},{4,0},{5,1},{6,2},{7,3},{8,4},{9,5},{1... | collective-permute-start | bytes 344072 | tf_op jit(solution)/shard_map/ppermute | solution.py:29
  68.5 5.7 %collective-permute-start.9 = (bf16[16,3584]{1,0:T(8,128)(2,1)S(1)}, bf16[16,3584]{1,0:T(8,128)(2,1)S(1)}, u32[]{:S(2)}, u32[]{:S(2)}) collective-permute-start(bf16[16,3584]{1,0:T(8,128)(2,1)S(1)} %get-tuple-element.22), channel_id=1, source_target_pairs={{0,8},{1,9},{2,10},{3,11},{4,12},{5,13},{6,14},{7,15},{8,0},{9,1},... | collective-permute-start | bytes 344072 | tf_op jit(solution)/shard_map/ppermute | solution.py:29
  74.3 3.7 %collective-permute-start.18 = (bf16[16,3584]{1,0:T(8,128)(2,1)S(1)}, bf16[16,3584]{1,0:T(8,128)(2,1)S(1)}, u32[]{:S(2)}, u32[]{:S(2)}) collective-permute-start(bf16[16,3584]{1,0:T(8,128)(2,1)S(1)} %get-tuple-element.19), channel_id=1, source_target_pairs={{0,12},{1,13},{2,14},{3,15},{4,0},{5,1},{6,2},{7,3},{8,4},{9,5},{1... | collective-permute-start | bytes 344072 | tf_op jit(solution)/shard_map/ppermute | solution.py:29
  74.7 5.2 %collective-permute-start.19 = (bf16[16,3584]{1,0:T(8,128)(2,1)S(1)}, bf16[16,3584]{1,0:T(8,128)(2,1)S(1)}, u32[]{:S(2)}, u32[]{:S(2)}) collective-permute-start(bf16[16,3584]{1,0:T(8,128)(2,1)S(1)} %get-tuple-element.19), channel_id=1, source_target_pairs={{0,8},{1,9},{2,10},{3,11},{4,12},{5,13},{6,14},{7,15},{8,0},{9,1},... | collective-permute-start | bytes 344072 | tf_op jit(solution)/shard_map/ppermute | solution.py:29
  75.5 5.6 %collective-permute-start.20 = (bf16[16,3584]{1,0:T(8,128)(2,1)S(1)}, bf16[16,3584]{1,0:T(8,128)(2,1)S(1)}, u32[]{:S(2)}, u32[]{:S(2)}) collective-permute-start(bf16[16,3584]{1,0:T(8,128)(2,1)S(1)} %get-tuple-element.19), channel_id=1, source_target_pairs={{0,4},{1,5},{2,6},{3,7},{4,8},{5,9},{6,10},{7,11},{8,12},{9,13},{1... | collective-permute-start | bytes 344072 | tf_op jit(solution)/shard_map/ppermute | solution.py:29
  76.3 11.5 %collective-permute-start.10 = (bf16[16,3584]{1,0:T(8,128)(2,1)S(1)}, bf16[16,3584]{1,0:T(8,128)(2,1)S(1)}, u32[]{:S(2)}, u32[]{:S(2)}) collective-permute-start(bf16[16,3584]{1,0:T(8,128)(2,1)S(1)} %get-tuple-element.20), channel_id=1, source_target_pairs={{0,2},{1,3},{2,0},{3,1},{4,6},{5,7},{6,4},{7,5},{8,10},{9,11},{10,... | collective-permute-start | bytes 344072 | tf_op jit(solution)/shard_map/ppermute | solution.py:29
  81.2 21.5 %collective-permute-start.21 = (bf16[64,3584]{1,0:T(8,128)(2,1)S(1)}, bf16[64,3584]{1,0:T(8,128)(2,1)S(1)}, u32[]{:S(2)}, u32[]{:S(2)}) collective-permute-start(bf16[64,3584]{1,0:T(8,128)(2,1)S(1)} %pad_maximum_fusion.refs_1_), channel_id=1, source_target_pairs={{0,2},{1,3},{2,0},{3,1},{4,6},{5,7},{6,4},{7,5},{8,10},{9,11},{10,... | collective-permute-start | bytes 1376264 | tf_op jit(solution)/shard_map/ppermute | solution.py:29
  82.4 20.3 %collective-permute-start.22 = (bf16[64,3584]{1,0:T(8,128)(2,1)S(1)}, bf16[64,3584]{1,0:T(8,128)(2,1)S(1)}, u32[]{:S(2)}, u32[]{:S(2)}) collective-permute-start(bf16[64,3584]{1,0:T(8,128)(2,1)S(1)} %pad_maximum_fusion.refs_1_), channel_id=1, source_target_pairs={{0,1},{1,0},{2,3},{3,2},{4,5},{5,4},{6,7},{7,6},{8,9},{9,8},{10,11... | collective-permute-start | bytes 1376264 | tf_op jit(solution)/shard_map/ppermute | solution.py:29
  87.8 6.5 %collective-permute-start.11 = (bf16[32,3584]{1,0:T(8,128)(2,1)S(1)}, bf16[32,3584]{1,0:T(8,128)(2,1)S(1)}, u32[]{:S(2)}, u32[]{:S(2)}) collective-permute-start(bf16[32,3584]{1,0:T(8,128)(2,1)S(1)} %pad_maximum_fusion.1.refs_1_), channel_id=1, source_target_pairs={{0,12},{1,13},{2,14},{3,15},{4,0},{5,1},{6,2},{7,3},{8,4},{9,5},{1... | collective-permute-start | bytes 688136 | tf_op jit(solution)/shard_map/ppermute | solution.py:29
  88.3 8.8 %collective-permute-start.12 = (bf16[32,3584]{1,0:T(8,128)(2,1)S(1)}, bf16[32,3584]{1,0:T(8,128)(2,1)S(1)}, u32[]{:S(2)}, u32[]{:S(2)}) collective-permute-start(bf16[32,3584]{1,0:T(8,128)(2,1)S(1)} %pad_maximum_fusion.1.refs_1_), channel_id=1, source_target_pairs={{0,8},{1,9},{2,10},{3,11},{4,12},{5,13},{6,14},{7,15},{8,0},{9,1},... | collective-permute-start | bytes 688136 | tf_op jit(solution)/shard_map/ppermute | solution.py:29
  89.4 12.4 %collective-permute-start.13 = (bf16[32,3584]{1,0:T(8,128)(2,1)S(1)}, bf16[32,3584]{1,0:T(8,128)(2,1)S(1)}, u32[]{:S(2)}, u32[]{:S(2)}) collective-permute-start(bf16[32,3584]{1,0:T(8,128)(2,1)S(1)} %pad_maximum_fusion.1.refs_1_), channel_id=1, source_target_pairs={{0,4},{1,5},{2,6},{3,7},{4,8},{5,9},{6,10},{7,11},{8,12},{9,13},{1... | collective-permute-start | bytes 688136 | tf_op jit(solution)/shard_map/ppermute | solution.py:29
  94.3 18.6 %collective-permute-start.14 = (bf16[32,3584]{1,0:T(8,128)(2,1)S(1)}, bf16[32,3584]{1,0:T(8,128)(2,1)S(1)}, u32[]{:S(2)}, u32[]{:S(2)}) collective-permute-start(bf16[32,3584]{1,0:T(8,128)(2,1)S(1)} %pad_maximum_fusion.1.refs_1_), channel_id=1, source_target_pairs={{0,1},{1,0},{2,3},{3,2},{4,5},{5,4},{6,7},{7,6},{8,9},{9,8},{10,11... | collective-permute-start | bytes 688136 | tf_op jit(solution)/shard_map/ppermute | solution.py:29
  97.1 15.9 %collective-permute-start.15 = (bf16[32,3584]{1,0:T(8,128)(2,1)S(1)}, bf16[32,3584]{1,0:T(8,128)(2,1)S(1)}, u32[]{:S(2)}, u32[]{:S(2)}) collective-permute-start(bf16[32,3584]{1,0:T(8,128)(2,1)S(1)} %collective-permute-done.11.refs_2_), channel_id=1, source_target_pairs={{0,1},{1,0},{2,3},{3,2},{4,5},{5,4},{6,7},{7,6},{8,9},{9,8},{10,11... | collective-permute-start | bytes 688136 | tf_op jit(solution)/shard_map/ppermute | solution.py:29
  101.8 11.2 %collective-permute-start.16 = (bf16[32,3584]{1,0:T(8,128)(2,1)S(1)}, bf16[32,3584]{1,0:T(8,128)(2,1)S(1)}, u32[]{:S(2)}, u32[]{:S(2)}) collective-permute-start(bf16[32,3584]{1,0:T(8,128)(2,1)S(1)} %collective-permute-done.12.refs_3_), channel_id=1, source_target_pairs={{0,1},{1,0},{2,3},{3,2},{4,5},{5,4},{6,7},{7,6},{8,9},{9,8},{10,11... | collective-permute-start | bytes 688136 | tf_op jit(solution)/shard_map/ppermute | solution.py:29
  102.7 10.3 %collective-permute-start.17 = (bf16[32,3584]{1,0:T(8,128)(2,1)S(1)}, bf16[32,3584]{1,0:T(8,128)(2,1)S(1)}, u32[]{:S(2)}, u32[]{:S(2)}) collective-permute-start(bf16[32,3584]{1,0:T(8,128)(2,1)S(1)} %collective-permute-done.13.refs_4_), channel_id=1, source_target_pairs={{0,1},{1,0},{2,3},{3,2},{4,5},{5,4},{6,7},{7,6},{8,9},{9,8},{10,11... | collective-permute-start | bytes 688136 | tf_op jit(solution)/shard_map/ppermute | solution.py:29
  102.7 2.1 %collective-permute-start.23 = (bf16[64,3584]{1,0:T(8,128)(2,1)S(1)}, bf16[64,3584]{1,0:T(8,128)(2,1)S(1)}, u32[]{:S(2)}, u32[]{:S(2)}) collective-permute-start(bf16[64,3584]{1,0:T(8,128)(2,1)S(1)} %collective-permute-done.21.refs_2_), channel_id=1, source_target_pairs={{0,1},{1,0},{2,3},{3,2},{4,5},{5,4},{6,7},{7,6},{8,9},{9,8},{10,11... | collective-permute-start | bytes 1376264 | tf_op jit(solution)/shard_map/ppermute | solution.py:29

commit v2 on v1

v2 whole, which is shorter than its diff:
```python
import functools

import jax
import jax.numpy as jnp
import numpy as np
from jax import lax
from jax.experimental import pallas as pl
from jax.experimental.pallas import tpu as pltpu
from jax.sharding import PartitionSpec as P

score_scale = 192.0 ** (-0.5)
neg_large = -1e30
f32 = jnp.float32
bf16 = jnp.bfloat16
vmem_limit = 20 * 1024 * 1024
large_vmem = 56 * 1024 * 1024
x_size, z_size, core_size = 4, 2, 2
tp_size = x_size * z_size * core_size


def tp_perm(dx=0, dz=0, dc=0):
    pairs = []
    for i in range(tp_size):
        x, z, c = i // 4, (i // 2) % 2, i % 2
        pairs.append((i, ((x + dx) % 4) * 4 + (z ^ dz) * 2 + (c ^ dc)))
    return pairs


def send(value, dx=0, dz=0, dc=0):
    return lax.ppermute(value, "tp", tp_perm(dx, dz, dc))


def rotary_tables(positions, rope):
    half = rope // 2
    exponent = jnp.arange(half, dtype=f32) * (2.0 / rope)
    angles = positions.astype(f32)[..., None] * (10000.0 ** (-exponent))
    cosine, sine = jnp.cos(angles), jnp.sin(angles)
    return jnp.concatenate([cosine, cosine, -sine, sine], axis=-1)


def attention_kernel(
    group, span, latent, len_ref, q_hbm, c_hbm, n_ref, t_ref, out_ref, q_ref, c_ref, held, q_sem, c_sem
):
    count, heads, width = q_ref.shape
    rope = width - latent
    half = rope // 2
    per = len_ref.shape[1]

    copies = []
    for i in range(count // span):
        at = pl.ds(i * span, span)
        copies.append(
            (
                pltpu.make_async_copy(q_hbm.at[at], q_ref.at[at], q_sem.at[i]),
                pltpu.make_async_copy(c_hbm.at[at], c_ref.at[at], c_sem.at[i]),
            )
        )
    for pair in copies:
        for copy in pair:
            copy.start()

    def turn(values, cosine, sine):
        swapped = jnp.concatenate([values[:, half:], values[:, :half]], axis=-1)
        return (values * cosine + swapped * sine).astype(bf16)

    for begin in range(0, count, group):
        scored = []
        for r in range(begin, begin + group):
            if r % span == 0:
                for copy in copies[r // span]:
                    copy.wait()
            table = t_ref[r : r + 1, :]
            cosine, sine = table[:, :rope], table[:, rope:]
            q_lat = q_ref[r, :, :latent]
            q_rope = turn(q_ref[r, :, latent:].astype(f32), cosine, sine)
            n_lat = n_ref[r : r + 1, :latent].astype(f32)
            n_rope = turn(n_ref[r : r + 1, latent:].astype(f32), cosine, sine).astype(f32)
            scores = jnp.dot(q_lat, c_ref[r, :latent, :], preferred_element_type=f32)
            scores += jnp.dot(q_rope, c_ref[r, latent:, :], preferred_element_type=f32)
            own = jnp.sum(q_lat.astype(f32) * n_lat, axis=-1, keepdims=True)
            own += jnp.sum(q_rope.astype(f32) * n_rope, axis=-1, keepdims=True)
            scored.append((scores, own * score_scale, n_lat))
        weighted = []
        for r in range(begin, begin + group):
            scores, own, n_lat = scored[r - begin]
            visible = lax.broadcasted_iota(jnp.int32, scores.shape, 1) < len_ref[r // per, r % per]
            scores = jnp.where(visible, scores * score_scale, neg_large)
            top = jnp.maximum(jnp.max(scores, axis=-1, keepdims=True), own)
            weights = jnp.where(visible, jnp.exp(scores - top), 0.0)
            own_weight = jnp.exp(own - top)
            total = jnp.sum(weights, axis=-1, keepdims=True) + own_weight
            weighted.append((weights.astype(bf16), own_weight, total, n_lat))
        for r in range(begin, begin + group):
            weights, own_weight, total, n_lat = weighted[r - begin]
            context = lax.dot_general(
                weights, c_ref[r, :latent, :], (((1,), (1,)), ((), ())), preferred_element_type=f32
            )
            context += own_weight.astype(bf16).astype(f32) * n_lat
            held[:, r, :] = context * (1.0 / total)
    out_ref[...] = held[...].astype(bf16)


def attention(queries, cache, new_latent, lengths, tables, latent, group=8, span=8):
    count, heads, width = queries.shape
    slots = cache.shape[2]
    vmem = pl.BlockSpec(memory_space=pltpu.VMEM)
    return pl.pallas_call(
        functools.partial(attention_kernel, group, span, latent),
        in_specs=[
            pl.BlockSpec(memory_space=pltpu.SMEM),
            pl.BlockSpec(memory_space=pltpu.HBM),
            pl.BlockSpec(memory_space=pltpu.HBM),
            vmem,
            vmem,
        ],
        out_specs=vmem,
        scratch_shapes=[
            pltpu.VMEM(queries.shape, bf16),
            pltpu.VMEM(cache.shape, bf16),
            pltpu.VMEM((heads, count, latent), f32),
            pltpu.SemaphoreType.DMA((count // span,)),
            pltpu.SemaphoreType.DMA((count // span,)),
        ],
        out_shape=jax.ShapeDtypeStruct((heads, count, latent), bf16),
        compiler_params=pltpu.CompilerParams(vmem_limit_bytes=vmem_limit),
        cost_estimate=pl.CostEstimate(
            flops=4 * count * heads * width * slots,
            bytes_accessed=2 * count * width * (heads + slots),
            transcendentals=count * heads * slots,
        ),
        name="attention",
    )(lengths, queries, cache, new_latent, tables)


def value_kernel(block, order_ref, a_ref, v_ref, w_ref, send_ref, keep_ref, value_ref, gathered):
    step = pl.program_id(0)
    heads, width = v_ref.shape[0], v_ref.shape[2]

    @pl.when(step == 0)
    def _():
        for p in range(tp_size):
            gathered[:, p * block : (p + 1) * block, :] = a_ref[order_ref[p]]
        for h in range(heads):
            value_ref[:, h * width : (h + 1) * width] = jnp.dot(
                gathered[h], v_ref[h], preferred_element_type=f32
            ).astype(bf16)

    project(value_ref[...], w_ref, send_ref, keep_ref, block, False)


def project(values, w_ref, send_ref, keep_ref, block, x_major):
    half = values.shape[0] // 2
    if x_major:
        parts = []
        for c in range(core_size):
            for px in range(x_size):
                for pz in range(z_size):
                    at = ((c * z_size + pz) * x_size + px) * block
                    parts.append(values[at : at + block])
        values = jnp.concatenate(parts, axis=0)
    result = jnp.dot(values, w_ref[...], preferred_element_type=f32).astype(bf16)
    keep_ref[...] = result[:half]
    send_ref[...] = result[half:]


def out_kernel(block, v_ref, w_ref, send_ref, keep_ref):
    project(v_ref[...], w_ref, send_ref, keep_ref, block, True)


def value_and_out(order, arrived, value_weight, w_out, start, columns, tile):
    sources, heads, block, latent = arrived.shape
    rows = sources * block
    depth = w_out.shape[0]
    first = start // tile
    return pl.pallas_call(
        functools.partial(value_kernel, block),
        grid_spec=pltpu.PrefetchScalarGridSpec(
            num_scalar_prefetch=1,
            grid=(columns // tile,),
            in_specs=[
                pl.BlockSpec(arrived.shape, lambda i, o: (0, 0, 0, 0)),
                pl.BlockSpec(value_weight.shape, lambda i, o: (0, 0, 0)),
                pl.BlockSpec((depth, tile), lambda i, o: (0, first + i)),
            ],
            out_specs=[
                pl.BlockSpec((rows // 2, tile), lambda i, o: (0, i)),
                pl.BlockSpec((rows // 2, tile), lambda i, o: (0, i)),
                pl.BlockSpec((rows, depth), lambda i, o: (0, 0)),
            ],
            scratch_shapes=[pltpu.VMEM((heads, rows, latent), bf16)],
        ),
        out_shape=[
            jax.ShapeDtypeStruct((rows // 2, columns), bf16),
            jax.ShapeDtypeStruct((rows // 2, columns), bf16),
            jax.ShapeDtypeStruct((rows, depth), bf16),
        ],
        compiler_params=pltpu.CompilerParams(vmem_limit_bytes=large_vmem),
        cost_estimate=pl.CostEstimate(
            flops=2 * rows * depth * (columns + latent),
            bytes_accessed=2 * depth * columns,
            transcendentals=0,
        ),
        name="value_out",
    )(order, arrived, value_weight, w_out)


def out_only(values, w_out, block, start, columns, tile):
    rows, depth = values.shape
    first = start // tile
    return pl.pallas_call(
        functools.partial(out_kernel, block),
        grid=(columns // tile,),
        in_specs=[
            pl.BlockSpec((rows, depth), lambda i: (0, 0)),
            pl.BlockSpec((depth, tile), lambda i: (0, first + i)),
        ],
        out_specs=[
            pl.BlockSpec((rows // 2, tile), lambda i: (0, i)),
            pl.BlockSpec((rows // 2, tile), lambda i: (0, i)),
        ],
        out_shape=[
            jax.ShapeDtypeStruct((rows // 2, columns), bf16),
            jax.ShapeDtypeStruct((rows // 2, columns), bf16),
        ],
        compiler_params=pltpu.CompilerParams(vmem_limit_bytes=large_vmem),
        cost_estimate=pl.CostEstimate(
            flops=2 * rows * depth * columns, bytes_accessed=2 * depth * columns, transcendentals=0
        ),
        name="out_proj",
    )(values, w_out)


def gated_kernel(layout, start, tile, first, last, width, *refs):
    pieces = 1 + max(p for p, _ in layout)
    refs = list(refs)
    order_ref = refs.pop(0)
    x_refs = [refs.pop(0) for _ in range(pieces)]
    gain_ref, gate_ref, up_ref = refs.pop(0), refs.pop(0), refs.pop(0)
    if not first:
        acc_in, square_in = refs.pop(0), refs.pop(0)
    if last:
        out_ref, scaled_ref, ordered = refs
    else:
        acc_ref, square_ref, scaled_ref = refs
    block, lanes = 16, 128
    columns = x_refs[0].shape[1]
    hidden = gate_ref.shape[1]

    squares = None if first else square_in[...]
    for k in range(0, columns, tile):
        wide = jnp.concatenate(
            [x_refs[p][at : at + block, k : k + tile] for p, at in layout], axis=0
        ).astype(f32)
        for j in range(0, tile, lanes):
            part = wide[:, j : j + lanes]
            squares = part * part if squares is None else squares + part * part
        gain = gain_ref[:, start + k : start + k + tile].astype(f32)
        scaled_ref[:, k : k + tile] = (wide * gain).astype(bf16)

    def product(w_ref):
        return jnp.dot(
            scaled_ref[...], w_ref[start : start + columns, :], preferred_element_type=f32
        )

    if not last:
        acc_ref[:, :hidden] = product(gate_ref)
        acc_ref[:, hidden:] = product(up_ref)
        square_ref[...] = squares
        return
    scale = lax.rsqrt(jnp.sum(squares, axis=-1, keepdims=True) * (1.0 / width) + 1e-06)
    gate = (product(gate_ref) + acc_in[:, :hidden]) * scale
    up = (product(up_ref) + acc_in[:, hidden:]) * scale
    active = gate / (1.0 + jnp.exp(-gate)) * up
    for p in range(tp_size):
        at = pl.multiple_of(order_ref[p] * 8, 8)
        for m in range(2):
            begin = p * block + m * 8
            ordered[m, pl.ds(at, 8), :] = active[begin : begin + 8]
    out_ref[...] = ordered[...].astype(bf16)


def gated(order, pieces, layout, gain, gate, up, start, tile, carried, width):
    first = carried is None
    last = not first
    columns = pieces[0].shape[1]
    hidden = gate.shape[1]
    rows = sum(p.shape[0] for p in pieces)
    args = [order] + list(pieces) + [gain, gate, up]
    acc_shape, square_shape = (rows, 2 * hidden), (rows, 128)
    if not first:
        args += list(carried)
    vmem = pl.BlockSpec(memory_space=pltpu.VMEM)
    in_specs = [pl.BlockSpec(memory_space=pltpu.SMEM)] + [vmem] * (len(args) - 1)
    scratch = [pltpu.VMEM((rows, columns), bf16)]
    if last:
        out_dims = (2, rows // 2, hidden)
        out_specs = vmem
        out_shape = jax.ShapeDtypeStruct(out_dims, bf16)
        scratch += [pltpu.VMEM(out_dims, f32)]
    else:
        out_specs = [vmem, vmem]
        out_shape = [jax.ShapeDtypeStruct(acc_shape, f32), jax.ShapeDtypeStruct(square_shape, f32)]
    return pl.pallas_call(
        functools.partial(gated_kernel, layout, start, tile, first, last, width),
        in_specs=in_specs,
        out_specs=out_specs,
        scratch_shapes=scratch,
        out_shape=out_shape,
        compiler_params=pltpu.CompilerParams(vmem_limit_bytes=vmem_limit),
        cost_estimate=pl.CostEstimate(
            flops=4 * rows * columns * hidden,
            bytes_accessed=4 * columns * hidden,
            transcendentals=0,
        ),
        name="gated_pair",
    )(*args)


def shards(
    residual,
    queries,
    latent_cache,
    new_latent,
    lengths,
    positions,
    latent_value_weight,
    w_out,
    norm_gain,
    gate_weight,
    up_weight,
):
    latent = latent_value_weight.shape[1]
    micro, own_rows, width = residual.shape
    block = micro * own_rows
    heads = queries.shape[2]
    me = lax.axis_index("tp")
    my_x, my_z, my_c = me // 4, (me // 2) % 2, me % 2
    order = jnp.stack(
        [
            ((my_x + px) % 4) * 4 + (my_z ^ pz) * 2 + (my_c ^ pc)
            for pc in range(core_size)
            for pz in range(z_size)
            for px in range(x_size)
        ]
    ).astype(jnp.int32)
    tables = rotary_tables(positions.reshape(-1), queries.shape[3] - latent)
    attended = attention(
        queries.reshape((block,) + queries.shape[2:]),
        jnp.swapaxes(latent_cache, 2, 3).reshape(block, latent_cache.shape[3], -1),
        new_latent.reshape(block, -1),
        lengths,
        tables,
        latent,
    )
    arrived = lax.all_to_all(
        attended.reshape(tp_size, heads // tp_size, block, latent),
        "tp",
        split_axis=0,
        concat_axis=0,
        tiled=True,
    )
    cut = 4096
    tile = 1024
    send_b, keep_b, values = value_and_out(
        order, arrived, latent_value_weight, w_out, cut, width - cut, tile
    )
    send_a, keep_a = out_only(values, w_out, block, 0, cut, tile)
    flat_residual = residual.reshape(block, width).astype(f32)

    def add(*parts):
        total = parts[0].astype(f32)
        for part in parts[1:]:
            total = total + part.astype(f32)
        return total

    def x_sum(value, rows):
        right = send(value[rows : 2 * rows], dx=1)
        left = send(value[3 * rows :], dx=3)
        across = send(value[2 * rows : 3 * rows], dx=2)
        return value[:rows], right, left, across

    def x_gather(value):
        return [value, send(value, dx=3), send(value, dx=2), send(value, dx=1)]

    pair_b = add(keep_b, send(send_b, dc=1)).astype(bf16)
    pair_a = add(keep_a, send(send_a, dc=1)).astype(bf16)
    line_b = add(pair_b[: 4 * block], send(pair_b[4 * block :], dz=1)).astype(bf16)
    line_a = add(*x_sum(pair_a, 2 * block))
    line_a = jnp.concatenate(
        [line_a[:block] + flat_residual[:, :cut], line_a[block:]], axis=0
    ).astype(bf16)
    other_a = send(line_a, dz=1)
    both_a = jnp.concatenate(
        [add(line_a[:block], other_a[block:]), add(line_a[block:], other_a[:block])], axis=0
    ).astype(bf16)
    after_a = both_a[:block]
    after_b = add(flat_residual[:, cut:], *x_sum(line_b, block)).astype(bf16)

    near_b = jnp.concatenate(x_gather(after_b), axis=0)
    pieces_a = x_gather(both_a)
    far_b = send(near_b, dz=1)
    pieces_a = pieces_a + [send(g, dc=1) for g in pieces_a]
    near_core_b = send(near_b, dc=1)

    canonical = [
        (pc, pz, px) for pc in range(core_size) for pz in range(z_size) for px in range(x_size)
    ]
    layout_a = [(pc * 4 + px, pz * block) for pc, pz, px in canonical]
    layout_b = [(pc * 2 + pz, px * block) for pc, pz, px in canonical]
    gain_row = norm_gain.reshape(1, width)
    k_tile = 512
    carried = gated(
        order, pieces_a, layout_a, gain_row, gate_weight, up_weight, 0, k_tile, None, width
    )
    pieces_b = [near_b, far_b, near_core_b, send(far_b, dc=1)]
    activation = gated(
        order, pieces_b, layout_b, gain_row, gate_weight, up_weight, cut, k_tile, carried, width
    )
    after_attention = jnp.concatenate([after_a, after_b], axis=1).reshape(residual.shape)
    return (after_attention, activation)


def solution(mesh):
    return jax.shard_map(
        shards,
        mesh=mesh,
        in_specs=(
            P(None, ("dp", "tp"), None),
            P(None, ("dp", "tp"), None, None),
            P(None, ("dp", "tp"), None, None),
            P(None, ("dp", "tp"), None),
            P(None, ("dp", "tp")),
            P(None, ("dp", "tp")),
            P("tp", None, None),
            P("tp", None),
            P(),
            P(None, "tp"),
            P(None, "tp"),
        ),
        out_specs=(P(None, ("dp", "tp"), None), P(None, "dp", "tp")),
        check_vma=False,
    )
```

time: 123 us -> 121 us (0.984)
  Pallas kernels: 35.1 us -> 24.5 us
  waiting for transfers between devices: 38.6 us -> 49.1 us
  starting transfers between devices: 37.1 us -> 32.5 us
  local copies, waits for them, and re-layouts: 8.2 us -> 10.6 us
    pallas_call x3, Pallas kernels: 28.2 us -> 13.4 us  [the longest x2 7.98 us: gated(): pl.pallas_call(functools.partial(gated_kernel, layout, start, tile, first...]
    ppermute x24 -> x23, waiting for transfers between devices: 23 us -> 34.1 us  [send(): return lax.ppermute(value, 'tp', tp_perm(dx, dz, dc))]
    ppermute x24 -> x23, starting transfers between devices: 29.8 us -> 25.3 us  [send(): return lax.ppermute(value, 'tp', tp_perm(dx, dz, dc))]
    pallas_call x1, Pallas kernels: 2.92 us -> 5.18 us  [out_only(): pl.pallas_call(functools.partial(out_kernel, block), grid=(columns // til...]
    pallas_call x1, Pallas kernels: 3.95 us -> 5.91 us  [value_and_out(): pl.pallas_call(functools.partial(value_kernel, block), grid_spec=pltpu.Pr...]
    unnamed x13 -> x28, local copies, waits for them, and re-layouts: 7.82 us -> 9.7 us
  transfers between devices with their start and end apart: 25 -> 24, of which waited for: 12 -> 14; matrix products, arithmetic and copies ran while one was open for 1% -> 2% of each run, Pallas kernels for 9% -> 8%
where the time goes in v2:
time: 121 us; the launch traced here: 120 us
  waiting for transfers between devices  49.1 us (41%)
  starting transfers between devices  32.5 us (27%)
  Pallas kernels  24.5 us (20%)
  local copies, waits for them, and re-layouts  10.6 us (9%)
  other arithmetic  2.49 us (2%)
    ppermute x23, waiting for transfers between devices, send(): return lax.ppermute(value, 'tp', tp_perm(dx, dz, dc))  34.1 us
    ppermute x23, starting transfers between devices, send(): return lax.ppermute(value, 'tp', tp_perm(dx, dz, dc))  25.3 us
    all_to_all x1, waiting for transfers between devices, shards(): lax.all_to_all(attended.reshape(tp_size, heads // tp_size, block, latent)...  15 us
    unnamed x28, local copies, waits for them, and re-layouts  9.7 us
    pallas_call x2, Pallas kernels, gated(): pl.pallas_call(functools.partial(gated_kernel, layout, start, tile, first...  7.98 us
    all_to_all x1, starting transfers between devices, shards(): lax.all_to_all(attended.reshape(tp_size, heads // tp_size, block, latent)...  7.19 us
    pallas_call x1, Pallas kernels, value_and_out(): pl.pallas_call(functools.partial(value_kernel, block), grid_spec=pltpu.Pr...  5.91 us
    pallas_call x1, Pallas kernels, attention(): pl.pallas_call(functools.partial(attention_kernel, group, span, latent),...  5.47 us
  transfers between devices with their start and end apart: 24, of which 14 were waited for; matrix products, arithmetic and copies ran while one was open for 2% of the time, Pallas kernels for 8%

profile of v2, /device:TPU:1, one launch (start us, length us, event | category | flops | bytes accessed | tf_op | source)
XLA Modules:
  0.0 120.1 jit_solution(16504989165903956119)
XLA Ops:
  1.6 2.3 %copy-done.1 = bf16[2,8,256,576]{2,3,1,0:T(8,128)(2,1)S(1)} copy-done((bf16[2,8,256,576]{2,3,1,0:T(8,128)(2,1)S(1)}, bf16[2,8,256,576]{2,3,1,0:T(8,128)(2,1)}, u32[]{:S(2)}) %copy-start.1) | copy-done | bytes 4718616
  4.0 1.3 %copy-done.2 = bf16[2,8,64,576]{3,2,1,0:T(8,128)(2,1)S(1)} copy-done((bf16[2,8,64,576]{3,2,1,0:T(8,128)(2,1)S(1)}, bf16[2,8,64,576]{3,2,1,0:T(8,128)(2,1)}, u32[]{:S(2)}) %copy-start.2) | copy-done | bytes 1179672
  6.7 5.5 %attention.1 = bf16[64,16,512]{2,1,0:T(8,128)(2,1)} custom-call(s32[2,8]{1,0:T(2,128)S(1)} %copy-done.5, bf16[16,64,576]{2,1,0:T(8,128)(2,1)S(1)} %bitcast.30, bf16[16,576,256]{2,1,0:T(8,128)(2,1)S(1)} %bitcast.29, bf16[16,576]{1,0:T(8,128)(2,1)S(1)} %bitcast.31, f32[16,128]{1,0:T(8,128)S(1)} %pad_maximum_fusion.3.t_ref), custom_call_target="tpu_custom_call" | custom-call | flops 603979776 | bytes 5898240 | tf_op jit(solution)/shard_map/attention/pallas_call | solution.py:107
  12.2 7.2 %all-to-all-start = ((bf16[16,4,16,512]{3,2,1,0:T(8,128)(2,1)}), bf16[16,4,16,512]{3,2,1,0:T(8,128)(2,1)S(1)}, u32[]{:S(2)}, u32[]{:S(2)}) async-start(bf16[16,4,16,512]{3,2,1,0:T(8,128)(2,1)} %bitcast.20), calls=%async_computation | async-start | bytes 2097152 | tf_op jit(solution)/shard_map/all_to_all | solution.py:355
  20.0 15.0 %all-to-all-done.a_ref = bf16[16,4,16,512]{3,2,1,0:T(8,128)(2,1)S(1)} async-done(((bf16[16,4,16,512]{3,2,1,0:T(8,128)(2,1)}), bf16[16,4,16,512]{3,2,1,0:T(8,128)(2,1)S(1)}, u32[]{:S(2)}, u32[]{:S(2)}) %all-to-all-start) | async-done | bytes 1048608 | tf_op jit(solution)/shard_map/all_to_all | solution.py:355
  35.1 1.0 copy-done.6
  36.1 5.9 %value_out.1 = (bf16[128,3072]{1,0:T(8,128)(2,1)}, bf16[128,3072]{1,0:T(8,128)(2,1)}, bf16[256,512]{1,0:T(8,128)(2,1)}) custom-call(s32[16]{0:T(128)} %stack.67.order_ref.refs_0_, bf16[16,4,16,512]{3,2,1,0:T(8,128)(2,1)} %copy-done.6, bf16[4,512,128]{2,1,0:T(8,128)(2,1)} %v_ref.1, bf16[512,7168]{1,0:T(8,128)(2,1)} %w_ref.3), custom_call_target="tpu_custom_call" | custom-call | flops 939524096 | bytes 3145728 | tf_op jit(solution)/shard_map/value_out/pallas_call | solution.py:175
  42.0 0.9 collective-permute-start.5
  42.8 5.2 %out_proj.1 = (bf16[128,4096]{1,0:T(8,128)(2,1)}, bf16[128,4096]{1,0:T(8,128)(2,1)}) custom-call(bf16[256,512]{1,0:T(8,128)(2,1)} %get-tuple-element.9.v_ref, bf16[512,7168]{1,0:T(8,128)(2,1)} %w_ref.3), custom_call_target="tpu_custom_call" | custom-call | flops 1073741824 | bytes 4194304 | tf_op jit(solution)/shard_map/out_proj/pallas_call | solution.py:210
  48.9 2.1 %collective-permute-done = bf16[128,4096]{1,0:T(8,128)(2,1)S(1)} collective-permute-done((bf16[128,4096]{1,0:T(8,128)(2,1)}, bf16[128,4096]{1,0:T(8,128)(2,1)S(1)}, u32[]{:S(2)}, u32[]{:S(2)}) %collective-permute-start) | collective-permute-done | bytes 1048608 | tf_op jit(solution)/shard_map/ppermute | solution.py:30
  51.2 7.5 %collective-permute-done.6 = bf16[64,3072]{1,0:T(8,128)(2,1)S(1)} collective-permute-done((bf16[64,3072]{1,0:T(8,128)(2,1)S(1)}, bf16[64,3072]{1,0:T(8,128)(2,1)S(1)}, u32[]{:S(2)}, u32[]{:S(2)}) %collective-permute-start.6) | collective-permute-done | bytes 393248 | tf_op jit(solution)/shard_map/ppermute | solution.py:30
  58.9 1.8 %collective-permute-start.9 = (bf16[16,3072]{1,0:T(8,128)(2,1)S(1)}, bf16[16,3072]{1,0:T(8,128)(2,1)S(1)}, u32[]{:S(2)}, u32[]{:S(2)}) collective-permute-start(bf16[16,3072]{1,0:T(8,128)(2,1)S(1)} %get-tuple-element.20), channel_id=1, source_target_pairs={{0,8},{1,9},{2,10},{3,11},{4,12},{5,13},{6,14},{7,15},{8,0},{9,1},... | collective-permute-start | bytes 294920 | tf_op jit(solution)/shard_map/ppermute | solution.py:30
  60.8 1.2 collective-permute-start.8
  62.4 1.8 %collective-permute-start.3 = (bf16[32,4096]{1,0:T(8,128)(2,1)S(1)}, bf16[32,4096]{1,0:T(8,128)(2,1)S(1)}, u32[]{:S(2)}, u32[]{:S(2)}) collective-permute-start(bf16[32,4096]{1,0:T(8,128)(2,1)S(1)} %get-tuple-element.17), channel_id=1, source_target_pairs={{0,8},{1,9},{2,10},{3,11},{4,12},{5,13},{6,14},{7,15},{8,0},{9,1},... | collective-permute-start | bytes 786440 | tf_op jit(solution)/shard_map/ppermute | solution.py:30
  64.2 0.9 collective-permute-done.7
  65.1 1.1 collective-permute-start.2
  66.7 2.2 %collective-permute-start.11 = (bf16[16,3072]{1,0:T(8,128)(2,1)S(1)}, bf16[16,3072]{1,0:T(8,128)(2,1)S(1)}, u32[]{:S(2)}, u32[]{:S(2)}) collective-permute-start(bf16[16,3072]{1,0:T(8,128)(2,1)S(1)} %fusion.4), channel_id=1, source_target_pairs={{0,8},{1,9},{2,10},{3,11},{4,12},{5,13},{6,14},{7,15},{8,0},{9,1},... | collective-permute-start | bytes 294920 | tf_op jit(solution)/shard_map/ppermute | solution.py:30
  69.0 2.5 %collective-permute-done.1 = bf16[32,4096]{1,0:T(8,128)(2,1)S(1)} collective-permute-done((bf16[32,4096]{1,0:T(8,128)(2,1)S(1)}, bf16[32,4096]{1,0:T(8,128)(2,1)S(1)}, u32[]{:S(2)}, u32[]{:S(2)}) %collective-permute-start.1) | collective-permute-done | bytes 262176 | tf_op jit(solution)/shard_map/ppermute | solution.py:30
  71.4 4.9 %collective-permute-done.3 = bf16[32,4096]{1,0:T(8,128)(2,1)S(1)} collective-permute-done((bf16[32,4096]{1,0:T(8,128)(2,1)S(1)}, bf16[32,4096]{1,0:T(8,128)(2,1)S(1)}, u32[]{:S(2)}, u32[]{:S(2)}) %collective-permute-start.3) | collective-permute-done | bytes 262176 | tf_op jit(solution)/shard_map/ppermute | solution.py:30
  76.3 2.0 %collective-permute-done.2 = bf16[32,4096]{1,0:T(8,128)(2,1)S(1)} collective-permute-done((bf16[32,4096]{1,0:T(8,128)(2,1)S(1)}, bf16[32,4096]{1,0:T(8,128)(2,1)S(1)}, u32[]{:S(2)}, u32[]{:S(2)}) %collective-permute-start.2) | collective-permute-done | bytes 262176 | tf_op jit(solution)/shard_map/ppermute | solution.py:30
  78.6 1.2 collective-permute-start.4
  80.2 0.9 collective-permute-done.10
  81.5 2.7 %collective-permute-done.4 = bf16[32,4096]{1,0:T(8,128)(2,1)S(1)} collective-permute-done((bf16[32,4096]{1,0:T(8,128)(2,1)S(1)}, bf16[32,4096]{1,0:T(8,128)(2,1)S(1)}, u32[]{:S(2)}, u32[]{:S(2)}) %collective-permute-start.4) | collective-permute-done | bytes 262176 | tf_op jit(solution)/shard_map/ppermute | solution.py:30
  84.3 6.6 %collective-permute-start.19 = (bf16[32,4096]{1,0:T(8,128)(2,1)S(1)}, bf16[32,4096]{1,0:T(8,128)(2,1)S(1)}, u32[]{:S(2)}, u32[]{:S(2)}) collective-permute-start(bf16[32,4096]{1,0:T(8,128)(2,1)S(1)} %pad_maximum_fusion.2.refs_1_), channel_id=1, source_target_pairs={{0,1},{1,0},{2,3},{3,2},{4,5},{5,4},{6,7},{7,6},{8,9},{9,8},{10,11... | collective-permute-start | bytes 786440 | tf_op jit(solution)/shard_map/ppermute | solution.py:30
  90.9 1.3 %collective-permute-start.18 = (bf16[32,4096]{1,0:T(8,128)(2,1)S(1)}, bf16[32,4096]{1,0:T(8,128)(2,1)S(1)}, u32[]{:S(2)}, u32[]{:S(2)}) collective-permute-start(bf16[32,4096]{1,0:T(8,128)(2,1)S(1)} %pad_maximum_fusion.2.refs_1_), channel_id=1, source_target_pairs={{0,4},{1,5},{2,6},{3,7},{4,8},{5,9},{6,10},{7,11},{8,12},{9,13},{1... | collective-permute-start | bytes 786440 | tf_op jit(solution)/shard_map/ppermute | solution.py:30
  92.2 1.9 %collective-permute-start.17 = (bf16[32,4096]{1,0:T(8,128)(2,1)S(1)}, bf16[32,4096]{1,0:T(8,128)(2,1)S(1)}, u32[]{:S(2)}, u32[]{:S(2)}) collective-permute-start(bf16[32,4096]{1,0:T(8,128)(2,1)S(1)} %pad_maximum_fusion.2.refs_1_), channel_id=1, source_target_pairs={{0,8},{1,9},{2,10},{3,11},{4,12},{5,13},{6,14},{7,15},{8,0},{9,1},... | collective-permute-start | bytes 786440 | tf_op jit(solution)/shard_map/ppermute | solution.py:30
  94.6 1.2 %collective-permute-start.14 = (bf16[64,3072]{1,0:T(8,128)(2,1)S(1)}, bf16[64,3072]{1,0:T(8,128)(2,1)S(1)}, u32[]{:S(2)}, u32[]{:S(2)}) collective-permute-start(bf16[64,3072]{1,0:T(8,128)(2,1)S(1)} %pad_maximum_fusion.refs_1_), channel_id=1, source_target_pairs={{0,1},{1,0},{2,3},{3,2},{4,5},{5,4},{6,7},{7,6},{8,9},{9,8},{10,11... | collective-permute-start | bytes 1179656 | tf_op jit(solution)/shard_map/ppermute | solution.py:30
  95.8 4.2 %collective-permute-done.18.refs_4_ = bf16[32,4096]{1,0:T(8,128)(2,1)S(1)} collective-permute-done((bf16[32,4096]{1,0:T(8,128)(2,1)S(1)}, bf16[32,4096]{1,0:T(8,128)(2,1)S(1)}, u32[]{:S(2)}, u32[]{:S(2)}) %collective-permute-start.18) | collective-permute-done | bytes 262176 | tf_op jit(solution)/shard_map/ppermute | solution.py:30
  100.8 5.2 %collective-permute-done.17.refs_3_ = bf16[32,4096]{1,0:T(8,128)(2,1)S(1)} collective-permute-done((bf16[32,4096]{1,0:T(8,128)(2,1)S(1)}, bf16[32,4096]{1,0:T(8,128)(2,1)S(1)}, u32[]{:S(2)}, u32[]{:S(2)}) %collective-permute-start.17) | collective-permute-done | bytes 262176 | tf_op jit(solution)/shard_map/ppermute | solution.py:30
  108.5 3.6 %copy-done = bf16[7168,640]{1,0:T(8,128)(2,1)S(1)} copy-done((bf16[7168,640]{1,0:T(8,128)(2,1)S(1)}, bf16[7168,640]{1,0:T(8,128)(2,1)}, u32[]{:S(2)}) %copy-start) | copy-done | bytes 9175064
  112.1 4.0 %gated_pair.2 = (f32[256,1280]{1,0:T(8,128)S(1)}, f32[256,128]{1,0:T(8,128)S(1)}) custom-call(s32[16]{0:T(128)S(1)} %copy-done.4, bf16[32,4096]{1,0:T(8,128)(2,1)S(1)} %pad_maximum_fusion.2.refs_1_, bf16[32,4096]{1,0:T(8,128)(2,1)S(1)} %collective-permute-done.16.refs_2_, bf16[32,4096]{1,0:T(8,128)(2,1)S(1)} %collective-permute-done.17.refs_3_, ...), custom_call_target="tpu_custom_call" | custom-call | flops 2684354560 | bytes 10485760 | tf_op jit(solution)/shard_map/gated_pair/pallas_call | solution.py:303
  116.2 4.0 %gated_pair.3 = bf16[2,128,640]{2,1,0:T(8,128)(2,1)} custom-call(s32[16]{0:T(128)S(1)} %copy-done.4, bf16[64,3072]{1,0:T(8,128)(2,1)S(1)} %pad_maximum_fusion.refs_1_, bf16[64,3072]{1,0:T(8,128)(2,1)S(1)} %collective-permute-done.13.refs_2_, bf16[64,3072]{1,0:T(8,128)(2,1)S(1)} %collective-permute-done.14.refs_3_, ...), custom_call_target="tpu_custom_call" | custom-call | flops 2013265920 | bytes 7864320 | tf_op jit(solution)/shard_map/gated_pair/pallas_call | solution.py:303
  (73 shorter events, 10.2 us)
Async XLA Ops:
  12.2 22.9 %all-to-all-start = ((bf16[16,4,16,512]{3,2,1,0:T(8,128)(2,1)}), bf16[16,4,16,512]{3,2,1,0:T(8,128)(2,1)S(1)}, u32[]{:S(2)}, u32[]{:S(2)}) async-start(bf16[16,4,16,512]{3,2,1,0:T(8,128)(2,1)} %bitcast.20), calls=%async_computation | async-start | bytes 2097152 | tf_op jit(solution)/shard_map/all_to_all | solution.py:355
  42.0 6.2 %collective-permute-start.5 = (bf16[128,3072]{1,0:T(8,128)(2,1)}, bf16[128,3072]{1,0:T(8,128)(2,1)S(1)}, u32[]{:S(2)}, u32[]{:S(2)}) collective-permute-start(bf16[128,3072]{1,0:T(8,128)(2,1)} %get-tuple-element.13), channel_id=1, source_target_pairs={{0,1},{1,0},{2,3},{3,2},{4,5},{5,4},{6,7},{7,6},{8,9},{9,8},{10,11... | collective-permute-start | bytes 2359304 | tf_op jit(solution)/shard_map/ppermute | solution.py:30
  42.8 5.3 %copy-start.9 = (bf16[2,8,7168]{2,1,0:T(8,128)(2,1)S(1)}, bf16[2,8,7168]{2,1,0:T(8,128)(2,1)}, u32[]{:S(2)}) copy-start(bf16[2,8,7168]{2,1,0:T(8,128)(2,1)} %param.11) | copy-start | bytes 688132
  42.8 5.4 %copy-start.8 = (bf16[128,3072]{1,0:T(8,128)(2,1)S(1)}, bf16[128,3072]{1,0:T(8,128)(2,1)}, u32[]{:S(2)}) copy-start(bf16[128,3072]{1,0:T(8,128)(2,1)} %get-tuple-element.12) | copy-start | bytes 2359300
  42.8 65.6 %slice-start = ((s8[9175040]{0:T(1024)(128)(4,1)}), s8[786432]{0:T(1024)(128)(4,1)S(1)}, s32[]{:S(2)}) async-start(s8[9175040]{0:T(1024)(128)(4,1)} %bitcast.27), calls=%async_computation.1 | async-start | bytes 1572864
  48.0 60.5 %slice-start.1 = ((s8[9175040]{0:T(1024)(128)(4,1)}), s8[4194304]{0:T(1024)(128)(4,1)S(1)}, s32[]{:S(2)}) async-start(s8[9175040]{0:T(1024)(128)(4,1)} %bitcast.27), calls=%async_computation.2 | async-start | bytes 8388608
  48.0 3.0 %collective-permute-start = (bf16[128,4096]{1,0:T(8,128)(2,1)}, bf16[128,4096]{1,0:T(8,128)(2,1)S(1)}, u32[]{:S(2)}, u32[]{:S(2)}) collective-permute-start(bf16[128,4096]{1,0:T(8,128)(2,1)} %get-tuple-element.11), channel_id=1, source_target_pairs={{0,1},{1,0},{2,3},{3,2},{4,5},{5,4},{6,7},{7,6},{8,9},{9,8},{10,11... | collective-permute-start | bytes 3145736 | tf_op jit(solution)/shard_map/ppermute | solution.py:30
  48.4 10.3 %collective-permute-start.6 = (bf16[64,3072]{1,0:T(8,128)(2,1)S(1)}, bf16[64,3072]{1,0:T(8,128)(2,1)S(1)}, u32[]{:S(2)}, u32[]{:S(2)}) collective-permute-start(bf16[64,3072]{1,0:T(8,128)(2,1)S(1)} %slice.84), channel_id=1, source_target_pairs={{0,2},{1,3},{2,0},{3,1},{4,6},{5,7},{6,4},{7,5},{8,10},{9,11},{10,... | collective-permute-start | bytes 1179656 | tf_op jit(solution)/shard_map/ppermute | solution.py:30
  58.8 49.7 %slice-start.2 = ((s8[9175040]{0:T(1024)(128)(4,1)}), s8[4194304]{0:T(1024)(128)(4,1)S(1)}, s32[]{:S(2)}) async-start(s8[9175040]{0:T(1024)(128)(4,1)} %bitcast.27), calls=%async_computation.3 | async-start | bytes 8388608
  58.9 6.2 %collective-permute-start.7 = (bf16[16,3072]{1,0:T(8,128)(2,1)S(1)}, bf16[16,3072]{1,0:T(8,128)(2,1)S(1)}, u32[]{:S(2)}, u32[]{:S(2)}) collective-permute-start(bf16[16,3072]{1,0:T(8,128)(2,1)S(1)} %get-tuple-element.19), channel_id=1, source_target_pairs={{0,4},{1,5},{2,6},{3,7},{4,8},{5,9},{6,10},{7,11},{8,12},{9,13},{1... | collective-permute-start | bytes 294920 | tf_op jit(solution)/shard_map/ppermute | solution.py:30
  58.9 7.2 %collective-permute-start.9 = (bf16[16,3072]{1,0:T(8,128)(2,1)S(1)}, bf16[16,3072]{1,0:T(8,128)(2,1)S(1)}, u32[]{:S(2)}, u32[]{:S(2)}) collective-permute-start(bf16[16,3072]{1,0:T(8,128)(2,1)S(1)} %get-tuple-element.20), channel_id=1, source_target_pairs={{0,8},{1,9},{2,10},{3,11},{4,12},{5,13},{6,14},{7,15},{8,0},{9,1},... | collective-permute-start | bytes 294920 | tf_op jit(solution)/shard_map/ppermute | solution.py:30
  60.8 5.4 %collective-permute-start.8 = (bf16[16,3072]{1,0:T(8,128)(2,1)S(1)}, bf16[16,3072]{1,0:T(8,128)(2,1)S(1)}, u32[]{:S(2)}, u32[]{:S(2)}) collective-permute-start(bf16[16,3072]{1,0:T(8,128)(2,1)S(1)} %get-tuple-element.21), channel_id=1, source_target_pairs={{0,12},{1,13},{2,14},{3,15},{4,0},{5,1},{6,2},{7,3},{8,4},{9,5},{1... | collective-permute-start | bytes 294920 | tf_op jit(solution)/shard_map/ppermute | solution.py:30
  62.0 9.4 %collective-permute-start.1 = (bf16[32,4096]{1,0:T(8,128)(2,1)S(1)}, bf16[32,4096]{1,0:T(8,128)(2,1)S(1)}, u32[]{:S(2)}, u32[]{:S(2)}) collective-permute-start(bf16[32,4096]{1,0:T(8,128)(2,1)S(1)} %get-tuple-element.16), channel_id=1, source_target_pairs={{0,4},{1,5},{2,6},{3,7},{4,8},{5,9},{6,10},{7,11},{8,12},{9,13},{1... | collective-permute-start | bytes 786440 | tf_op jit(solution)/shard_map/ppermute | solution.py:30
  62.4 13.9 %collective-permute-start.3 = (bf16[32,4096]{1,0:T(8,128)(2,1)S(1)}, bf16[32,4096]{1,0:T(8,128)(2,1)S(1)}, u32[]{:S(2)}, u32[]{:S(2)}) collective-permute-start(bf16[32,4096]{1,0:T(8,128)(2,1)S(1)} %get-tuple-element.17), channel_id=1, source_target_pairs={{0,8},{1,9},{2,10},{3,11},{4,12},{5,13},{6,14},{7,15},{8,0},{9,1},... | collective-permute-start | bytes 786440 | tf_op jit(solution)/shard_map/ppermute | solution.py:30
  65.1 13.2 %collective-permute-start.2 = (bf16[32,4096]{1,0:T(8,128)(2,1)S(1)}, bf16[32,4096]{1,0:T(8,128)(2,1)S(1)}, u32[]{:S(2)}, u32[]{:S(2)}) collective-permute-start(bf16[32,4096]{1,0:T(8,128)(2,1)S(1)} %get-tuple-element.18), channel_id=1, source_target_pairs={{0,12},{1,13},{2,14},{3,15},{4,0},{5,1},{6,2},{7,3},{8,4},{9,5},{1... | collective-permute-start | bytes 786440 | tf_op jit(solution)/shard_map/ppermute | solution.py:30
  66.3 13.5 %collective-permute-start.12 = (bf16[16,3072]{1,0:T(8,128)(2,1)S(1)}, bf16[16,3072]{1,0:T(8,128)(2,1)S(1)}, u32[]{:S(2)}, u32[]{:S(2)}) collective-permute-start(bf16[16,3072]{1,0:T(8,128)(2,1)S(1)} %fusion.4), channel_id=1, source_target_pairs={{0,4},{1,5},{2,6},{3,7},{4,8},{5,9},{6,10},{7,11},{8,12},{9,13},{1... | collective-permute-start | bytes 294920 | tf_op jit(solution)/shard_map/ppermute | solution.py:30
  66.7 13.5 %collective-permute-start.11 = (bf16[16,3072]{1,0:T(8,128)(2,1)S(1)}, bf16[16,3072]{1,0:T(8,128)(2,1)S(1)}, u32[]{:S(2)}, u32[]{:S(2)}) collective-permute-start(bf16[16,3072]{1,0:T(8,128)(2,1)S(1)} %fusion.4), channel_id=1, source_target_pairs={{0,8},{1,9},{2,10},{3,11},{4,12},{5,13},{6,14},{7,15},{8,0},{9,1},... | collective-permute-start | bytes 294920 | tf_op jit(solution)/shard_map/ppermute | solution.py:30
  71.4 9.7 %collective-permute-start.10 = (bf16[16,3072]{1,0:T(8,128)(2,1)S(1)}, bf16[16,3072]{1,0:T(8,128)(2,1)S(1)}, u32[]{:S(2)}, u32[]{:S(2)}) collective-permute-start(bf16[16,3072]{1,0:T(8,128)(2,1)S(1)} %fusion.4), channel_id=1, source_target_pairs={{0,12},{1,13},{2,14},{3,15},{4,0},{5,1},{6,2},{7,3},{8,4},{9,5},{1... | collective-permute-start | bytes 294920 | tf_op jit(solution)/shard_map/ppermute | solution.py:30
  78.5 16.1 %copy-start.10 = (bf16[7168]{0:T(1024)(128)(2,1)S(1)}, bf16[7168]{0:T(1024)(128)(2,1)}, u32[]{:S(2)}) copy-start(bf16[7168]{0:T(1024)(128)(2,1)} %param.19) | copy-start | bytes 43012
  78.5 30.0 %copy-start.4 = (s32[16]{0:T(128)S(1)}, s32[16]{0:T(128)}, u32[]{:S(2)}) copy-start(s32[16]{0:T(128)} %stack.67.order_ref.refs_0_) | copy-start | bytes 196
  78.6 5.6 %collective-permute-start.4 = (bf16[32,4096]{1,0:T(8,128)(2,1)S(1)}, bf16[32,4096]{1,0:T(8,128)(2,1)S(1)}, u32[]{:S(2)}, u32[]{:S(2)}) collective-permute-start(bf16[32,4096]{1,0:T(8,128)(2,1)S(1)} %pad_maximum_fusion.1), channel_id=1, source_target_pairs={{0,2},{1,3},{2,0},{3,1},{4,6},{5,7},{6,4},{7,5},{8,10},{9,11},{10,... | collective-permute-start | bytes 786440 | tf_op jit(solution)/shard_map/ppermute | solution.py:30
  81.2 13.4 %collective-permute-start.13 = (bf16[64,3072]{1,0:T(8,128)(2,1)S(1)}, bf16[64,3072]{1,0:T(8,128)(2,1)S(1)}, u32[]{:S(2)}, u32[]{:S(2)}) collective-permute-start(bf16[64,3072]{1,0:T(8,128)(2,1)S(1)} %pad_maximum_fusion.refs_1_), channel_id=1, source_target_pairs={{0,2},{1,3},{2,0},{3,1},{4,6},{5,7},{6,4},{7,5},{8,10},{9,11},{10,... | collective-permute-start | bytes 1179656 | tf_op jit(solution)/shard_map/ppermute | solution.py:30
  84.3 11.5 %collective-permute-start.19 = (bf16[32,4096]{1,0:T(8,128)(2,1)S(1)}, bf16[32,4096]{1,0:T(8,128)(2,1)S(1)}, u32[]{:S(2)}, u32[]{:S(2)}) collective-permute-start(bf16[32,4096]{1,0:T(8,128)(2,1)S(1)} %pad_maximum_fusion.2.refs_1_), channel_id=1, source_target_pairs={{0,1},{1,0},{2,3},{3,2},{4,5},{5,4},{6,7},{7,6},{8,9},{9,8},{10,11... | collective-permute-start | bytes 786440 | tf_op jit(solution)/shard_map/ppermute | solution.py:30
  90.9 9.1 %collective-permute-start.18 = (bf16[32,4096]{1,0:T(8,128)(2,1)S(1)}, bf16[32,4096]{1,0:T(8,128)(2,1)S(1)}, u32[]{:S(2)}, u32[]{:S(2)}) collective-permute-start(bf16[32,4096]{1,0:T(8,128)(2,1)S(1)} %pad_maximum_fusion.2.refs_1_), channel_id=1, source_target_pairs={{0,4},{1,5},{2,6},{3,7},{4,8},{5,9},{6,10},{7,11},{8,12},{9,13},{1... | collective-permute-start | bytes 786440 | tf_op jit(solution)/shard_map/ppermute | solution.py:30
  92.2 13.9 %collective-permute-start.17 = (bf16[32,4096]{1,0:T(8,128)(2,1)S(1)}, bf16[32,4096]{1,0:T(8,128)(2,1)S(1)}, u32[]{:S(2)}, u32[]{:S(2)}) collective-permute-start(bf16[32,4096]{1,0:T(8,128)(2,1)S(1)} %pad_maximum_fusion.2.refs_1_), channel_id=1, source_target_pairs={{0,8},{1,9},{2,10},{3,11},{4,12},{5,13},{6,14},{7,15},{8,0},{9,1},... | collective-permute-start | bytes 786440 | tf_op jit(solution)/shard_map/ppermute | solution.py:30
  94.1 12.9 %collective-permute-start.16 = (bf16[32,4096]{1,0:T(8,128)(2,1)S(1)}, bf16[32,4096]{1,0:T(8,128)(2,1)S(1)}, u32[]{:S(2)}, u32[]{:S(2)}) collective-permute-start(bf16[32,4096]{1,0:T(8,128)(2,1)S(1)} %pad_maximum_fusion.2.refs_1_), channel_id=1, source_target_pairs={{0,12},{1,13},{2,14},{3,15},{4,0},{5,1},{6,2},{7,3},{8,4},{9,5},{1... | collective-permute-start | bytes 786440 | tf_op jit(solution)/shard_map/ppermute | solution.py:30
  94.6 21.6 %collective-permute-start.14 = (bf16[64,3072]{1,0:T(8,128)(2,1)S(1)}, bf16[64,3072]{1,0:T(8,128)(2,1)S(1)}, u32[]{:S(2)}, u32[]{:S(2)}) collective-permute-start(bf16[64,3072]{1,0:T(8,128)(2,1)S(1)} %pad_maximum_fusion.refs_1_), channel_id=1, source_target_pairs={{0,1},{1,0},{2,3},{3,2},{4,5},{5,4},{6,7},{7,6},{8,9},{9,8},{10,11... | collective-permute-start | bytes 1179656 | tf_op jit(solution)/shard_map/ppermute | solution.py:30
  95.8 20.3 %collective-permute-start.15 = (bf16[64,3072]{1,0:T(8,128)(2,1)S(1)}, bf16[64,3072]{1,0:T(8,128)(2,1)S(1)}, u32[]{:S(2)}, u32[]{:S(2)}) collective-permute-start(bf16[64,3072]{1,0:T(8,128)(2,1)S(1)} %collective-permute-done.13.refs_2_), channel_id=1, source_target_pairs={{0,1},{1,0},{2,3},{3,2},{4,5},{5,4},{6,7},{7,6},{8,9},{9,8},{10,11... | collective-permute-start | bytes 1179656 | tf_op jit(solution)/shard_map/ppermute | solution.py:30
  100.0 7.8 %collective-permute-start.22 = (bf16[32,4096]{1,0:T(8,128)(2,1)S(1)}, bf16[32,4096]{1,0:T(8,128)(2,1)S(1)}, u32[]{:S(2)}, u32[]{:S(2)}) collective-permute-start(bf16[32,4096]{1,0:T(8,128)(2,1)S(1)} %collective-permute-done.18.refs_4_), channel_id=1, source_target_pairs={{0,1},{1,0},{2,3},{3,2},{4,5},{5,4},{6,7},{7,6},{8,9},{9,8},{10,11... | collective-permute-start | bytes 786440 | tf_op jit(solution)/shard_map/ppermute | solution.py:30
  106.1 2.0 %collective-permute-start.21 = (bf16[32,4096]{1,0:T(8,128)(2,1)S(1)}, bf16[32,4096]{1,0:T(8,128)(2,1)S(1)}, u32[]{:S(2)}, u32[]{:S(2)}) collective-permute-start(bf16[32,4096]{1,0:T(8,128)(2,1)S(1)} %collective-permute-done.17.refs_3_), channel_id=1, source_target_pairs={{0,1},{1,0},{2,3},{3,2},{4,5},{5,4},{6,7},{7,6},{8,9},{9,8},{10,11... | collective-permute-start | bytes 786440 | tf_op jit(solution)/shard_map/ppermute | solution.py:30
  106.9 1.5 %collective-permute-start.20 = (bf16[32,4096]{1,0:T(8,128)(2,1)S(1)}, bf16[32,4096]{1,0:T(8,128)(2,1)S(1)}, u32[]{:S(2)}, u32[]{:S(2)}) collective-permute-start(bf16[32,4096]{1,0:T(8,128)(2,1)S(1)} %collective-permute-done.16.refs_2_), channel_id=1, source_target_pairs={{0,1},{1,0},{2,3},{3,2},{4,5},{5,4},{6,7},{7,6},{8,9},{9,8},{10,11... | collective-permute-start | bytes 786440 | tf_op jit(solution)/shard_map/ppermute | solution.py:30
  108.5 3.6 %copy-start = (bf16[7168,640]{1,0:T(8,128)(2,1)S(1)}, bf16[7168,640]{1,0:T(8,128)(2,1)}, u32[]{:S(2)}) copy-start(bf16[7168,640]{1,0:T(8,128)(2,1)} %refs_7_.1) | copy-start | bytes 27525124
  (6 other events, 9.0 us)

commit v3 on v2

v3 whole, which is shorter than its diff:
```python
import functools

import jax
import jax.numpy as jnp
import numpy as np
from jax import lax
from jax.experimental import pallas as pl
from jax.experimental.pallas import tpu as pltpu
from jax.sharding import PartitionSpec as P

score_scale = 192.0 ** (-0.5)
neg_large = -1e30
f32 = jnp.float32
bf16 = jnp.bfloat16
vmem_limit = 20 * 1024 * 1024
large_vmem = 56 * 1024 * 1024
x_size, z_size, core_size = 4, 2, 2
tp_size = x_size * z_size * core_size


flips = {"p": (1, 0, 0), "q": (3, 0, 0), "z": (0, 1, 0), "c": (0, 0, 1)}


def send(value, *dims):
    pairs = []
    for i in range(tp_size):
        x, z, c = i // 4, (i // 2) % 2, i % 2
        for dim in dims:
            fx, fz, fc = flips[dim]
            x, z, c = x ^ fx, z ^ fz, c ^ fc
        pairs.append((i, x * 4 + z * 2 + c))
    return lax.ppermute(value, "tp", pairs)


def rotary_tables(positions, rope):
    half = rope // 2
    exponent = jnp.arange(half, dtype=f32) * (2.0 / rope)
    angles = positions.astype(f32)[..., None] * (10000.0 ** (-exponent))
    cosine, sine = jnp.cos(angles), jnp.sin(angles)
    return jnp.concatenate([cosine, cosine, -sine, sine], axis=-1)


def attention_kernel(
    group, span, latent, len_ref, q_hbm, c_hbm, n_ref, t_ref, out_ref, q_ref, c_ref, held, q_sem, c_sem
):
    count, heads, width = q_ref.shape
    rope = width - latent
    half = rope // 2
    per = len_ref.shape[1]

    copies = []
    for i in range(count // span):
        at = pl.ds(i * span, span)
        copies.append(
            (
                pltpu.make_async_copy(q_hbm.at[at], q_ref.at[at], q_sem.at[i]),
                pltpu.make_async_copy(c_hbm.at[at], c_ref.at[at], c_sem.at[i]),
            )
        )
    for pair in copies:
        for copy in pair:
            copy.start()

    def turn(values, cosine, sine):
        swapped = jnp.concatenate([values[:, half:], values[:, :half]], axis=-1)
        return (values * cosine + swapped * sine).astype(bf16)

    for begin in range(0, count, group):
        scored = []
        for r in range(begin, begin + group):
            if r % span == 0:
                for copy in copies[r // span]:
                    copy.wait()
            table = t_ref[r : r + 1, :]
            cosine, sine = table[:, :rope], table[:, rope:]
            q_lat = q_ref[r, :, :latent]
            q_rope = turn(q_ref[r, :, latent:].astype(f32), cosine, sine)
            n_lat = n_ref[r : r + 1, :latent].astype(f32)
            n_rope = turn(n_ref[r : r + 1, latent:].astype(f32), cosine, sine).astype(f32)
            scores = jnp.dot(q_lat, c_ref[r, :latent, :], preferred_element_type=f32)
            scores += jnp.dot(q_rope, c_ref[r, latent:, :], preferred_element_type=f32)
            own = jnp.sum(q_lat.astype(f32) * n_lat, axis=-1, keepdims=True)
            own += jnp.sum(q_rope.astype(f32) * n_rope, axis=-1, keepdims=True)
            scored.append((scores, own * score_scale, n_lat))
        weighted = []
        for r in range(begin, begin + group):
            scores, own, n_lat = scored[r - begin]
            visible = lax.broadcasted_iota(jnp.int32, scores.shape, 1) < len_ref[r // per, r % per]
            scores = jnp.where(visible, scores * score_scale, neg_large)
            top = jnp.maximum(jnp.max(scores, axis=-1, keepdims=True), own)
            weights = jnp.where(visible, jnp.exp(scores - top), 0.0)
            own_weight = jnp.exp(own - top)
            total = jnp.sum(weights, axis=-1, keepdims=True) + own_weight
            weighted.append((weights.astype(bf16), own_weight, total, n_lat))
        for r in range(begin, begin + group):
            weights, own_weight, total, n_lat = weighted[r - begin]
            context = lax.dot_general(
                weights, c_ref[r, :latent, :], (((1,), (1,)), ((), ())), preferred_element_type=f32
            )
            context += own_weight.astype(bf16).astype(f32) * n_lat
            held[:, r, :] = context * (1.0 / total)
    out_ref[...] = held[...].astype(bf16)


def attention(queries, cache, new_latent, lengths, tables, latent, group=8, span=4):
    count, heads, width = queries.shape
    slots = cache.shape[2]
    vmem = pl.BlockSpec(memory_space=pltpu.VMEM)
    return pl.pallas_call(
        functools.partial(attention_kernel, group, span, latent),
        in_specs=[
            pl.BlockSpec(memory_space=pltpu.SMEM),
            pl.BlockSpec(memory_space=pltpu.HBM),
            pl.BlockSpec(memory_space=pltpu.HBM),
            vmem,
            vmem,
        ],
        out_specs=vmem,
        scratch_shapes=[
            pltpu.VMEM(queries.shape, bf16),
            pltpu.VMEM(cache.shape, bf16),
            pltpu.VMEM((heads, count, latent), f32),
            pltpu.SemaphoreType.DMA((count // span,)),
            pltpu.SemaphoreType.DMA((count // span,)),
        ],
        out_shape=jax.ShapeDtypeStruct((heads, count, latent), bf16),
        compiler_params=pltpu.CompilerParams(vmem_limit_bytes=large_vmem),
        cost_estimate=pl.CostEstimate(
            flops=4 * count * heads * width * slots,
            bytes_accessed=2 * count * width * (heads + slots),
            transcendentals=count * heads * slots,
        ),
        name="attention",
    )(lengths, queries, cache, new_latent, tables)


def out_kernel(block, spans, orders, with_values, *refs):
    refs = list(refs)
    if with_values:
        order_ref, a_ref, v_ref = refs.pop(0), refs.pop(0), refs.pop(0)
    else:
        value_ref = refs.pop(0)
    w_hbm = refs.pop(0)
    outs = [(refs.pop(0), refs.pop(0)) for _ in spans]
    if with_values:
        value_ref = refs.pop(0)
    w_refs = [refs.pop(0) for _ in spans]
    if with_values:
        gathered = refs.pop(0)
    sem = refs.pop(0)
    copies = []
    for i, (begin, columns) in enumerate(spans):
        copies.append(
            pltpu.make_async_copy(w_hbm.at[:, begin : begin + columns], w_refs[i], sem.at[i])
        )
        copies[i].start()
    if with_values:
        for p in range(tp_size):
            gathered[:, p * block : (p + 1) * block, :] = a_ref[order_ref[p]]
        heads, width = v_ref.shape[0], v_ref.shape[2]
        for h in range(heads):
            value_ref[:, h * width : (h + 1) * width] = jnp.dot(
                gathered[h], v_ref[h], preferred_element_type=f32
            ).astype(bf16)
    values = value_ref[...]
    half = values.shape[0] // 2
    for i in range(len(spans)):
        rows = jnp.concatenate([values[p * block : (p + 1) * block] for p in orders[i]], axis=0)
        copies[i].wait()
        result = jnp.dot(rows, w_refs[i][...], preferred_element_type=f32).astype(bf16)
        outs[i][0][...] = result[:half]
        outs[i][1][...] = result[half:]


def project(order, source, value_weight, w_out, block, spans, orders):
    with_values = value_weight is not None
    depth = w_out.shape[0]
    rows = tp_size * block
    vmem = pl.BlockSpec(memory_space=pltpu.VMEM)
    args, in_specs = [source], [vmem]
    if with_values:
        args, in_specs = [order, source, value_weight], [
            pl.BlockSpec(memory_space=pltpu.SMEM),
            vmem,
            vmem,
        ]
    out_shape = []
    for _, columns in spans:
        out_shape += [jax.ShapeDtypeStruct((rows // 2, columns), bf16)] * 2
    scratch = [pltpu.VMEM((depth, columns), bf16) for _, columns in spans]
    if with_values:
        out_shape.append(jax.ShapeDtypeStruct((rows, depth), bf16))
        scratch.append(pltpu.VMEM((source.shape[1], rows, source.shape[3]), bf16))
    total = sum(columns for _, columns in spans)
    return pl.pallas_call(
        functools.partial(out_kernel, block, spans, orders, with_values),
        in_specs=in_specs + [pl.BlockSpec(memory_space=pltpu.HBM)],
        out_specs=[vmem] * len(out_shape),
        out_shape=out_shape,
        scratch_shapes=scratch + [pltpu.SemaphoreType.DMA((len(spans),))],
        compiler_params=pltpu.CompilerParams(vmem_limit_bytes=vmem_limit),
        cost_estimate=pl.CostEstimate(
            flops=2 * rows * depth * total, bytes_accessed=2 * depth * total, transcendentals=0
        ),
        name="out_proj",
    )(*args, w_out)


def gated_kernel(spans, layouts, block, *refs):
    refs = list(refs)
    order_ref = refs.pop(0)
    x_refs = [[refs.pop(0) for _ in range(4)] for _ in spans]
    gain_ref, gate_ref, up_ref, out_ref, ordered = refs
    lanes = 128
    squares = gate = up = None
    for (begin, columns), pieces, layout in zip(spans, x_refs, layouts):
        wide = jnp.concatenate(
            [pieces[p][at : at + block, :] for p, at in layout], axis=0
        ).astype(f32)
        for j in range(0, columns, lanes):
            part = wide[:, j : j + lanes]
            squares = part * part if squares is None else squares + part * part
        gain = gain_ref[:, begin : begin + columns].astype(f32)
        scaled = (wide * gain).astype(bf16)

        def product(w_ref):
            return jnp.dot(scaled, w_ref[begin : begin + columns, :], preferred_element_type=f32)

        gate = product(gate_ref) if gate is None else gate + product(gate_ref)
        up = product(up_ref) if up is None else up + product(up_ref)
    width = gate_ref.shape[0]
    scale = lax.rsqrt(jnp.sum(squares, axis=-1, keepdims=True) * (1.0 / width) + 1e-06)
    gate, up = gate * scale, up * scale
    active = gate / (1.0 + jnp.exp(-gate)) * up
    own = out_ref.shape[1] // tp_size
    for p in range(tp_size):
        at = pl.multiple_of(order_ref[p] * own, own)
        for m in range(out_ref.shape[0]):
            start = p * block + m * own
            ordered[m, pl.ds(at, own), :] = active[start : start + own]
    out_ref[...] = ordered[...].astype(bf16)


def gated(order, pieces, spans, layouts, block, gain, gate, up, micro):
    columns, hidden = gate.shape
    rows = tp_size * block
    out_dims = (micro, rows // micro, hidden)
    vmem = pl.BlockSpec(memory_space=pltpu.VMEM)
    args = [piece for stream in pieces for piece in stream] + [gain, gate, up]
    return pl.pallas_call(
        functools.partial(gated_kernel, spans, layouts, block),
        in_specs=[pl.BlockSpec(memory_space=pltpu.SMEM)] + [vmem] * len(args),
        out_specs=vmem,
        out_shape=jax.ShapeDtypeStruct(out_dims, bf16),
        scratch_shapes=[pltpu.VMEM(out_dims, f32)],
        compiler_params=pltpu.CompilerParams(vmem_limit_bytes=vmem_limit),
        cost_estimate=pl.CostEstimate(
            flops=4 * rows * columns * hidden,
            bytes_accessed=4 * columns * hidden,
            transcendentals=0,
        ),
        name="gated_pair",
    )(order, *args)


def add(*parts):
    total = parts[0].astype(f32)
    for part in parts[1:]:
        total = total + part.astype(f32)
    return total


def shards(
    residual,
    queries,
    latent_cache,
    new_latent,
    lengths,
    positions,
    latent_value_weight,
    w_out,
    norm_gain,
    gate_weight,
    up_weight,
):
    latent = latent_value_weight.shape[1]
    micro, own_rows, width = residual.shape
    block = micro * own_rows
    heads = queries.shape[2]
    me = lax.axis_index("tp")
    places = [(c, p, q, z) for c in range(2) for p in range(2) for q in range(2) for z in range(2)]
    order = jnp.stack(
        [((me // 4) ^ p ^ (3 * q)) * 4 + (((me // 2) % 2) ^ z) * 2 + ((me % 2) ^ c) for c, p, q, z in places]
    ).astype(jnp.int32)
    tables = rotary_tables(positions.reshape(-1), queries.shape[3] - latent)
    attended = attention(
        queries.reshape((block,) + queries.shape[2:]),
        jnp.swapaxes(latent_cache, 2, 3).reshape(block, latent_cache.shape[3], -1),
        new_latent.reshape(block, -1),
        lengths,
        tables,
        latent,
    )
    arrived = lax.all_to_all(
        attended.reshape(tp_size, heads // tp_size, block, latent),
        "tp",
        split_axis=0,
        concat_axis=0,
        tiled=True,
    )

    streams = ("pqz", "qzp", "zpq")
    third = -(-width // (3 * 128)) * 128
    spans = [(i * third, min(third, width - i * third)) for i in range(3)]
    names = "cpqz"
    orders, layouts = [], []
    for dims in streams:
        rank = [names.index(d) for d in "c" + dims]
        orders.append(sorted(range(tp_size), key=lambda i: [places[i][k] for k in rank]))
        layouts.append(
            [
                (at[rank[0]] * 2 + at[rank[1]], (at[rank[2]] * 2 + at[rank[3]]) * block)
                for at in places
            ]
        )
    keep_0, send_0, values = project(
        order, arrived, latent_value_weight, w_out, block, spans[:1], orders[:1]
    )
    keep_1, send_1, keep_2, send_2 = project(
        order, values, None, w_out, block, spans[1:], orders[1:]
    )
    kept, sent = [keep_0, keep_1, keep_2], [send_0, send_1, send_2]
    flat_residual = residual.reshape(block, width)

    each = range(3)
    pair = [add(kept[i], send(sent[i], "c")).astype(bf16) for i in each]
    four = [
        add(pair[i][: 4 * block], send(pair[i][4 * block :], streams[i][0])).astype(bf16)
        for i in each
    ]
    two = []
    for i in each:
        total = add(four[i][: 2 * block], send(four[i][2 * block :], streams[i][1]))
        begin, columns = spans[i]
        own = total[:block] + flat_residual[:, begin : begin + columns].astype(f32)
        two.append(jnp.concatenate([own, total[block:]], axis=0).astype(bf16))
    other = [send(two[i], streams[i][2]) for i in each]
    both = [
        jnp.concatenate(
            [add(two[i][:block], other[i][block:]), add(two[i][block:], other[i][:block])], axis=0
        ).astype(bf16)
        for i in each
    ]
    near = [jnp.concatenate([both[i], send(both[i], streams[i][1])], axis=0) for i in each]
    far = [send(near[i], streams[i][0]) for i in each]
    pieces = [[near[i], far[i], send(near[i], "c"), send(far[i], "c")] for i in each]
    activation = gated(
        order,
        pieces,
        spans,
        layouts,
        block,
        norm_gain.reshape(1, width),
        gate_weight,
        up_weight,
        micro,
    )
    after_attention = jnp.concatenate([both[i][:block] for i in each], axis=1)
    return (after_attention.reshape(residual.shape), activation)


def solution(mesh):
    return jax.shard_map(
        shards,
        mesh=mesh,
        in_specs=(
            P(None, ("dp", "tp"), None),
            P(None, ("dp", "tp"), None, None),
            P(None, ("dp", "tp"), None, None),
            P(None, ("dp", "tp"), None),
            P(None, ("dp", "tp")),
            P(None, ("dp", "tp")),
            P("tp", None, None),
            P("tp", None),
            P(),
            P(None, "tp"),
            P(None, "tp"),
        ),
        out_specs=(P(None, ("dp", "tp"), None), P(None, "dp", "tp")),
        check_vma=False,
    )
```

time: 121 us -> 95.6 us (0.79)
  starting transfers between devices: 32.5 us -> 23.9 us
  local copies, waits for them, and re-layouts: 10.6 us -> 4.32 us
  Pallas kernels: 24.5 us -> 18.6 us
  waiting for transfers between devices: 49.1 us -> 44.1 us
    ppermute x23 -> x24, starting transfers between devices: 25.3 us -> 16.6 us  [send(): return lax.ppermute(value, 'tp', pairs)]
    pallas_call x4 -> x3, Pallas kernels: 19.1 us -> 12.1 us  [the longest x1 7.42 us: gated(): pl.pallas_call(functools.partial(gated_kernel, spans, layouts, block), in...]
    unnamed x28 -> x22, local copies, waits for them, and re-layouts: 9.7 us -> 4 us
    ppermute x23 -> x24, waiting for transfers between devices: 34.1 us -> 28.5 us  [send(): return lax.ppermute(value, 'tp', pairs)]
  transfers between devices with their start and end apart: 24 -> 25, of which waited for: 14 -> 16; matrix products, arithmetic and copies ran while one was open for 2% -> 2% of each run, Pallas kernels for 8% -> 0%
where the time goes in v3:
time: 95.6 us; the launch traced here: 95.3 us
  waiting for transfers between devices  44.1 us (46%)
  starting transfers between devices  23.9 us (25%)
  Pallas kernels  18.6 us (19%)
  local copies, waits for them, and re-layouts  4.32 us (5%)
  other arithmetic  3.3 us (3%)
  between operations  0.98 us (1%)
    ppermute x24, waiting for transfers between devices, send(): return lax.ppermute(value, 'tp', pairs)  28.5 us
    ppermute x24, starting transfers between devices, send(): return lax.ppermute(value, 'tp', pairs)  16.6 us
    all_to_all x1, waiting for transfers between devices, shards(): lax.all_to_all(attended.reshape(tp_size, heads // tp_size, block, latent)...  15.6 us
    pallas_call x1, Pallas kernels, gated(): pl.pallas_call(functools.partial(gated_kernel, spans, layouts, block), in...  7.42 us
    all_to_all x1, starting transfers between devices, shards(): lax.all_to_all(attended.reshape(tp_size, heads // tp_size, block, latent)...  7.31 us
    pallas_call x1, Pallas kernels, attention(): pl.pallas_call(functools.partial(attention_kernel, group, span, latent),...  6.53 us
    pallas_call x2, Pallas kernels, project(): pl.pallas_call(functools.partial(out_kernel, block, spans, orders, with_v...  4.65 us
    unnamed x22, local copies, waits for them, and re-layouts  4 us
  transfers between devices with their start and end apart: 25, of which 16 were waited for; matrix products, arithmetic and copies ran while one was open for 2% of the time, Pallas kernels for 0%

profile of v3, /device:TPU:1, one launch (start us, length us, event | category | flops | bytes accessed | tf_op | source)
XLA Modules:
  0.0 95.3 jit_solution(12695054369380987997)
XLA Ops:
  0.6 0.7 convert_element_type.133
  1.5 0.7 pad_maximum_fusion.9.t_ref
  2.2 6.5 %attention.1 = bf16[64,16,512]{2,1,0:T(8,128)(2,1)} custom-call(s32[2,8]{1,0:T(2,128)} %len_ref.1, bf16[16,64,576]{2,1,0:T(8,128)(2,1)} %bitcast.31, bf16[16,576,256]{2,1,0:T(8,128)(2,1)} %bitcast.29, bf16[16,576]{1,0:T(8,128)(2,1)} %bitcast.34, f32[16,128]{1,0:T(8,128)} %pad_maximum_fusion.9.t_ref), custom_call_target="tpu_custom_call" | custom-call | flops 603979776 | bytes 5898240 | tf_op jit(solution)/shard_map/attention/pallas_call | solution.py:109
  8.8 7.3 %all-to-all-start = ((bf16[16,4,16,512]{3,2,1,0:T(8,128)(2,1)}), bf16[16,4,16,512]{3,2,1,0:T(8,128)(2,1)S(1)}, u32[]{:S(2)}, u32[]{:S(2)}) async-start(bf16[16,4,16,512]{3,2,1,0:T(8,128)(2,1)} %bitcast.30), calls=%async_computation | async-start | bytes 2097152 | tf_op jit(solution)/shard_map/all_to_all | solution.py:304
  16.2 15.6 %all-to-all-done.refs_1_ = bf16[16,4,16,512]{3,2,1,0:T(8,128)(2,1)S(1)} async-done(((bf16[16,4,16,512]{3,2,1,0:T(8,128)(2,1)}), bf16[16,4,16,512]{3,2,1,0:T(8,128)(2,1)S(1)}, u32[]{:S(2)}, u32[]{:S(2)}) %all-to-all-start) | async-done | bytes 1048608 | tf_op jit(solution)/shard_map/all_to_all | solution.py:304
  31.8 3.1 %copy-done = bf16[512,7168]{1,0:T(8,128)(2,1)S(1)} copy-done((bf16[512,7168]{1,0:T(8,128)(2,1)S(1)}, bf16[512,7168]{1,0:T(8,128)(2,1)}, u32[]{:S(2)}) %copy-start) | copy-done | bytes 7340056
  34.9 2.2 %out_proj.2 = (bf16[128,2432]{1,0:T(8,128)(2,1)S(1)}, bf16[128,2432]{1,0:T(8,128)(2,1)S(1)}, bf16[256,512]{1,0:T(8,128)(2,1)S(1)}) custom-call(s32[16]{0:T(128)S(1)} %stack.67.refs_0_, bf16[16,4,16,512]{3,2,1,0:T(8,128)(2,1)S(1)} %all-to-all-done.refs_1_, bf16[4,512,128]{2,1,0:T(8,128)(2,1)S(1)} %copy-done.2, bf16[512,7168]{1,0:T(8,128)(2,1)S(1)} %copy-done), custom_call_target="tpu_custom_call" | custom-call | flops 637534208 | bytes 2490368 | tf_op jit(solution)/shard_map/out_proj/pallas_call | solution.py:195
  37.1 0.9 copy-done.1
  38.0 2.4 %out_proj.3 = (bf16[128,2432]{1,0:T(8,128)(2,1)S(1)}, bf16[128,2432]{1,0:T(8,128)(2,1)S(1)}, bf16[128,2304]{1,0:T(8,128)(2,1)S(1)}, bf16[128,2304]{1,0:T(8,128)(2,1)S(1)}) custom-call(bf16[256,512]{1,0:T(8,128)(2,1)S(1)} %get-tuple-element.11.refs_0_, bf16[512,7168]{1,0:T(8,128)(2,1)S(1)} %copy-done.1), custom_call_target="tpu_custom_call" | custom-call | flops 1241513984 | bytes 4849664 | tf_op jit(solution)/shard_map/out_proj/pallas_call | solution.py:195
  40.4 0.9 collective-permute-start.8
  41.9 1.1 %collective-permute-done.8 = bf16[128,2304]{1,0:T(8,128)(2,1)S(1)} collective-permute-done((bf16[128,2304]{1,0:T(8,128)(2,1)S(1)}, bf16[128,2304]{1,0:T(8,128)(2,1)S(1)}, u32[]{:S(2)}, u32[]{:S(2)}) %collective-permute-start.8) | collective-permute-done | bytes 589856 | tf_op jit(solution)/shard_map/ppermute | solution.py:32
  44.2 0.6 collective-permute-done.4
  45.0 1.1 %collective-permute-start.5 = (bf16[64,2432]{1,0:T(8,128)(2,1)S(1)}, bf16[64,2432]{1,0:T(8,128)(2,1)S(1)}, u32[]{:S(2)}, u32[]{:S(2)}) collective-permute-start(bf16[64,2432]{1,0:T(8,128)(2,1)S(1)} %slice.147), channel_id=1, source_target_pairs={{0,12},{1,13},{2,14},{3,15},{4,8},{5,9},{6,10},{7,11},{8,4},{9,5},... | collective-permute-start | bytes 933896 | tf_op jit(solution)/shard_map/ppermute | solution.py:32
  46.1 5.3 %collective-permute-done.9 = bf16[64,2304]{1,0:T(8,128)(2,1)S(1)} collective-permute-done((bf16[64,2304]{1,0:T(8,128)(2,1)S(1)}, bf16[64,2304]{1,0:T(8,128)(2,1)S(1)}, u32[]{:S(2)}, u32[]{:S(2)}) %collective-permute-start.9) | collective-permute-done | bytes 294944 | tf_op jit(solution)/shard_map/ppermute | solution.py:32
  51.6 1.1 %collective-permute-done.1 = bf16[64,2432]{1,0:T(8,128)(2,1)S(1)} collective-permute-done((bf16[64,2432]{1,0:T(8,128)(2,1)S(1)}, bf16[64,2432]{1,0:T(8,128)(2,1)S(1)}, u32[]{:S(2)}, u32[]{:S(2)}) %collective-permute-start.1) | collective-permute-done | bytes 311328 | tf_op jit(solution)/shard_map/ppermute | solution.py:32
  52.8 0.7 collective-permute-start.2
  53.6 1.2 %collective-permute-done.5 = bf16[64,2432]{1,0:T(8,128)(2,1)S(1)} collective-permute-done((bf16[64,2432]{1,0:T(8,128)(2,1)S(1)}, bf16[64,2432]{1,0:T(8,128)(2,1)S(1)}, u32[]{:S(2)}, u32[]{:S(2)}) %collective-permute-start.5) | collective-permute-done | bytes 311328 | tf_op jit(solution)/shard_map/ppermute | solution.py:32
  55.1 0.6 collective-permute-done.10
  55.7 1.0 %collective-permute-start.11 = (bf16[32,2304]{1,0:T(8,128)(2,1)S(1)}, bf16[32,2304]{1,0:T(8,128)(2,1)S(1)}, u32[]{:S(2)}, u32[]{:S(2)}) collective-permute-start(bf16[32,2304]{1,0:T(8,128)(2,1)S(1)} %pad_maximum_fusion.7), channel_id=1, source_target_pairs={{0,12},{1,13},{2,14},{3,15},{4,8},{5,9},{6,10},{7,11},{8,4},{9,5},... | collective-permute-start | bytes 442376 | tf_op jit(solution)/shard_map/ppermute | solution.py:32
  56.8 1.4 %collective-permute-done.2 = bf16[32,2432]{1,0:T(8,128)(2,1)S(1)} collective-permute-done((bf16[32,2432]{1,0:T(8,128)(2,1)S(1)}, bf16[32,2432]{1,0:T(8,128)(2,1)S(1)}, u32[]{:S(2)}, u32[]{:S(2)}) %collective-permute-start.2) | collective-permute-done | bytes 155680 | tf_op jit(solution)/shard_map/ppermute | solution.py:32
  58.3 1.1 %collective-permute-done.6 = bf16[32,2432]{1,0:T(8,128)(2,1)S(1)} collective-permute-done((bf16[32,2432]{1,0:T(8,128)(2,1)S(1)}, bf16[32,2432]{1,0:T(8,128)(2,1)S(1)}, u32[]{:S(2)}, u32[]{:S(2)}) %collective-permute-start.6) | collective-permute-done | bytes 155680 | tf_op jit(solution)/shard_map/ppermute | solution.py:32
  59.8 1.7 %collective-permute-done.11 = bf16[32,2304]{1,0:T(8,128)(2,1)S(1)} collective-permute-done((bf16[32,2304]{1,0:T(8,128)(2,1)S(1)}, bf16[32,2304]{1,0:T(8,128)(2,1)S(1)}, u32[]{:S(2)}, u32[]{:S(2)}) %collective-permute-start.11) | collective-permute-done | bytes 147488 | tf_op jit(solution)/shard_map/ppermute | solution.py:32
  61.6 2.5 %collective-permute-done.3 = bf16[32,2432]{1,0:T(8,128)(2,1)S(1)} collective-permute-done((bf16[32,2432]{1,0:T(8,128)(2,1)S(1)}, bf16[32,2432]{1,0:T(8,128)(2,1)S(1)}, u32[]{:S(2)}, u32[]{:S(2)}) %collective-permute-start.3) | collective-permute-done | bytes 155680 | tf_op jit(solution)/shard_map/ppermute | solution.py:32
  64.2 0.8 collective-permute-start.12
  65.5 4.0 %collective-permute-done.12 = bf16[32,2432]{1,0:T(8,128)(2,1)S(1)} collective-permute-done((bf16[32,2432]{1,0:T(8,128)(2,1)S(1)}, bf16[32,2432]{1,0:T(8,128)(2,1)S(1)}, u32[]{:S(2)}, u32[]{:S(2)}) %collective-permute-start.12) | collective-permute-done | bytes 155680 | tf_op jit(solution)/shard_map/ppermute | solution.py:32
  69.9 1.4 %collective-permute-start.17 = (bf16[64,2432]{1,0:T(8,128)(2,1)S(1)}, bf16[64,2432]{1,0:T(8,128)(2,1)S(1)}, u32[]{:S(2)}, u32[]{:S(2)}) collective-permute-start(bf16[64,2432]{1,0:T(8,128)(2,1)S(1)} %pad_maximum_fusion.1.refs_5_), channel_id=1, source_target_pairs={{0,12},{1,13},{2,14},{3,15},{4,8},{5,9},{6,10},{7,11},{8,4},{9,5},... | collective-permute-start | bytes 933896 | tf_op jit(solution)/shard_map/ppermute | solution.py:32
  71.3 5.0 %collective-permute-start.22 = (bf16[64,2304]{1,0:T(8,128)(2,1)S(1)}, bf16[64,2304]{1,0:T(8,128)(2,1)S(1)}, u32[]{:S(2)}, u32[]{:S(2)}) collective-permute-start(bf16[64,2304]{1,0:T(8,128)(2,1)S(1)} %pad_maximum_fusion.2.refs_9_), channel_id=1, source_target_pairs={{0,1},{1,0},{2,3},{3,2},{4,5},{5,4},{6,7},{7,6},{8,9},{9,8},{10,11... | collective-permute-start | bytes 884744 | tf_op jit(solution)/shard_map/ppermute | solution.py:32
  76.2 1.4 %collective-permute-start.21 = (bf16[64,2304]{1,0:T(8,128)(2,1)S(1)}, bf16[64,2304]{1,0:T(8,128)(2,1)S(1)}, u32[]{:S(2)}, u32[]{:S(2)}) collective-permute-start(bf16[64,2304]{1,0:T(8,128)(2,1)S(1)} %pad_maximum_fusion.2.refs_9_), channel_id=1, source_target_pairs={{0,2},{1,3},{2,0},{3,1},{4,6},{5,7},{6,4},{7,5},{8,10},{9,11},{10,... | collective-permute-start | bytes 884744 | tf_op jit(solution)/shard_map/ppermute | solution.py:32
  78.2 6.6 %collective-permute-done.21.refs_10_ = bf16[64,2304]{1,0:T(8,128)(2,1)S(1)} collective-permute-done((bf16[64,2304]{1,0:T(8,128)(2,1)S(1)}, bf16[64,2304]{1,0:T(8,128)(2,1)S(1)}, u32[]{:S(2)}, u32[]{:S(2)}) %collective-permute-start.21) | collective-permute-done | bytes 294944 | tf_op jit(solution)/shard_map/ppermute | solution.py:32
  84.8 0.9 collective-permute-start.23
  86.2 0.7 maximum_bitcast_fusion
  87.8 7.4 %gated_pair.1 = bf16[2,128,640]{2,1,0:T(8,128)(2,1)} custom-call(s32[16]{0:T(128)S(1)} %stack.67.refs_0_, bf16[64,2432]{1,0:T(8,128)(2,1)S(1)} %pad_maximum_fusion.refs_1_, bf16[64,2432]{1,0:T(8,128)(2,1)S(1)} %collective-permute-done.13.refs_2_, bf16[64,2432]{1,0:T(8,128)(2,1)S(1)} %collective-permute-done.14.refs_3_, ...), custom_call_target="tpu_custom_call" | custom-call | flops 4697620480 | bytes 18350080 | tf_op jit(solution)/shard_map/gated_pair/pallas_call | solution.py:250
  (86 shorter events, 6.2 us)
Async XLA Ops:
  8.8 23.0 %copy-start.2 = (bf16[4,512,128]{2,1,0:T(8,128)(2,1)S(1)}, bf16[4,512,128]{2,1,0:T(8,128)(2,1)}, u32[]{:S(2)}) copy-start(bf16[4,512,128]{2,1,0:T(8,128)(2,1)} %refs_2_.1) | copy-start | bytes 1572868
  8.8 23.0 %all-to-all-start = ((bf16[16,4,16,512]{3,2,1,0:T(8,128)(2,1)}), bf16[16,4,16,512]{3,2,1,0:T(8,128)(2,1)S(1)}, u32[]{:S(2)}, u32[]{:S(2)}) async-start(bf16[16,4,16,512]{3,2,1,0:T(8,128)(2,1)} %bitcast.30), calls=%async_computation | async-start | bytes 2097152 | tf_op jit(solution)/shard_map/all_to_all | solution.py:304
  34.9 52.9 %slice-start.3 = ((s8[9175040]{0:T(1024)(128)(4,1)}), s8[4194304]{0:T(1024)(128)(4,1)S(1)}, s32[]{:S(2)}) async-start(s8[9175040]{0:T(1024)(128)(4,1)} %bitcast.27), calls=%async_computation.4 | async-start | bytes 8388608
  38.0 49.8 %slice-start = ((s8[9175040]{0:T(1024)(128)(4,1)}), s8[4194304]{0:T(1024)(128)(4,1)S(1)}, s32[]{:S(2)}) async-start(s8[9175040]{0:T(1024)(128)(4,1)} %bitcast.25), calls=%async_computation.1 | async-start | bytes 8388608
  38.0 49.8 %slice-start.4 = ((s8[9175040]{0:T(1024)(128)(4,1)}), s8[4194304]{0:T(1024)(128)(4,1)S(1)}, s32[]{:S(2)}) async-start(s8[9175040]{0:T(1024)(128)(4,1)} %bitcast.27), calls=%async_computation.5 | async-start | bytes 8388608
  40.4 2.6 %collective-permute-start.8 = (bf16[128,2304]{1,0:T(8,128)(2,1)S(1)}, bf16[128,2304]{1,0:T(8,128)(2,1)S(1)}, u32[]{:S(2)}, u32[]{:S(2)}) collective-permute-start(bf16[128,2304]{1,0:T(8,128)(2,1)S(1)} %get-tuple-element.15), channel_id=1, source_target_pairs={{0,1},{1,0},{2,3},{3,2},{4,5},{5,4},{6,7},{7,6},{8,9},{9,8},{10,11... | collective-permute-start | bytes 1769480 | tf_op jit(solution)/shard_map/ppermute | solution.py:32
  41.4 2.5 %collective-permute-start = (bf16[128,2432]{1,0:T(8,128)(2,1)S(1)}, bf16[128,2432]{1,0:T(8,128)(2,1)S(1)}, u32[]{:S(2)}, u32[]{:S(2)}) collective-permute-start(bf16[128,2432]{1,0:T(8,128)(2,1)S(1)} %get-tuple-element.10), channel_id=1, source_target_pairs={{0,1},{1,0},{2,3},{3,2},{4,5},{5,4},{6,7},{7,6},{8,9},{9,8},{10,11... | collective-permute-start | bytes 1867784 | tf_op jit(solution)/shard_map/ppermute | solution.py:32
  41.5 3.3 %collective-permute-start.4 = (bf16[128,2432]{1,0:T(8,128)(2,1)S(1)}, bf16[128,2432]{1,0:T(8,128)(2,1)S(1)}, u32[]{:S(2)}, u32[]{:S(2)}) collective-permute-start(bf16[128,2432]{1,0:T(8,128)(2,1)S(1)} %get-tuple-element.13), channel_id=1, source_target_pairs={{0,1},{1,0},{2,3},{3,2},{4,5},{5,4},{6,7},{7,6},{8,9},{9,8},{10,11... | collective-permute-start | bytes 1867784 | tf_op jit(solution)/shard_map/ppermute | solution.py:32
  43.0 44.8 %slice-start.1 = ((s8[9175040]{0:T(1024)(128)(4,1)}), s8[4194304]{0:T(1024)(128)(4,1)S(1)}, s32[]{:S(2)}) async-start(s8[9175040]{0:T(1024)(128)(4,1)} %bitcast.25), calls=%async_computation.2 | async-start | bytes 8388608
  43.2 8.3 %collective-permute-start.9 = (bf16[64,2304]{1,0:T(8,128)(2,1)S(1)}, bf16[64,2304]{1,0:T(8,128)(2,1)S(1)}, u32[]{:S(2)}, u32[]{:S(2)}) collective-permute-start(bf16[64,2304]{1,0:T(8,128)(2,1)S(1)} %slice.155), channel_id=1, source_target_pairs={{0,2},{1,3},{2,0},{3,1},{4,6},{5,7},{6,4},{7,5},{8,10},{9,11},{10,... | collective-permute-start | bytes 884744 | tf_op jit(solution)/shard_map/ppermute | solution.py:32
  44.1 8.7 %collective-permute-start.1 = (bf16[64,2432]{1,0:T(8,128)(2,1)S(1)}, bf16[64,2432]{1,0:T(8,128)(2,1)S(1)}, u32[]{:S(2)}, u32[]{:S(2)}) collective-permute-start(bf16[64,2432]{1,0:T(8,128)(2,1)S(1)} %slice.139), channel_id=1, source_target_pairs={{0,4},{1,5},{2,6},{3,7},{4,0},{5,1},{6,2},{7,3},{8,12},{9,13},{10,... | collective-permute-start | bytes 933896 | tf_op jit(solution)/shard_map/ppermute | solution.py:32
  44.9 42.9 %slice-start.5 = ((s8[9175040]{0:T(1024)(128)(4,1)}), s8[786432]{0:T(1024)(128)(4,1)S(1)}, s32[]{:S(2)}) async-start(s8[9175040]{0:T(1024)(128)(4,1)} %bitcast.27), calls=%async_computation.6 | async-start | bytes 1572864
  45.0 9.9 %collective-permute-start.5 = (bf16[64,2432]{1,0:T(8,128)(2,1)S(1)}, bf16[64,2432]{1,0:T(8,128)(2,1)S(1)}, u32[]{:S(2)}, u32[]{:S(2)}) collective-permute-start(bf16[64,2432]{1,0:T(8,128)(2,1)S(1)} %slice.147), channel_id=1, source_target_pairs={{0,12},{1,13},{2,14},{3,15},{4,8},{5,9},{6,10},{7,11},{8,4},{9,5},... | collective-permute-start | bytes 933896 | tf_op jit(solution)/shard_map/ppermute | solution.py:32
  51.6 4.1 %collective-permute-start.10 = (bf16[32,2304]{1,0:T(8,128)(2,1)S(1)}, bf16[32,2304]{1,0:T(8,128)(2,1)S(1)}, u32[]{:S(2)}, u32[]{:S(2)}) collective-permute-start(bf16[32,2304]{1,0:T(8,128)(2,1)S(1)} %slice.157), channel_id=1, source_target_pairs={{0,4},{1,5},{2,6},{3,7},{4,0},{5,1},{6,2},{7,3},{8,12},{9,13},{10,... | collective-permute-start | bytes 442376 | tf_op jit(solution)/shard_map/ppermute | solution.py:32
  52.8 35.0 %slice-start.2 = ((s8[9175040]{0:T(1024)(128)(4,1)}), s8[786432]{0:T(1024)(128)(4,1)S(1)}, s32[]{:S(2)}) async-start(s8[9175040]{0:T(1024)(128)(4,1)} %bitcast.25), calls=%async_computation.3 | async-start | bytes 1572864
  52.8 5.4 %collective-permute-start.2 = (bf16[32,2432]{1,0:T(8,128)(2,1)S(1)}, bf16[32,2432]{1,0:T(8,128)(2,1)S(1)}, u32[]{:S(2)}, u32[]{:S(2)}) collective-permute-start(bf16[32,2432]{1,0:T(8,128)(2,1)S(1)} %slice.141), channel_id=1, source_target_pairs={{0,12},{1,13},{2,14},{3,15},{4,8},{5,9},{6,10},{7,11},{8,4},{9,5},... | collective-permute-start | bytes 466952 | tf_op jit(solution)/shard_map/ppermute | solution.py:32
  54.9 4.5 %collective-permute-start.6 = (bf16[32,2432]{1,0:T(8,128)(2,1)S(1)}, bf16[32,2432]{1,0:T(8,128)(2,1)S(1)}, u32[]{:S(2)}, u32[]{:S(2)}) collective-permute-start(bf16[32,2432]{1,0:T(8,128)(2,1)S(1)} %slice.149), channel_id=1, source_target_pairs={{0,2},{1,3},{2,0},{3,1},{4,6},{5,7},{6,4},{7,5},{8,10},{9,11},{10,... | collective-permute-start | bytes 466952 | tf_op jit(solution)/shard_map/ppermute | solution.py:32
  55.7 5.7 %collective-permute-start.11 = (bf16[32,2304]{1,0:T(8,128)(2,1)S(1)}, bf16[32,2304]{1,0:T(8,128)(2,1)S(1)}, u32[]{:S(2)}, u32[]{:S(2)}) collective-permute-start(bf16[32,2304]{1,0:T(8,128)(2,1)S(1)} %pad_maximum_fusion.7), channel_id=1, source_target_pairs={{0,12},{1,13},{2,14},{3,15},{4,8},{5,9},{6,10},{7,11},{8,4},{9,5},... | collective-permute-start | bytes 442376 | tf_op jit(solution)/shard_map/ppermute | solution.py:32
  59.5 5.5 %collective-permute-start.7 = (bf16[32,2432]{1,0:T(8,128)(2,1)S(1)}, bf16[32,2432]{1,0:T(8,128)(2,1)S(1)}, u32[]{:S(2)}, u32[]{:S(2)}) collective-permute-start(bf16[32,2432]{1,0:T(8,128)(2,1)S(1)} %pad_maximum_fusion.4), channel_id=1, source_target_pairs={{0,4},{1,5},{2,6},{3,7},{4,0},{5,1},{6,2},{7,3},{8,12},{9,13},{10,... | collective-permute-start | bytes 466952 | tf_op jit(solution)/shard_map/ppermute | solution.py:32
  59.6 4.5 %collective-permute-start.3 = (bf16[32,2432]{1,0:T(8,128)(2,1)S(1)}, bf16[32,2432]{1,0:T(8,128)(2,1)S(1)}, u32[]{:S(2)}, u32[]{:S(2)}) collective-permute-start(bf16[32,2432]{1,0:T(8,128)(2,1)S(1)} %pad_maximum_fusion.3), channel_id=1, source_target_pairs={{0,2},{1,3},{2,0},{3,1},{4,6},{5,7},{6,4},{7,5},{8,10},{9,11},{10,... | collective-permute-start | bytes 466952 | tf_op jit(solution)/shard_map/ppermute | solution.py:32
  61.5 9.7 %collective-permute-start.20 = (bf16[32,2304]{1,0:T(8,128)(2,1)S(1)}, bf16[32,2304]{1,0:T(8,128)(2,1)S(1)}, u32[]{:S(2)}, u32[]{:S(2)}) collective-permute-start(bf16[32,2304]{1,0:T(8,128)(2,1)S(1)} %pad_maximum_fusion.8), channel_id=1, source_target_pairs={{0,4},{1,5},{2,6},{3,7},{4,0},{5,1},{6,2},{7,3},{8,12},{9,13},{10,... | collective-permute-start | bytes 442376 | tf_op jit(solution)/shard_map/ppermute | solution.py:32
  64.2 5.4 %collective-permute-start.12 = (bf16[32,2432]{1,0:T(8,128)(2,1)S(1)}, bf16[32,2432]{1,0:T(8,128)(2,1)S(1)}, u32[]{:S(2)}, u32[]{:S(2)}) collective-permute-start(bf16[32,2432]{1,0:T(8,128)(2,1)S(1)} %pad_maximum_fusion.5), channel_id=1, source_target_pairs={{0,12},{1,13},{2,14},{3,15},{4,8},{5,9},{6,10},{7,11},{8,4},{9,5},... | collective-permute-start | bytes 466952 | tf_op jit(solution)/shard_map/ppermute | solution.py:32
  65.0 4.8 %collective-permute-start.16 = (bf16[32,2432]{1,0:T(8,128)(2,1)S(1)}, bf16[32,2432]{1,0:T(8,128)(2,1)S(1)}, u32[]{:S(2)}, u32[]{:S(2)}) collective-permute-start(bf16[32,2432]{1,0:T(8,128)(2,1)S(1)} %pad_maximum_fusion.6), channel_id=1, source_target_pairs={{0,2},{1,3},{2,0},{3,1},{4,6},{5,7},{6,4},{7,5},{8,10},{9,11},{10,... | collective-permute-start | bytes 466952 | tf_op jit(solution)/shard_map/ppermute | solution.py:32
  69.6 16.1 %collective-permute-start.13 = (bf16[64,2432]{1,0:T(8,128)(2,1)S(1)}, bf16[64,2432]{1,0:T(8,128)(2,1)S(1)}, u32[]{:S(2)}, u32[]{:S(2)}) collective-permute-start(bf16[64,2432]{1,0:T(8,128)(2,1)S(1)} %pad_maximum_fusion.refs_1_), channel_id=1, source_target_pairs={{0,4},{1,5},{2,6},{3,7},{4,0},{5,1},{6,2},{7,3},{8,12},{9,13},{10,... | collective-permute-start | bytes 933896 | tf_op jit(solution)/shard_map/ppermute | solution.py:32
  69.9 15.8 %collective-permute-start.17 = (bf16[64,2432]{1,0:T(8,128)(2,1)S(1)}, bf16[64,2432]{1,0:T(8,128)(2,1)S(1)}, u32[]{:S(2)}, u32[]{:S(2)}) collective-permute-start(bf16[64,2432]{1,0:T(8,128)(2,1)S(1)} %pad_maximum_fusion.1.refs_5_), channel_id=1, source_target_pairs={{0,12},{1,13},{2,14},{3,15},{4,8},{5,9},{6,10},{7,11},{8,4},{9,5},... | collective-permute-start | bytes 933896 | tf_op jit(solution)/shard_map/ppermute | solution.py:32
  71.3 6.8 %collective-permute-start.22 = (bf16[64,2304]{1,0:T(8,128)(2,1)S(1)}, bf16[64,2304]{1,0:T(8,128)(2,1)S(1)}, u32[]{:S(2)}, u32[]{:S(2)}) collective-permute-start(bf16[64,2304]{1,0:T(8,128)(2,1)S(1)} %pad_maximum_fusion.2.refs_9_), channel_id=1, source_target_pairs={{0,1},{1,0},{2,3},{3,2},{4,5},{5,4},{6,7},{7,6},{8,9},{9,8},{10,11... | collective-permute-start | bytes 884744 | tf_op jit(solution)/shard_map/ppermute | solution.py:32
  76.2 8.6 %collective-permute-start.21 = (bf16[64,2304]{1,0:T(8,128)(2,1)S(1)}, bf16[64,2304]{1,0:T(8,128)(2,1)S(1)}, u32[]{:S(2)}, u32[]{:S(2)}) collective-permute-start(bf16[64,2304]{1,0:T(8,128)(2,1)S(1)} %pad_maximum_fusion.2.refs_9_), channel_id=1, source_target_pairs={{0,2},{1,3},{2,0},{3,1},{4,6},{5,7},{6,4},{7,5},{8,10},{9,11},{10,... | collective-permute-start | bytes 884744 | tf_op jit(solution)/shard_map/ppermute | solution.py:32
  77.7 9.3 %collective-permute-start.14 = (bf16[64,2432]{1,0:T(8,128)(2,1)S(1)}, bf16[64,2432]{1,0:T(8,128)(2,1)S(1)}, u32[]{:S(2)}, u32[]{:S(2)}) collective-permute-start(bf16[64,2432]{1,0:T(8,128)(2,1)S(1)} %pad_maximum_fusion.refs_1_), channel_id=1, source_target_pairs={{0,1},{1,0},{2,3},{3,2},{4,5},{5,4},{6,7},{7,6},{8,9},{9,8},{10,11... | collective-permute-start | bytes 933896 | tf_op jit(solution)/shard_map/ppermute | solution.py:32
  78.1 8.8 %collective-permute-start.18 = (bf16[64,2432]{1,0:T(8,128)(2,1)S(1)}, bf16[64,2432]{1,0:T(8,128)(2,1)S(1)}, u32[]{:S(2)}, u32[]{:S(2)}) collective-permute-start(bf16[64,2432]{1,0:T(8,128)(2,1)S(1)} %pad_maximum_fusion.1.refs_5_), channel_id=1, source_target_pairs={{0,1},{1,0},{2,3},{3,2},{4,5},{5,4},{6,7},{7,6},{8,9},{9,8},{10,11... | collective-permute-start | bytes 933896 | tf_op jit(solution)/shard_map/ppermute | solution.py:32
  84.8 2.1 %collective-permute-start.23 = (bf16[64,2304]{1,0:T(8,128)(2,1)S(1)}, bf16[64,2304]{1,0:T(8,128)(2,1)S(1)}, u32[]{:S(2)}, u32[]{:S(2)}) collective-permute-start(bf16[64,2304]{1,0:T(8,128)(2,1)S(1)} %collective-permute-done.21.refs_10_), channel_id=1, source_target_pairs={{0,1},{1,0},{2,3},{3,2},{4,5},{5,4},{6,7},{7,6},{8,9},{9,8},{10,11... | collective-permute-start | bytes 884744 | tf_op jit(solution)/shard_map/ppermute | solution.py:32
  85.7 1.7 %collective-permute-start.15 = (bf16[64,2432]{1,0:T(8,128)(2,1)S(1)}, bf16[64,2432]{1,0:T(8,128)(2,1)S(1)}, u32[]{:S(2)}, u32[]{:S(2)}) collective-permute-start(bf16[64,2432]{1,0:T(8,128)(2,1)S(1)} %collective-permute-done.13.refs_2_), channel_id=1, source_target_pairs={{0,1},{1,0},{2,3},{3,2},{4,5},{5,4},{6,7},{7,6},{8,9},{9,8},{10,11... | collective-permute-start | bytes 933896 | tf_op jit(solution)/shard_map/ppermute | solution.py:32
  85.7 2.1 %collective-permute-start.19 = (bf16[64,2432]{1,0:T(8,128)(2,1)S(1)}, bf16[64,2432]{1,0:T(8,128)(2,1)S(1)}, u32[]{:S(2)}, u32[]{:S(2)}) collective-permute-start(bf16[64,2432]{1,0:T(8,128)(2,1)S(1)} %collective-permute-done.17.refs_6_), channel_id=1, source_target_pairs={{0,1},{1,0},{2,3},{3,2},{4,5},{5,4},{6,7},{7,6},{8,9},{9,8},{10,11... | collective-permute-start | bytes 933896 | tf_op jit(solution)/shard_map/ppermute | solution.py:32
  (4 other events, 22.5 us)

commit v4 on v3

v4 whole, which is shorter than its diff:
```python
import functools

import jax
import jax.numpy as jnp
import numpy as np
from jax import lax
from jax.experimental import pallas as pl
from jax.experimental.pallas import tpu as pltpu
from jax.sharding import PartitionSpec as P

score_scale = 192.0 ** (-0.5)
neg_large = -1e30
f32 = jnp.float32
bf16 = jnp.bfloat16
vmem_limit = 20 * 1024 * 1024
large_vmem = 56 * 1024 * 1024
x_size, z_size, core_size = 4, 2, 2
tp_size = x_size * z_size * core_size
stream_sets = 1


flips = {"p": (1, 0, 0), "q": (3, 0, 0), "z": (0, 1, 0), "c": (0, 0, 1)}


def send(value, *dims):
    pairs = []
    for i in range(tp_size):
        x, z, c = i // 4, (i // 2) % 2, i % 2
        for dim in dims:
            fx, fz, fc = flips[dim]
            x, z, c = x ^ fx, z ^ fz, c ^ fc
        pairs.append((i, x * 4 + z * 2 + c))
    return lax.ppermute(value, "tp", pairs)


def rotary_frequencies(rope):
    exponent = np.arange(rope // 2) * (2.0 / rope)
    return jnp.asarray(np.tile(10000.0**-exponent, 2)[None, :], f32)


def attention_kernel(
    group, span, latent, len_ref, pos_ref, q_hbm, c_hbm, n_ref, f_ref, out_ref, q_ref, c_ref, held, q_sem, c_sem
):
    count, heads, width = q_ref.shape
    rope = width - latent
    half = rope // 2
    per = len_ref.shape[1]

    copies = []
    for i in range(count // span):
        at = pl.ds(i * span, span)
        copies.append(
            (
                pltpu.make_async_copy(q_hbm.at[at], q_ref.at[at], q_sem.at[i]),
                pltpu.make_async_copy(c_hbm.at[at], c_ref.at[at], c_sem.at[i]),
            )
        )
    for pair in copies:
        for copy in pair:
            copy.start()

    row_ids = lax.broadcasted_iota(jnp.int32, (count, rope), 0)
    positions = jnp.zeros((count, rope), f32)
    for r in range(count):
        positions = jnp.where(row_ids == r, pos_ref[r // per, r % per].astype(f32), positions)
    angles = positions * f_ref[...]
    cosines, sines = jnp.cos(angles), jnp.sin(angles)
    leading = lax.broadcasted_iota(jnp.int32, (count, rope), 1) < half
    sines = jnp.where(leading, -sines, sines)

    def turn(values, cosine, sine):
        swapped = jnp.concatenate([values[:, half:], values[:, :half]], axis=-1)
        return (values * cosine + swapped * sine).astype(bf16)

    for begin in range(0, count, group):
        scored = []
        for r in range(begin, begin + group):
            if r % span == 0:
                for copy in copies[r // span]:
                    copy.wait()
            cosine, sine = cosines[r : r + 1], sines[r : r + 1]
            q_lat = q_ref[r, :, :latent]
            q_rope = turn(q_ref[r, :, latent:].astype(f32), cosine, sine)
            n_lat = n_ref[r : r + 1, :latent].astype(f32)
            n_rope = turn(n_ref[r : r + 1, latent:].astype(f32), cosine, sine).astype(f32)
            scores = jnp.dot(q_lat, c_ref[r, :latent, :], preferred_element_type=f32)
            scores += jnp.dot(q_rope, c_ref[r, latent:, :], preferred_element_type=f32)
            own = jnp.sum(q_lat.astype(f32) * n_lat, axis=-1, keepdims=True)
            own += jnp.sum(q_rope.astype(f32) * n_rope, axis=-1, keepdims=True)
            scored.append((scores, own * score_scale, n_lat))
        weighted = []
        for r in range(begin, begin + group):
            scores, own, n_lat = scored[r - begin]
            visible = lax.broadcasted_iota(jnp.int32, scores.shape, 1) < len_ref[r // per, r % per]
            scores = jnp.where(visible, scores * score_scale, neg_large)
            top = jnp.maximum(jnp.max(scores, axis=-1, keepdims=True), own)
            weights = jnp.where(visible, jnp.exp(scores - top), 0.0)
            own_weight = jnp.exp(own - top)
            total = jnp.sum(weights, axis=-1, keepdims=True) + own_weight
            weighted.append((weights.astype(bf16), own_weight, total, n_lat))
        for r in range(begin, begin + group):
            weights, own_weight, total, n_lat = weighted[r - begin]
            context = lax.dot_general(
                weights, c_ref[r, :latent, :], (((1,), (1,)), ((), ())), preferred_element_type=f32
            )
            context += own_weight.astype(bf16).astype(f32) * n_lat
            held[:, r, :] = context * (1.0 / total)
    out_ref[...] = held[...].astype(bf16)


def attention(queries, cache, new_latent, lengths, positions, latent, group=8, span=4):
    count, heads, width = queries.shape
    slots = cache.shape[2]
    vmem = pl.BlockSpec(memory_space=pltpu.VMEM)
    return pl.pallas_call(
        functools.partial(attention_kernel, group, span, latent),
        in_specs=[
            pl.BlockSpec(memory_space=pltpu.SMEM),
            pl.BlockSpec(memory_space=pltpu.SMEM),
            pl.BlockSpec(memory_space=pltpu.HBM),
            pl.BlockSpec(memory_space=pltpu.HBM),
            vmem,
            vmem,
        ],
        out_specs=vmem,
        scratch_shapes=[
            pltpu.VMEM(queries.shape, bf16),
            pltpu.VMEM(cache.shape, bf16),
            pltpu.VMEM((heads, count, latent), f32),
            pltpu.SemaphoreType.DMA((count // span,)),
            pltpu.SemaphoreType.DMA((count // span,)),
        ],
        out_shape=jax.ShapeDtypeStruct((heads, count, latent), bf16),
        compiler_params=pltpu.CompilerParams(vmem_limit_bytes=large_vmem),
        cost_estimate=pl.CostEstimate(
            flops=4 * count * heads * width * slots,
            bytes_accessed=2 * count * width * (heads + slots),
            transcendentals=count * heads * slots,
        ),
        name="attention",
    )(lengths, positions, queries, cache, new_latent, rotary_frequencies(width - latent))


def value_kernel(block, order_ref, a_ref, v_ref, value_ref, gathered):
    for p in range(tp_size):
        gathered[:, p * block : (p + 1) * block, :] = a_ref[order_ref[p]]
    heads, width = v_ref.shape[0], v_ref.shape[2]
    for h in range(heads):
        value_ref[:, h * width : (h + 1) * width] = jnp.dot(
            gathered[h], v_ref[h], preferred_element_type=f32
        ).astype(bf16)


def value_rows(order, arrived, value_weight):
    sources, heads, block, latent = arrived.shape
    rows, depth = sources * block, heads * value_weight.shape[2]
    vmem = pl.BlockSpec(memory_space=pltpu.VMEM)
    return pl.pallas_call(
        functools.partial(value_kernel, block),
        in_specs=[pl.BlockSpec(memory_space=pltpu.SMEM), vmem, vmem],
        out_specs=vmem,
        out_shape=jax.ShapeDtypeStruct((rows, depth), bf16),
        scratch_shapes=[pltpu.VMEM((heads, rows, latent), bf16)],
        compiler_params=pltpu.CompilerParams(vmem_limit_bytes=vmem_limit),
        cost_estimate=pl.CostEstimate(
            flops=2 * rows * depth * latent, bytes_accessed=4 * rows * depth, transcendentals=0
        ),
        name="value_rows",
    )(order, arrived, value_weight)


def out_kernel(block, spans, orders, value_ref, w_ref, *out_refs):
    values = value_ref[...]
    half = values.shape[0] // 2
    for i, (begin, columns) in enumerate(spans):
        rows = jnp.concatenate([values[p * block : (p + 1) * block] for p in orders[i]], axis=0)
        result = jnp.dot(
            rows, w_ref[:, begin : begin + columns], preferred_element_type=f32
        ).astype(bf16)
        out_refs[2 * i][...] = result[:half]
        out_refs[2 * i + 1][...] = result[half:]


def project(values, w_out, block, spans, orders):
    rows, depth = values.shape
    width = w_out.shape[1]
    vmem = pl.BlockSpec(memory_space=pltpu.VMEM)
    out_shape = []
    for _, columns in spans:
        out_shape += [jax.ShapeDtypeStruct((rows // 2, columns), bf16)] * 2
    return pl.pallas_call(
        functools.partial(out_kernel, block, spans, orders),
        in_specs=[vmem, vmem],
        out_specs=[vmem] * len(out_shape),
        out_shape=out_shape,
        compiler_params=pltpu.CompilerParams(vmem_limit_bytes=vmem_limit),
        cost_estimate=pl.CostEstimate(
            flops=2 * rows * depth * width, bytes_accessed=2 * depth * width, transcendentals=0
        ),
        name="out_proj",
    )(values, w_out)


def gated_kernel(spans, layouts, block, last, *refs):
    refs = list(refs)
    if last:
        order_ref = refs.pop(0)
    x_refs = [[refs.pop(0) for _ in range(2)] for _ in spans]
    gain_ref, gate_ref, up_ref = refs.pop(0), refs.pop(0), refs.pop(0)
    if last:
        acc_in, square_in, out_ref, ordered = refs
    else:
        acc_ref, square_ref = refs
    lanes = 128
    hidden = gate_ref.shape[1]
    squares, gates, ups = ([[] for _ in range(tp_size)] for _ in range(3))
    for (begin, columns), pieces, layout in zip(spans, x_refs, layouts):
        wide = jnp.concatenate(
            [pieces[p][at : at + block, :] for _, p, at in layout], axis=0
        ).astype(f32)
        square = None
        for j in range(0, columns, lanes):
            part = wide[:, j : j + lanes]
            square = part * part if square is None else square + part * part
        gain = gain_ref[:, begin : begin + columns].astype(f32)
        scaled = (wide * gain).astype(bf16)
        gate = jnp.dot(scaled, gate_ref[begin : begin + columns, :], preferred_element_type=f32)
        up = jnp.dot(scaled, up_ref[begin : begin + columns, :], preferred_element_type=f32)
        for i, (place, _, _) in enumerate(layout):
            rows = slice(i * block, (i + 1) * block)
            squares[place].append(square[rows])
            gates[place].append(gate[rows])
            ups[place].append(up[rows])

    for place in range(tp_size):
        rows = slice(place * block, (place + 1) * block)
        if last:
            squares[place].append(square_in[rows, :])
            gates[place].append(acc_in[rows, :hidden])
            ups[place].append(acc_in[rows, hidden:])
        elif not gates[place]:
            squares[place].append(jnp.zeros((block, lanes), f32))
            gates[place].append(jnp.zeros((block, hidden), f32))
            ups[place].append(jnp.zeros((block, hidden), f32))
        square, gate, up = (add(*found[place]) for found in (squares, gates, ups))
        if not last:
            square_ref[rows, :] = square
            acc_ref[rows, :hidden] = gate
            acc_ref[rows, hidden:] = up
            continue
        mean = jnp.sum(square, axis=-1, keepdims=True) * (1.0 / gate_ref.shape[0])
        scale = lax.rsqrt(mean + 1e-06)
        gate, up = gate * scale, up * scale
        active = gate / (1.0 + jnp.exp(-gate)) * up
        own = out_ref.shape[1] // tp_size
        at = pl.multiple_of(order_ref[place] * own, own)
        for m in range(out_ref.shape[0]):
            ordered[m, pl.ds(at, own), :] = active[m * own : (m + 1) * own]
    if last:
        out_ref[...] = ordered[...].astype(bf16)


def gated(order, pieces, spans, layouts, block, gain, gate, up, micro, carried):
    columns, hidden = gate.shape
    rows = tp_size * block
    last = carried is not None
    vmem = pl.BlockSpec(memory_space=pltpu.VMEM)
    args = [piece for stream in pieces for piece in stream] + [gain, gate, up]
    in_specs = [vmem] * len(args)
    if last:
        args = [order] + args + list(carried)
        in_specs = [pl.BlockSpec(memory_space=pltpu.SMEM)] + in_specs + [vmem] * 2
        out_dims = (micro, rows // micro, hidden)
        out_shape = jax.ShapeDtypeStruct(out_dims, bf16)
        out_specs, scratch = vmem, [pltpu.VMEM(out_dims, f32)]
    else:
        out_shape = [
            jax.ShapeDtypeStruct((rows, 2 * hidden), f32),
            jax.ShapeDtypeStruct((rows, 128), f32),
        ]
        out_specs, scratch = [vmem, vmem], []
    return pl.pallas_call(
        functools.partial(gated_kernel, spans, layouts, block, last),
        in_specs=in_specs,
        out_specs=out_specs,
        out_shape=out_shape,
        scratch_shapes=scratch,
        compiler_params=pltpu.CompilerParams(vmem_limit_bytes=vmem_limit),
        cost_estimate=pl.CostEstimate(
            flops=2 * rows * columns * hidden,
            bytes_accessed=4 * columns * hidden,
            transcendentals=0,
        ),
        name="gated_far" if last else "gated_near",
    )(*args)


def add(*parts):
    total = parts[0].astype(f32)
    for part in parts[1:]:
        total = total + part.astype(f32)
    return total


def shards(
    residual,
    queries,
    latent_cache,
    new_latent,
    lengths,
    positions,
    latent_value_weight,
    w_out,
    norm_gain,
    gate_weight,
    up_weight,
):
    latent = latent_value_weight.shape[1]
    micro, own_rows, width = residual.shape
    block = micro * own_rows
    heads = queries.shape[2]
    me = lax.axis_index("tp")
    places = [(c, p, q, z) for c in range(2) for p in range(2) for q in range(2) for z in range(2)]
    order = jnp.stack(
        [((me // 4) ^ p ^ (3 * q)) * 4 + (((me // 2) % 2) ^ z) * 2 + ((me % 2) ^ c) for c, p, q, z in places]
    ).astype(jnp.int32)
    attended = attention(
        queries.reshape((block,) + queries.shape[2:]),
        jnp.swapaxes(latent_cache, 2, 3).reshape(block, latent_cache.shape[3], -1),
        new_latent.reshape(block, -1),
        lengths,
        positions,
        latent,
    )
    arrived = lax.all_to_all(
        attended.reshape(tp_size, heads // tp_size, block, latent),
        "tp",
        split_axis=0,
        concat_axis=0,
        tiled=True,
    )

    streams = ("pqz", "qzp", "zpq") * stream_sets
    each = range(len(streams))
    step = -(-width // (len(streams) * 128)) * 128
    spans = [(i * step, min(step, width - i * step)) for i in each]
    names = "cpqz"
    orders, layouts = [], []
    for dims in streams:
        rank = [names.index(d) for d in "c" + dims]
        orders.append(sorted(range(tp_size), key=lambda i: [places[i][k] for k in rank]))
        layouts.append(
            [
                [
                    (i, at[rank[0]], (at[rank[2]] * 2 + at[rank[3]]) * block)
                    for i, at in enumerate(places)
                    if at[rank[1]] == side
                ]
                for side in range(2)
            ]
        )
    values = value_rows(order, arrived, latent_value_weight)
    projected = project(values, w_out, block, spans, orders)
    kept, sent = projected[0::2], projected[1::2]
    flat_residual = residual.reshape(block, width)

    pair = [add(kept[i], send(sent[i], "c")).astype(bf16) for i in each]
    four = [
        add(pair[i][: 4 * block], send(pair[i][4 * block :], streams[i][0])).astype(bf16)
        for i in each
    ]
    two = []
    for i in each:
        total = add(four[i][: 2 * block], send(four[i][2 * block :], streams[i][1]))
        begin, columns = spans[i]
        own = total[:block] + flat_residual[:, begin : begin + columns].astype(f32)
        two.append(jnp.concatenate([own, total[block:]], axis=0).astype(bf16))
    other = [send(two[i], streams[i][2]) for i in each]
    both = [
        jnp.concatenate(
            [add(two[i][:block], other[i][block:]), add(two[i][block:], other[i][:block])], axis=0
        ).astype(bf16)
        for i in each
    ]
    near = [jnp.concatenate([both[i], send(both[i], streams[i][1])], axis=0) for i in each]
    far = [send(near[i], streams[i][0]) for i in each]
    def products(sides, side, carried):
        return gated(
            order,
            [[sides[i], send(sides[i], "c")] for i in each],
            spans,
            [layout[side] for layout in layouts],
            block,
            norm_gain.reshape(1, width),
            gate_weight,
            up_weight,
            micro,
            carried,
        )

    carried = products(near, 0, None)
    far, carried = lax.optimization_barrier((far, carried))
    activation = products(far, 1, carried)
    after_attention = jnp.concatenate([both[i][:block] for i in each], axis=1)
    return (after_attention.reshape(residual.shape), activation)


def solution(mesh):
    return jax.shard_map(
        shards,
        mesh=mesh,
        in_specs=(
            P(None, ("dp", "tp"), None),
            P(None, ("dp", "tp"), None, None),
            P(None, ("dp", "tp"), None, None),
            P(None, ("dp", "tp"), None),
            P(None, ("dp", "tp")),
            P(None, ("dp", "tp")),
            P("tp", None, None),
            P("tp", None),
            P(),
            P(None, "tp"),
            P(None, "tp"),
        ),
        out_specs=(P(None, ("dp", "tp"), None), P(None, "dp", "tp")),
        check_vma=False,
    )
```

time: 95.6 us -> 89.8 us (0.939)
  waiting for transfers between devices: 44.1 us -> 40.3 us
  starting transfers between devices: 23.9 us -> 25.7 us
  other arithmetic: 3.3 us -> 1.81 us
  Pallas kernels: 18.6 us -> 17.3 us
    ppermute x24, waiting for transfers between devices: 28.5 us -> 24.7 us  [send(): return lax.ppermute(value, 'tp', pairs)]
    ppermute x24, starting transfers between devices: 16.6 us -> 18.4 us  [send(): return lax.ppermute(value, 'tp', pairs)]
    pallas_call x3 -> x4, Pallas kernels: 12.1 us -> 10.7 us  [the longest x2 7.62 us: gated(): pl.pallas_call(functools.partial(gated_kernel, spans, layouts, block, las...]
    unnamed x22 -> x20, local copies, waits for them, and re-layouts: 4 us -> 3.13 us
  transfers between devices with their start and end apart: 25 -> 25, of which waited for: 16 -> 15; matrix products, arithmetic and copies ran while one was open for 2% -> 2% of each run, Pallas kernels for 0% -> 4%
where the time goes in v4:
time: 89.8 us; the launch traced here: 89.5 us
  waiting for transfers between devices  40.3 us (45%)
  starting transfers between devices  25.7 us (29%)
  Pallas kernels  17.3 us (19%)
  local copies, waits for them, and re-layouts  3.37 us (4%)
  other arithmetic  1.81 us (2%)
  between operations  1.03 us (1%)
    ppermute x24, waiting for transfers between devices, send(): return lax.ppermute(value, 'tp', pairs)  24.7 us
    ppermute x24, starting transfers between devices, send(): return lax.ppermute(value, 'tp', pairs)  18.4 us
    all_to_all x1, waiting for transfers between devices, shards(): lax.all_to_all(attended.reshape(tp_size, heads // tp_size, block, latent)...  15.6 us
    pallas_call x2, Pallas kernels, gated(): pl.pallas_call(functools.partial(gated_kernel, spans, layouts, block, las...  7.62 us
    all_to_all x1, starting transfers between devices, shards(): lax.all_to_all(attended.reshape(tp_size, heads // tp_size, block, latent)...  7.32 us
    pallas_call x1, Pallas kernels, attention(): pl.pallas_call(functools.partial(attention_kernel, group, span, latent),...  6.56 us
    unnamed x20, local copies, waits for them, and re-layouts  3.13 us
    pallas_call x1, Pallas kernels, project(): pl.pallas_call(functools.partial(out_kernel, block, spans, orders), in_sp...  2.15 us
  transfers between devices with their start and end apart: 25, of which 15 were waited for; matrix products, arithmetic and copies ran while one was open for 2% of the time, Pallas kernels for 4%

profile of v4, /device:TPU:1, one launch (start us, length us, event | category | flops | bytes accessed | tf_op | source)
XLA Modules:
  0.0 89.5 jit_solution(525511635517692653)
XLA Ops:
  0.6 6.6 %attention.1 = bf16[64,16,512]{2,1,0:T(8,128)(2,1)} custom-call(s32[2,8]{1,0:T(2,128)} %len_ref.1, s32[2,8]{1,0:T(2,128)} %pos_ref.1, bf16[16,64,576]{2,1,0:T(8,128)(2,1)} %bitcast.31, bf16[16,576,256]{2,1,0:T(8,128)(2,1)} %bitcast.29, bf16[16,576]{1,0:T(8,128)(2,1)} %bitcast.34, f32[1,64]{1,0:T(1,128)} %constant.167.clone.f_ref), custom_call_target="tpu_custom_call" | custom-call | flops 603979776 | bytes 5898240 | tf_op jit(solution)/shard_map/attention/pallas_call | solution.py:115
  7.2 7.3 %all-to-all-start = ((bf16[16,4,16,512]{3,2,1,0:T(8,128)(2,1)}), bf16[16,4,16,512]{3,2,1,0:T(8,128)(2,1)S(1)}, u32[]{:S(2)}, u32[]{:S(2)}) async-start(bf16[16,4,16,512]{3,2,1,0:T(8,128)(2,1)} %bitcast.30), calls=%async_computation | async-start | bytes 2097152 | tf_op jit(solution)/shard_map/all_to_all | solution.py:335
  14.6 15.6 %all-to-all-done.a_ref = bf16[16,4,16,512]{3,2,1,0:T(8,128)(2,1)S(1)} async-done(((bf16[16,4,16,512]{3,2,1,0:T(8,128)(2,1)}), bf16[16,4,16,512]{3,2,1,0:T(8,128)(2,1)S(1)}, u32[]{:S(2)}, u32[]{:S(2)}) %all-to-all-start) | async-done | bytes 1048608 | tf_op jit(solution)/shard_map/all_to_all | solution.py:335
  30.3 1.0 %value_rows.1.value_ref = bf16[256,512]{1,0:T(8,128)(2,1)S(1)} custom-call(s32[16]{0:T(128)S(1)} %stack.67.order_ref.refs_0_, bf16[16,4,16,512]{3,2,1,0:T(8,128)(2,1)S(1)} %all-to-all-done.a_ref, bf16[4,512,128]{2,1,0:T(8,128)(2,1)S(1)} %copy-done.1), custom_call_target="tpu_custom_call" | custom-call | flops 134217728 | bytes 524288 | tf_op jit(solution)/shard_map/value_rows/pallas_call | solution.py:158
  31.2 3.1 %copy-done = bf16[512,7168]{1,0:T(8,128)(2,1)S(1)} copy-done((bf16[512,7168]{1,0:T(8,128)(2,1)S(1)}, bf16[512,7168]{1,0:T(8,128)(2,1)}, u32[]{:S(2)}) %copy-start) | copy-done | bytes 7340056
  34.3 2.1 %out_proj.1 = (bf16[128,2432]{1,0:T(8,128)(2,1)S(1)}, bf16[128,2432]{1,0:T(8,128)(2,1)S(1)}, bf16[128,2432]{1,0:T(8,128)(2,1)S(1)}, bf16[128,2432]{1,0:T(8,128)(...) custom-call(bf16[256,512]{1,0:T(8,128)(2,1)S(1)} %value_rows.1.value_ref, ...), custom_call_target="tpu_custom_call" | custom-call | flops 1879048192 | bytes 7340032 | tf_op jit(solution)/shard_map/out_proj/pallas_call | solution.py:191
  36.5 0.9 %collective-permute-start.8 = (bf16[128,2304]{1,0:T(8,128)(2,1)S(1)}, bf16[128,2304]{1,0:T(8,128)(2,1)S(1)}, u32[]{:S(2)}, u32[]{:S(2)}) collective-permute-start(bf16[128,2304]{1,0:T(8,128)(2,1)S(1)} %get-tuple-element.20), channel_id=1, source_target_pairs={{0,1},{1,0},{2,3},{3,2},{4,5},{5,4},{6,7},{7,6},{8,9},{9,8},{10,11... | collective-permute-start | bytes 1769480 | tf_op jit(solution)/shard_map/ppermute | solution.py:33
  37.9 1.1 %collective-permute-done.8 = bf16[128,2304]{1,0:T(8,128)(2,1)S(1)} collective-permute-done((bf16[128,2304]{1,0:T(8,128)(2,1)S(1)}, bf16[128,2304]{1,0:T(8,128)(2,1)S(1)}, u32[]{:S(2)}, u32[]{:S(2)}) %collective-permute-start.8) | collective-permute-done | bytes 589856 | tf_op jit(solution)/shard_map/ppermute | solution.py:33
  40.2 0.6 collective-permute-done.4
  41.0 1.2 %collective-permute-start.5 = (bf16[64,2432]{1,0:T(8,128)(2,1)S(1)}, bf16[64,2432]{1,0:T(8,128)(2,1)S(1)}, u32[]{:S(2)}, u32[]{:S(2)}) collective-permute-start(bf16[64,2432]{1,0:T(8,128)(2,1)S(1)} %slice.147), channel_id=1, source_target_pairs={{0,12},{1,13},{2,14},{3,15},{4,8},{5,9},{6,10},{7,11},{8,4},{9,5},... | collective-permute-start | bytes 933896 | tf_op jit(solution)/shard_map/ppermute | solution.py:33
  42.2 5.4 %collective-permute-done.9 = bf16[64,2304]{1,0:T(8,128)(2,1)S(1)} collective-permute-done((bf16[64,2304]{1,0:T(8,128)(2,1)S(1)}, bf16[64,2304]{1,0:T(8,128)(2,1)S(1)}, u32[]{:S(2)}, u32[]{:S(2)}) %collective-permute-start.9) | collective-permute-done | bytes 294944 | tf_op jit(solution)/shard_map/ppermute | solution.py:33
  47.7 1.0 %collective-permute-done.1 = bf16[64,2432]{1,0:T(8,128)(2,1)S(1)} collective-permute-done((bf16[64,2432]{1,0:T(8,128)(2,1)S(1)}, bf16[64,2432]{1,0:T(8,128)(2,1)S(1)}, u32[]{:S(2)}, u32[]{:S(2)}) %collective-permute-start.1) | collective-permute-done | bytes 311328 | tf_op jit(solution)/shard_map/ppermute | solution.py:33
  48.9 0.8 collective-permute-start.2
  49.6 1.2 %collective-permute-done.5 = bf16[64,2432]{1,0:T(8,128)(2,1)S(1)} collective-permute-done((bf16[64,2432]{1,0:T(8,128)(2,1)S(1)}, bf16[64,2432]{1,0:T(8,128)(2,1)S(1)}, u32[]{:S(2)}, u32[]{:S(2)}) %collective-permute-start.5) | collective-permute-done | bytes 311328 | tf_op jit(solution)/shard_map/ppermute | solution.py:33
  51.8 1.0 %collective-permute-start.11 = (bf16[32,2304]{1,0:T(8,128)(2,1)S(1)}, bf16[32,2304]{1,0:T(8,128)(2,1)S(1)}, u32[]{:S(2)}, u32[]{:S(2)}) collective-permute-start(bf16[32,2304]{1,0:T(8,128)(2,1)S(1)} %pad_maximum_fusion.7), channel_id=1, source_target_pairs={{0,12},{1,13},{2,14},{3,15},{4,8},{5,9},{6,10},{7,11},{8,4},{9,5},... | collective-permute-start | bytes 442376 | tf_op jit(solution)/shard_map/ppermute | solution.py:33
  52.9 2.6 %collective-permute-done.6 = bf16[32,2432]{1,0:T(8,128)(2,1)S(1)} collective-permute-done((bf16[32,2432]{1,0:T(8,128)(2,1)S(1)}, bf16[32,2432]{1,0:T(8,128)(2,1)S(1)}, u32[]{:S(2)}, u32[]{:S(2)}) %collective-permute-start.6) | collective-permute-done | bytes 155680 | tf_op jit(solution)/shard_map/ppermute | solution.py:33
  55.9 1.6 %collective-permute-done.11 = bf16[32,2304]{1,0:T(8,128)(2,1)S(1)} collective-permute-done((bf16[32,2304]{1,0:T(8,128)(2,1)S(1)}, bf16[32,2304]{1,0:T(8,128)(2,1)S(1)}, u32[]{:S(2)}, u32[]{:S(2)}) %collective-permute-start.11) | collective-permute-done | bytes 147488 | tf_op jit(solution)/shard_map/ppermute | solution.py:33
  57.6 2.4 %collective-permute-done.7 = bf16[32,2432]{1,0:T(8,128)(2,1)S(1)} collective-permute-done((bf16[32,2432]{1,0:T(8,128)(2,1)S(1)}, bf16[32,2432]{1,0:T(8,128)(2,1)S(1)}, u32[]{:S(2)}, u32[]{:S(2)}) %collective-permute-start.7) | collective-permute-done | bytes 155680 | tf_op jit(solution)/shard_map/ppermute | solution.py:33
  60.4 1.1 %collective-permute-start.12 = (bf16[32,2432]{1,0:T(8,128)(2,1)S(1)}, bf16[32,2432]{1,0:T(8,128)(2,1)S(1)}, u32[]{:S(2)}, u32[]{:S(2)}) collective-permute-start(bf16[32,2432]{1,0:T(8,128)(2,1)S(1)} %pad_maximum_fusion.5), channel_id=1, source_target_pairs={{0,12},{1,13},{2,14},{3,15},{4,8},{5,9},{6,10},{7,11},{8,4},{9,5},... | collective-permute-start | bytes 466952 | tf_op jit(solution)/shard_map/ppermute | solution.py:33
  61.5 1.4 %collective-permute-done.16 = bf16[32,2304]{1,0:T(8,128)(2,1)S(1)} collective-permute-done((bf16[32,2304]{1,0:T(8,128)(2,1)S(1)}, bf16[32,2304]{1,0:T(8,128)(2,1)S(1)}, u32[]{:S(2)}, u32[]{:S(2)}) %collective-permute-start.16) | collective-permute-done | bytes 147488 | tf_op jit(solution)/shard_map/ppermute | solution.py:33
  63.0 3.5 %collective-permute-start.20 = (bf16[64,2304]{1,0:T(8,128)(2,1)S(1)}, bf16[64,2304]{1,0:T(8,128)(2,1)S(1)}, u32[]{:S(2)}, u32[]{:S(2)}) collective-permute-start(bf16[64,2304]{1,0:T(8,128)(2,1)S(1)} %pad_maximum_fusion.2.refs_4_), channel_id=1, source_target_pairs={{0,1},{1,0},{2,3},{3,2},{4,5},{5,4},{6,7},{7,6},{8,9},{9,8},{10,11... | collective-permute-start | bytes 884744 | tf_op jit(solution)/shard_map/ppermute | solution.py:33
  66.5 2.9 %collective-permute-start.19 = (bf16[64,2432]{1,0:T(8,128)(2,1)S(1)}, bf16[64,2432]{1,0:T(8,128)(2,1)S(1)}, u32[]{:S(2)}, u32[]{:S(2)}) collective-permute-start(bf16[64,2432]{1,0:T(8,128)(2,1)S(1)} %pad_maximum_fusion.1.refs_2_), channel_id=1, source_target_pairs={{0,1},{1,0},{2,3},{3,2},{4,5},{5,4},{6,7},{7,6},{8,9},{9,8},{10,11... | collective-permute-start | bytes 933896 | tf_op jit(solution)/shard_map/ppermute | solution.py:33
  69.5 2.4 %collective-permute-start.18 = (bf16[64,2432]{1,0:T(8,128)(2,1)S(1)}, bf16[64,2432]{1,0:T(8,128)(2,1)S(1)}, u32[]{:S(2)}, u32[]{:S(2)}) collective-permute-start(bf16[64,2432]{1,0:T(8,128)(2,1)S(1)} %pad_maximum_fusion.refs_0_), channel_id=1, source_target_pairs={{0,1},{1,0},{2,3},{3,2},{4,5},{5,4},{6,7},{7,6},{8,9},{9,8},{10,11... | collective-permute-start | bytes 933896 | tf_op jit(solution)/shard_map/ppermute | solution.py:33
  72.0 0.7 collective-permute-start.15
  72.7 0.6 collective-permute-start.17
  73.4 3.1 %gated_near.1 = (f32[256,1280]{1,0:T(8,128)S(1)}, f32[256,128]{1,0:T(8,128)S(1)}) custom-call(bf16[64,2432]{1,0:T(8,128)(2,1)S(1)} %pad_maximum_fusion.refs_0_, bf16[64,2432]{1,0:T(8,128)(2,1)S(1)} %collective-permute-done.18.refs_1_, bf16[64,2432]{1,0:T(8,128)(2,1)S(1)} %pad_maximum_fusion.1.refs_2_, bf16[64,2432]{1,0:T(8,128)(2,1)S(1)} %collective-permute-done.19.refs_3_, ...), custom_call_target="tpu_custom_call" | custom-call | flops 2348810240 | bytes 18350080 | tf_op jit(solution)/shard_map/gated_near/pallas_call | solution.py:282
  76.6 4.4 %collective-permute-done.17.refs_5_ = bf16[64,2304]{1,0:T(8,128)(2,1)S(1)} collective-permute-done((bf16[64,2304]{1,0:T(8,128)(2,1)S(1)}, bf16[64,2304]{1,0:T(8,128)(2,1)S(1)}, u32[]{:S(2)}, u32[]{:S(2)}) %collective-permute-start.17) | collective-permute-done | bytes 294944 | tf_op jit(solution)/shard_map/ppermute | solution.py:33
  80.9 1.1 %collective-permute-done.15.refs_3_ = bf16[64,2432]{1,0:T(8,128)(2,1)S(1)} collective-permute-done((bf16[64,2432]{1,0:T(8,128)(2,1)S(1)}, bf16[64,2432]{1,0:T(8,128)(2,1)S(1)}, u32[]{:S(2)}, u32[]{:S(2)}) %collective-permute-start.15) | collective-permute-done | bytes 311328 | tf_op jit(solution)/shard_map/ppermute | solution.py:33
  82.1 0.9 collective-permute-start.21
  83.5 0.7 maximum_bitcast_fusion
  84.2 0.9 collective-permute-done.23.refs_6_
  85.1 4.5 %gated_far.1 = bf16[2,128,640]{2,1,0:T(8,128)(2,1)} custom-call(s32[16]{0:T(128)S(1)} %stack.67.order_ref.refs_0_, bf16[64,2432]{1,0:T(8,128)(2,1)S(1)} %collective-permute-done.13.refs_1_, bf16[64,2432]{1,0:T(8,128)(2,1)S(1)} %collective-permute-done.21.refs_2_, bf16[64,2432]{1,0:T(8,128)(2,1)S(1)} %collective-permute-done.15.refs_3_, ...), custom_call_target="tpu_custom_call" | custom-call | flops 2348810240 | bytes 18350080 | tf_op jit(solution)/shard_map/gated_far/pallas_call | solution.py:282
  (80 shorter events, 4.6 us)
Async XLA Ops:
  7.2 23.1 %copy-start.1 = (bf16[4,512,128]{2,1,0:T(8,128)(2,1)S(1)}, bf16[4,512,128]{2,1,0:T(8,128)(2,1)}, u32[]{:S(2)}) copy-start(bf16[4,512,128]{2,1,0:T(8,128)(2,1)} %v_ref.1) | copy-start | bytes 1572868
  7.2 66.1 %slice-start.3 = ((s8[9175040]{0:T(1024)(128)(4,1)}), s8[786432]{0:T(1024)(128)(4,1)S(1)}, s32[]{:S(2)}) async-start(s8[9175040]{0:T(1024)(128)(4,1)} %bitcast.27), calls=%async_computation.4 | async-start | bytes 1572864
  7.2 23.0 %all-to-all-start = ((bf16[16,4,16,512]{3,2,1,0:T(8,128)(2,1)}), bf16[16,4,16,512]{3,2,1,0:T(8,128)(2,1)S(1)}, u32[]{:S(2)}, u32[]{:S(2)}) async-start(bf16[16,4,16,512]{3,2,1,0:T(8,128)(2,1)} %bitcast.30), calls=%async_computation | async-start | bytes 2097152 | tf_op jit(solution)/shard_map/all_to_all | solution.py:335
  34.3 39.0 %slice-start = ((s8[9175040]{0:T(1024)(128)(4,1)}), s8[4194304]{0:T(1024)(128)(4,1)S(1)}, s32[]{:S(2)}) async-start(s8[9175040]{0:T(1024)(128)(4,1)} %bitcast.25), calls=%async_computation.1 | async-start | bytes 8388608
  34.3 39.1 %slice-start.4 = ((s8[9175040]{0:T(1024)(128)(4,1)}), s8[4194304]{0:T(1024)(128)(4,1)S(1)}, s32[]{:S(2)}) async-start(s8[9175040]{0:T(1024)(128)(4,1)} %bitcast.27), calls=%async_computation.5 | async-start | bytes 8388608
  36.5 2.6 %collective-permute-start.8 = (bf16[128,2304]{1,0:T(8,128)(2,1)S(1)}, bf16[128,2304]{1,0:T(8,128)(2,1)S(1)}, u32[]{:S(2)}, u32[]{:S(2)}) collective-permute-start(bf16[128,2304]{1,0:T(8,128)(2,1)S(1)} %get-tuple-element.20), channel_id=1, source_target_pairs={{0,1},{1,0},{2,3},{3,2},{4,5},{5,4},{6,7},{7,6},{8,9},{9,8},{10,11... | collective-permute-start | bytes 1769480 | tf_op jit(solution)/shard_map/ppermute | solution.py:33
  37.4 2.5 %collective-permute-start = (bf16[128,2432]{1,0:T(8,128)(2,1)S(1)}, bf16[128,2432]{1,0:T(8,128)(2,1)S(1)}, u32[]{:S(2)}, u32[]{:S(2)}) collective-permute-start(bf16[128,2432]{1,0:T(8,128)(2,1)S(1)} %get-tuple-element.16), channel_id=1, source_target_pairs={{0,1},{1,0},{2,3},{3,2},{4,5},{5,4},{6,7},{7,6},{8,9},{9,8},{10,11... | collective-permute-start | bytes 1867784 | tf_op jit(solution)/shard_map/ppermute | solution.py:33
  37.5 3.3 %collective-permute-start.4 = (bf16[128,2432]{1,0:T(8,128)(2,1)S(1)}, bf16[128,2432]{1,0:T(8,128)(2,1)S(1)}, u32[]{:S(2)}, u32[]{:S(2)}) collective-permute-start(bf16[128,2432]{1,0:T(8,128)(2,1)S(1)} %get-tuple-element.18), channel_id=1, source_target_pairs={{0,1},{1,0},{2,3},{3,2},{4,5},{5,4},{6,7},{7,6},{8,9},{9,8},{10,11... | collective-permute-start | bytes 1867784 | tf_op jit(solution)/shard_map/ppermute | solution.py:33
  39.0 34.3 %slice-start.1 = ((s8[9175040]{0:T(1024)(128)(4,1)}), s8[4194304]{0:T(1024)(128)(4,1)S(1)}, s32[]{:S(2)}) async-start(s8[9175040]{0:T(1024)(128)(4,1)} %bitcast.25), calls=%async_computation.2 | async-start | bytes 8388608
  39.2 8.3 %collective-permute-start.9 = (bf16[64,2304]{1,0:T(8,128)(2,1)S(1)}, bf16[64,2304]{1,0:T(8,128)(2,1)S(1)}, u32[]{:S(2)}, u32[]{:S(2)}) collective-permute-start(bf16[64,2304]{1,0:T(8,128)(2,1)S(1)} %slice.155), channel_id=1, source_target_pairs={{0,2},{1,3},{2,0},{3,1},{4,6},{5,7},{6,4},{7,5},{8,10},{9,11},{10,... | collective-permute-start | bytes 884744 | tf_op jit(solution)/shard_map/ppermute | solution.py:33
  40.1 8.7 %collective-permute-start.1 = (bf16[64,2432]{1,0:T(8,128)(2,1)S(1)}, bf16[64,2432]{1,0:T(8,128)(2,1)S(1)}, u32[]{:S(2)}, u32[]{:S(2)}) collective-permute-start(bf16[64,2432]{1,0:T(8,128)(2,1)S(1)} %slice.139), channel_id=1, source_target_pairs={{0,4},{1,5},{2,6},{3,7},{4,0},{5,1},{6,2},{7,3},{8,12},{9,13},{10,... | collective-permute-start | bytes 933896 | tf_op jit(solution)/shard_map/ppermute | solution.py:33
  41.0 9.9 %collective-permute-start.5 = (bf16[64,2432]{1,0:T(8,128)(2,1)S(1)}, bf16[64,2432]{1,0:T(8,128)(2,1)S(1)}, u32[]{:S(2)}, u32[]{:S(2)}) collective-permute-start(bf16[64,2432]{1,0:T(8,128)(2,1)S(1)} %slice.147), channel_id=1, source_target_pairs={{0,12},{1,13},{2,14},{3,15},{4,8},{5,9},{6,10},{7,11},{8,4},{9,5},... | collective-permute-start | bytes 933896 | tf_op jit(solution)/shard_map/ppermute | solution.py:33
  47.6 25.8 %slice-start.5 = ((s8[9175040]{0:T(1024)(128)(4,1)}), s8[4194304]{0:T(1024)(128)(4,1)S(1)}, s32[]{:S(2)}) async-start(s8[9175040]{0:T(1024)(128)(4,1)} %bitcast.27), calls=%async_computation.6 | async-start | bytes 8388608
  47.6 4.1 %collective-permute-start.10 = (bf16[32,2304]{1,0:T(8,128)(2,1)S(1)}, bf16[32,2304]{1,0:T(8,128)(2,1)S(1)}, u32[]{:S(2)}, u32[]{:S(2)}) collective-permute-start(bf16[32,2304]{1,0:T(8,128)(2,1)S(1)} %slice.157), channel_id=1, source_target_pairs={{0,4},{1,5},{2,6},{3,7},{4,0},{5,1},{6,2},{7,3},{8,12},{9,13},{10,... | collective-permute-start | bytes 442376 | tf_op jit(solution)/shard_map/ppermute | solution.py:33
  48.9 24.5 %slice-start.2 = ((s8[9175040]{0:T(1024)(128)(4,1)}), s8[786432]{0:T(1024)(128)(4,1)S(1)}, s32[]{:S(2)}) async-start(s8[9175040]{0:T(1024)(128)(4,1)} %bitcast.25), calls=%async_computation.3 | async-start | bytes 1572864
  48.9 6.6 %collective-permute-start.2 = (bf16[32,2432]{1,0:T(8,128)(2,1)S(1)}, bf16[32,2432]{1,0:T(8,128)(2,1)S(1)}, u32[]{:S(2)}, u32[]{:S(2)}) collective-permute-start(bf16[32,2432]{1,0:T(8,128)(2,1)S(1)} %slice.141), channel_id=1, source_target_pairs={{0,12},{1,13},{2,14},{3,15},{4,8},{5,9},{6,10},{7,11},{8,4},{9,5},... | collective-permute-start | bytes 466952 | tf_op jit(solution)/shard_map/ppermute | solution.py:33
  51.0 4.5 %collective-permute-start.6 = (bf16[32,2432]{1,0:T(8,128)(2,1)S(1)}, bf16[32,2432]{1,0:T(8,128)(2,1)S(1)}, u32[]{:S(2)}, u32[]{:S(2)}) collective-permute-start(bf16[32,2432]{1,0:T(8,128)(2,1)S(1)} %slice.149), channel_id=1, source_target_pairs={{0,2},{1,3},{2,0},{3,1},{4,6},{5,7},{6,4},{7,5},{8,10},{9,11},{10,... | collective-permute-start | bytes 466952 | tf_op jit(solution)/shard_map/ppermute | solution.py:33
  51.8 5.7 %collective-permute-start.11 = (bf16[32,2304]{1,0:T(8,128)(2,1)S(1)}, bf16[32,2304]{1,0:T(8,128)(2,1)S(1)}, u32[]{:S(2)}, u32[]{:S(2)}) collective-permute-start(bf16[32,2304]{1,0:T(8,128)(2,1)S(1)} %pad_maximum_fusion.7), channel_id=1, source_target_pairs={{0,12},{1,13},{2,14},{3,15},{4,8},{5,9},{6,10},{7,11},{8,4},{9,5},... | collective-permute-start | bytes 442376 | tf_op jit(solution)/shard_map/ppermute | solution.py:33
  55.6 4.5 %collective-permute-start.7 = (bf16[32,2432]{1,0:T(8,128)(2,1)S(1)}, bf16[32,2432]{1,0:T(8,128)(2,1)S(1)}, u32[]{:S(2)}, u32[]{:S(2)}) collective-permute-start(bf16[32,2432]{1,0:T(8,128)(2,1)S(1)} %pad_maximum_fusion.4), channel_id=1, source_target_pairs={{0,4},{1,5},{2,6},{3,7},{4,0},{5,1},{6,2},{7,3},{8,12},{9,13},{10,... | collective-permute-start | bytes 466952 | tf_op jit(solution)/shard_map/ppermute | solution.py:33
  55.7 4.6 %collective-permute-start.3 = (bf16[32,2432]{1,0:T(8,128)(2,1)S(1)}, bf16[32,2432]{1,0:T(8,128)(2,1)S(1)}, u32[]{:S(2)}, u32[]{:S(2)}) collective-permute-start(bf16[32,2432]{1,0:T(8,128)(2,1)S(1)} %pad_maximum_fusion.3), channel_id=1, source_target_pairs={{0,2},{1,3},{2,0},{3,1},{4,6},{5,7},{6,4},{7,5},{8,10},{9,11},{10,... | collective-permute-start | bytes 466952 | tf_op jit(solution)/shard_map/ppermute | solution.py:33
  57.6 5.4 %collective-permute-start.16 = (bf16[32,2304]{1,0:T(8,128)(2,1)S(1)}, bf16[32,2304]{1,0:T(8,128)(2,1)S(1)}, u32[]{:S(2)}, u32[]{:S(2)}) collective-permute-start(bf16[32,2304]{1,0:T(8,128)(2,1)S(1)} %pad_maximum_fusion.8), channel_id=1, source_target_pairs={{0,4},{1,5},{2,6},{3,7},{4,0},{5,1},{6,2},{7,3},{8,12},{9,13},{10,... | collective-permute-start | bytes 442376 | tf_op jit(solution)/shard_map/ppermute | solution.py:33
  60.2 6.4 %collective-permute-start.14 = (bf16[32,2432]{1,0:T(8,128)(2,1)S(1)}, bf16[32,2432]{1,0:T(8,128)(2,1)S(1)}, u32[]{:S(2)}, u32[]{:S(2)}) collective-permute-start(bf16[32,2432]{1,0:T(8,128)(2,1)S(1)} %pad_maximum_fusion.6), channel_id=1, source_target_pairs={{0,2},{1,3},{2,0},{3,1},{4,6},{5,7},{6,4},{7,5},{8,10},{9,11},{10,... | collective-permute-start | bytes 466952 | tf_op jit(solution)/shard_map/ppermute | solution.py:33
  60.4 9.1 %collective-permute-start.12 = (bf16[32,2432]{1,0:T(8,128)(2,1)S(1)}, bf16[32,2432]{1,0:T(8,128)(2,1)S(1)}, u32[]{:S(2)}, u32[]{:S(2)}) collective-permute-start(bf16[32,2432]{1,0:T(8,128)(2,1)S(1)} %pad_maximum_fusion.5), channel_id=1, source_target_pairs={{0,12},{1,13},{2,14},{3,15},{4,8},{5,9},{6,10},{7,11},{8,4},{9,5},... | collective-permute-start | bytes 466952 | tf_op jit(solution)/shard_map/ppermute | solution.py:33
  63.0 9.7 %collective-permute-start.20 = (bf16[64,2304]{1,0:T(8,128)(2,1)S(1)}, bf16[64,2304]{1,0:T(8,128)(2,1)S(1)}, u32[]{:S(2)}, u32[]{:S(2)}) collective-permute-start(bf16[64,2304]{1,0:T(8,128)(2,1)S(1)} %pad_maximum_fusion.2.refs_4_), channel_id=1, source_target_pairs={{0,1},{1,0},{2,3},{3,2},{4,5},{5,4},{6,7},{7,6},{8,9},{9,8},{10,11... | collective-permute-start | bytes 884744 | tf_op jit(solution)/shard_map/ppermute | solution.py:33
  66.5 6.8 %collective-permute-start.19 = (bf16[64,2432]{1,0:T(8,128)(2,1)S(1)}, bf16[64,2432]{1,0:T(8,128)(2,1)S(1)}, u32[]{:S(2)}, u32[]{:S(2)}) collective-permute-start(bf16[64,2432]{1,0:T(8,128)(2,1)S(1)} %pad_maximum_fusion.1.refs_2_), channel_id=1, source_target_pairs={{0,1},{1,0},{2,3},{3,2},{4,5},{5,4},{6,7},{7,6},{8,9},{9,8},{10,11... | collective-permute-start | bytes 933896 | tf_op jit(solution)/shard_map/ppermute | solution.py:33
  69.5 3.8 %collective-permute-start.18 = (bf16[64,2432]{1,0:T(8,128)(2,1)S(1)}, bf16[64,2432]{1,0:T(8,128)(2,1)S(1)}, u32[]{:S(2)}, u32[]{:S(2)}) collective-permute-start(bf16[64,2432]{1,0:T(8,128)(2,1)S(1)} %pad_maximum_fusion.refs_0_), channel_id=1, source_target_pairs={{0,1},{1,0},{2,3},{3,2},{4,5},{5,4},{6,7},{7,6},{8,9},{9,8},{10,11... | collective-permute-start | bytes 933896 | tf_op jit(solution)/shard_map/ppermute | solution.py:33
  72.0 10.1 %collective-permute-start.15 = (bf16[64,2432]{1,0:T(8,128)(2,1)S(1)}, bf16[64,2432]{1,0:T(8,128)(2,1)S(1)}, u32[]{:S(2)}, u32[]{:S(2)}) collective-permute-start(bf16[64,2432]{1,0:T(8,128)(2,1)S(1)} %pad_maximum_fusion.1.refs_2_), channel_id=1, source_target_pairs={{0,12},{1,13},{2,14},{3,15},{4,8},{5,9},{6,10},{7,11},{8,4},{9,5},... | collective-permute-start | bytes 933896 | tf_op jit(solution)/shard_map/ppermute | solution.py:33
  72.7 9.4 %collective-permute-start.13 = (bf16[64,2432]{1,0:T(8,128)(2,1)S(1)}, bf16[64,2432]{1,0:T(8,128)(2,1)S(1)}, u32[]{:S(2)}, u32[]{:S(2)}) collective-permute-start(bf16[64,2432]{1,0:T(8,128)(2,1)S(1)} %pad_maximum_fusion.refs_0_), channel_id=1, source_target_pairs={{0,4},{1,5},{2,6},{3,7},{4,0},{5,1},{6,2},{7,3},{8,12},{9,13},{10,... | collective-permute-start | bytes 933896 | tf_op jit(solution)/shard_map/ppermute | solution.py:33
  72.7 8.2 %collective-permute-start.17 = (bf16[64,2304]{1,0:T(8,128)(2,1)S(1)}, bf16[64,2304]{1,0:T(8,128)(2,1)S(1)}, u32[]{:S(2)}, u32[]{:S(2)}) collective-permute-start(bf16[64,2304]{1,0:T(8,128)(2,1)S(1)} %pad_maximum_fusion.2.refs_4_), channel_id=1, source_target_pairs={{0,2},{1,3},{2,0},{3,1},{4,6},{5,7},{6,4},{7,5},{8,10},{9,11},{10,... | collective-permute-start | bytes 884744 | tf_op jit(solution)/shard_map/ppermute | solution.py:33
  82.1 3.0 %collective-permute-start.21 = (bf16[64,2432]{1,0:T(8,128)(2,1)S(1)}, bf16[64,2432]{1,0:T(8,128)(2,1)S(1)}, u32[]{:S(2)}, u32[]{:S(2)}) collective-permute-start(bf16[64,2432]{1,0:T(8,128)(2,1)S(1)} %collective-permute-done.13.refs_1_), channel_id=1, source_target_pairs={{0,1},{1,0},{2,3},{3,2},{4,5},{5,4},{6,7},{7,6},{8,9},{9,8},{10,11... | collective-permute-start | bytes 933896 | tf_op jit(solution)/shard_map/ppermute | solution.py:33
  83.0 2.1 %collective-permute-start.22 = (bf16[64,2432]{1,0:T(8,128)(2,1)S(1)}, bf16[64,2432]{1,0:T(8,128)(2,1)S(1)}, u32[]{:S(2)}, u32[]{:S(2)}) collective-permute-start(bf16[64,2432]{1,0:T(8,128)(2,1)S(1)} %collective-permute-done.15.refs_3_), channel_id=1, source_target_pairs={{0,1},{1,0},{2,3},{3,2},{4,5},{5,4},{6,7},{7,6},{8,9},{9,8},{10,11... | collective-permute-start | bytes 933896 | tf_op jit(solution)/shard_map/ppermute | solution.py:33
  83.0 2.1 %collective-permute-start.23 = (bf16[64,2304]{1,0:T(8,128)(2,1)S(1)}, bf16[64,2304]{1,0:T(8,128)(2,1)S(1)}, u32[]{:S(2)}, u32[]{:S(2)}) collective-permute-start(bf16[64,2304]{1,0:T(8,128)(2,1)S(1)} %collective-permute-done.17.refs_5_), channel_id=1, source_target_pairs={{0,1},{1,0},{2,3},{3,2},{4,5},{5,4},{6,7},{7,6},{8,9},{9,8},{10,11... | collective-permute-start | bytes 884744 | tf_op jit(solution)/shard_map/ppermute | solution.py:33
  (3 other events, 20.5 us)

commit v5 on v4

--- a/solution.py
+++ b/solution.py
@@ -16,7 +16,6 @@
 large_vmem = 56 * 1024 * 1024
 x_size, z_size, core_size = 4, 2, 2
 tp_size = x_size * z_size * core_size
-stream_sets = 1
 
 
 flips = {"p": (1, 0, 0), "q": (3, 0, 0), "z": (0, 1, 0), "c": (0, 0, 1)}
@@ -163,7 +162,7 @@
         scratch_shapes=[pltpu.VMEM((heads, rows, latent), bf16)],
         compiler_params=pltpu.CompilerParams(vmem_limit_bytes=vmem_limit),
         cost_estimate=pl.CostEstimate(
-            flops=2 * rows * depth * latent, bytes_accessed=4 * rows * depth, transcendentals=0
+            flops=32 * rows * depth * latent, bytes_accessed=32 * rows * depth, transcendentals=0
         ),
         name="value_rows",
     )(order, arrived, value_weight)
@@ -224,8 +223,11 @@
             square = part * part if square is None else square + part * part
         gain = gain_ref[:, begin : begin + columns].astype(f32)
         scaled = (wide * gain).astype(bf16)
-        gate = jnp.dot(scaled, gate_ref[begin : begin + columns, :], preferred_element_type=f32)
-        up = jnp.dot(scaled, up_ref[begin : begin + columns, :], preferred_element_type=f32)
+        weights = jnp.concatenate(
+            [gate_ref[begin : begin + columns, :], up_ref[begin : begin + columns, :]], axis=1
+        )
+        product = jnp.dot(scaled, weights, preferred_element_type=f32)
+        gate, up = product[:, :hidden], product[:, hidden:]
         for i, (place, _, _) in enumerate(layout):
             rows = slice(i * block, (i + 1) * block)
             squares[place].append(square[rows])
@@ -340,7 +342,7 @@
         tiled=True,
     )
 
-    streams = ("pqz", "qzp", "zpq") * stream_sets
+    streams = ("pqz", "qzp", "zpq")
     each = range(len(streams))
     step = -(-width // (len(streams) * 128)) * 128
     spans = [(i * step, min(step, width - i * step)) for i in each]
@@ -399,7 +401,8 @@
         )
 
     carried = products(near, 0, None)
-    far, carried = lax.optimization_barrier((far, carried))
+    for i in each:
+        far[i], carried = lax.optimization_barrier((far[i], carried))
     activation = products(far, 1, carried)
     after_attention = jnp.concatenate([both[i][:block] for i in each], axis=1)
     return (after_attention.reshape(residual.shape), activation)

time: 89.8 us -> 89.6 us (level)
  Pallas kernels: 17.3 us -> 16.4 us
    pallas_call x2, Pallas kernels: 7.62 us -> 6.72 us  [gated(): pl.pallas_call(functools.partial(gated_kernel, spans, layouts, block, las...]
  transfers between devices with their start and end apart: 25 -> 25, of which waited for: 15 -> 16; matrix products, arithmetic and copies ran while one was open for 2% -> 2% of each run, Pallas kernels for 4% -> 3%
where the time goes in v5:
time: 89.6 us; the launch traced here: 89.4 us
  waiting for transfers between devices  40.5 us (45%)
  starting transfers between devices  26 us (29%)
  Pallas kernels  16.4 us (18%)
  local copies, waits for them, and re-layouts  3.66 us (4%)
  other arithmetic  1.81 us (2%)
  between operations  1.02 us (1%)
    ppermute x24, waiting for transfers between devices, send(): return lax.ppermute(value, 'tp', pairs)  24.9 us
    ppermute x24, starting transfers between devices, send(): return lax.ppermute(value, 'tp', pairs)  18.7 us
    all_to_all x1, waiting for transfers between devices, shards(): lax.all_to_all(attended.reshape(tp_size, heads // tp_size, block, latent)...  15.6 us
    all_to_all x1, starting transfers between devices, shards(): lax.all_to_all(attended.reshape(tp_size, heads // tp_size, block, latent)...  7.32 us
    pallas_call x2, Pallas kernels, gated(): pl.pallas_call(functools.partial(gated_kernel, spans, layouts, block, las...  6.72 us
    pallas_call x1, Pallas kernels, attention(): pl.pallas_call(functools.partial(attention_kernel, group, span, latent),...  6.56 us
    unnamed x20, local copies, waits for them, and re-layouts  3.42 us
    pallas_call x1, Pallas kernels, project(): pl.pallas_call(functools.partial(out_kernel, block, spans, orders), in_sp...  2.15 us
  transfers between devices with their start and end apart: 25, of which 16 were waited for; matrix products, arithmetic and copies ran while one was open for 2% of the time, Pallas kernels for 3%

profile of v5, /device:TPU:1, one launch (start us, length us, event | category | flops | bytes accessed | tf_op | source)
XLA Modules:
  0.0 89.4 jit_solution(14937418966541235443)
XLA Ops:
  0.6 6.6 %attention.1 = bf16[64,16,512]{2,1,0:T(8,128)(2,1)} custom-call(s32[2,8]{1,0:T(2,128)} %len_ref.1, s32[2,8]{1,0:T(2,128)} %pos_ref.1, bf16[16,64,576]{2,1,0:T(8,128)(2,1)} %bitcast.31, bf16[16,576,256]{2,1,0:T(8,128)(2,1)} %bitcast.29, bf16[16,576]{1,0:T(8,128)(2,1)} %bitcast.34, f32[1,64]{1,0:T(1,128)} %constant.167.clone.f_ref), custom_call_target="tpu_custom_call" | custom-call | flops 603979776 | bytes 5898240 | tf_op jit(solution)/shard_map/attention/pallas_call | solution.py:114
  7.2 7.3 %all-to-all-start = ((bf16[16,4,16,512]{3,2,1,0:T(8,128)(2,1)}), bf16[16,4,16,512]{3,2,1,0:T(8,128)(2,1)S(1)}, u32[]{:S(2)}, u32[]{:S(2)}) async-start(bf16[16,4,16,512]{3,2,1,0:T(8,128)(2,1)} %bitcast.30), calls=%async_computation | async-start | bytes 2097152 | tf_op jit(solution)/shard_map/all_to_all | solution.py:337
  14.6 15.6 %all-to-all-done.a_ref = bf16[16,4,16,512]{3,2,1,0:T(8,128)(2,1)S(1)} async-done(((bf16[16,4,16,512]{3,2,1,0:T(8,128)(2,1)}), bf16[16,4,16,512]{3,2,1,0:T(8,128)(2,1)S(1)}, u32[]{:S(2)}, u32[]{:S(2)}) %all-to-all-start) | async-done | bytes 1048608 | tf_op jit(solution)/shard_map/all_to_all | solution.py:337
  30.2 1.0 %value_rows.1.value_ref = bf16[256,512]{1,0:T(8,128)(2,1)S(1)} custom-call(s32[16]{0:T(128)S(1)} %stack.67.order_ref.refs_0_, bf16[16,4,16,512]{3,2,1,0:T(8,128)(2,1)S(1)} %all-to-all-done.a_ref, bf16[4,512,128]{2,1,0:T(8,128)(2,1)S(1)} %copy-done.1), custom_call_target="tpu_custom_call" | custom-call | flops 2147483648 | bytes 4194304 | tf_op jit(solution)/shard_map/value_rows/pallas_call | solution.py:157
  31.2 3.4 %copy-done = bf16[512,7168]{1,0:T(8,128)(2,1)S(1)} copy-done((bf16[512,7168]{1,0:T(8,128)(2,1)S(1)}, bf16[512,7168]{1,0:T(8,128)(2,1)}, u32[]{:S(2)}) %copy-start) | copy-done | bytes 7340056
  34.6 2.1 %out_proj.1 = (bf16[128,2432]{1,0:T(8,128)(2,1)S(1)}, bf16[128,2432]{1,0:T(8,128)(2,1)S(1)}, bf16[128,2432]{1,0:T(8,128)(2,1)S(1)}, bf16[128,2432]{1,0:T(8,128)(...) custom-call(bf16[256,512]{1,0:T(8,128)(2,1)S(1)} %value_rows.1.value_ref, ...), custom_call_target="tpu_custom_call" | custom-call | flops 1879048192 | bytes 7340032 | tf_op jit(solution)/shard_map/out_proj/pallas_call | solution.py:190
  36.7 1.0 %collective-permute-start.8 = (bf16[128,2304]{1,0:T(8,128)(2,1)S(1)}, bf16[128,2304]{1,0:T(8,128)(2,1)S(1)}, u32[]{:S(2)}, u32[]{:S(2)}) collective-permute-start(bf16[128,2304]{1,0:T(8,128)(2,1)S(1)} %get-tuple-element.24), channel_id=1, source_target_pairs={{0,1},{1,0},{2,3},{3,2},{4,5},{5,4},{6,7},{7,6},{8,9},{9,8},{10,11... | collective-permute-start | bytes 1769480 | tf_op jit(solution)/shard_map/ppermute | solution.py:32
  38.2 1.1 %collective-permute-done.8 = bf16[128,2304]{1,0:T(8,128)(2,1)S(1)} collective-permute-done((bf16[128,2304]{1,0:T(8,128)(2,1)S(1)}, bf16[128,2304]{1,0:T(8,128)(2,1)S(1)}, u32[]{:S(2)}, u32[]{:S(2)}) %collective-permute-start.8) | collective-permute-done | bytes 589856 | tf_op jit(solution)/shard_map/ppermute | solution.py:32
  40.5 0.6 collective-permute-done.4
  41.3 1.1 %collective-permute-start.5 = (bf16[64,2432]{1,0:T(8,128)(2,1)S(1)}, bf16[64,2432]{1,0:T(8,128)(2,1)S(1)}, u32[]{:S(2)}, u32[]{:S(2)}) collective-permute-start(bf16[64,2432]{1,0:T(8,128)(2,1)S(1)} %slice.147), channel_id=1, source_target_pairs={{0,12},{1,13},{2,14},{3,15},{4,8},{5,9},{6,10},{7,11},{8,4},{9,5},... | collective-permute-start | bytes 933896 | tf_op jit(solution)/shard_map/ppermute | solution.py:32
  42.5 5.3 %collective-permute-done.9 = bf16[64,2304]{1,0:T(8,128)(2,1)S(1)} collective-permute-done((bf16[64,2304]{1,0:T(8,128)(2,1)S(1)}, bf16[64,2304]{1,0:T(8,128)(2,1)S(1)}, u32[]{:S(2)}, u32[]{:S(2)}) %collective-permute-start.9) | collective-permute-done | bytes 294944 | tf_op jit(solution)/shard_map/ppermute | solution.py:32
  48.0 1.1 %collective-permute-done.1 = bf16[64,2432]{1,0:T(8,128)(2,1)S(1)} collective-permute-done((bf16[64,2432]{1,0:T(8,128)(2,1)S(1)}, bf16[64,2432]{1,0:T(8,128)(2,1)S(1)}, u32[]{:S(2)}, u32[]{:S(2)}) %collective-permute-start.1) | collective-permute-done | bytes 311328 | tf_op jit(solution)/shard_map/ppermute | solution.py:32
  49.2 0.7 collective-permute-start.2
  49.9 1.2 %collective-permute-done.5 = bf16[64,2432]{1,0:T(8,128)(2,1)S(1)} collective-permute-done((bf16[64,2432]{1,0:T(8,128)(2,1)S(1)}, bf16[64,2432]{1,0:T(8,128)(2,1)S(1)}, u32[]{:S(2)}, u32[]{:S(2)}) %collective-permute-start.5) | collective-permute-done | bytes 311328 | tf_op jit(solution)/shard_map/ppermute | solution.py:32
  51.4 0.6 collective-permute-done.10
  52.1 1.0 %collective-permute-start.11 = (bf16[32,2304]{1,0:T(8,128)(2,1)S(1)}, bf16[32,2304]{1,0:T(8,128)(2,1)S(1)}, u32[]{:S(2)}, u32[]{:S(2)}) collective-permute-start(bf16[32,2304]{1,0:T(8,128)(2,1)S(1)} %pad_maximum_fusion.7), channel_id=1, source_target_pairs={{0,12},{1,13},{2,14},{3,15},{4,8},{5,9},{6,10},{7,11},{8,4},{9,5},... | collective-permute-start | bytes 442376 | tf_op jit(solution)/shard_map/ppermute | solution.py:32
  53.1 2.6 %collective-permute-done.6 = bf16[32,2432]{1,0:T(8,128)(2,1)S(1)} collective-permute-done((bf16[32,2432]{1,0:T(8,128)(2,1)S(1)}, bf16[32,2432]{1,0:T(8,128)(2,1)S(1)}, u32[]{:S(2)}, u32[]{:S(2)}) %collective-permute-start.6) | collective-permute-done | bytes 155680 | tf_op jit(solution)/shard_map/ppermute | solution.py:32
  56.2 1.6 %collective-permute-done.11 = bf16[32,2304]{1,0:T(8,128)(2,1)S(1)} collective-permute-done((bf16[32,2304]{1,0:T(8,128)(2,1)S(1)}, bf16[32,2304]{1,0:T(8,128)(2,1)S(1)}, u32[]{:S(2)}, u32[]{:S(2)}) %collective-permute-start.11) | collective-permute-done | bytes 147488 | tf_op jit(solution)/shard_map/ppermute | solution.py:32
  58.0 2.4 %collective-permute-done.7 = bf16[32,2432]{1,0:T(8,128)(2,1)S(1)} collective-permute-done((bf16[32,2432]{1,0:T(8,128)(2,1)S(1)}, bf16[32,2432]{1,0:T(8,128)(2,1)S(1)}, u32[]{:S(2)}, u32[]{:S(2)}) %collective-permute-start.7) | collective-permute-done | bytes 155680 | tf_op jit(solution)/shard_map/ppermute | solution.py:32
  60.6 1.2 %collective-permute-start.12 = (bf16[32,2432]{1,0:T(8,128)(2,1)S(1)}, bf16[32,2432]{1,0:T(8,128)(2,1)S(1)}, u32[]{:S(2)}, u32[]{:S(2)}) collective-permute-start(bf16[32,2432]{1,0:T(8,128)(2,1)S(1)} %pad_maximum_fusion.5), channel_id=1, source_target_pairs={{0,12},{1,13},{2,14},{3,15},{4,8},{5,9},{6,10},{7,11},{8,4},{9,5},... | collective-permute-start | bytes 466952 | tf_op jit(solution)/shard_map/ppermute | solution.py:32
  61.8 1.5 %collective-permute-done.17 = bf16[32,2304]{1,0:T(8,128)(2,1)S(1)} collective-permute-done((bf16[32,2304]{1,0:T(8,128)(2,1)S(1)}, bf16[32,2304]{1,0:T(8,128)(2,1)S(1)}, u32[]{:S(2)}, u32[]{:S(2)}) %collective-permute-start.17) | collective-permute-done | bytes 147488 | tf_op jit(solution)/shard_map/ppermute | solution.py:32
  63.4 3.4 %collective-permute-start.18 = (bf16[64,2304]{1,0:T(8,128)(2,1)S(1)}, bf16[64,2304]{1,0:T(8,128)(2,1)S(1)}, u32[]{:S(2)}, u32[]{:S(2)}) collective-permute-start(bf16[64,2304]{1,0:T(8,128)(2,1)S(1)} %pad_maximum_fusion.2.refs_4_), channel_id=1, source_target_pairs={{0,1},{1,0},{2,3},{3,2},{4,5},{5,4},{6,7},{7,6},{8,9},{9,8},{10,11... | collective-permute-start | bytes 884744 | tf_op jit(solution)/shard_map/ppermute | solution.py:32
  66.8 3.0 %collective-permute-start.16 = (bf16[64,2432]{1,0:T(8,128)(2,1)S(1)}, bf16[64,2432]{1,0:T(8,128)(2,1)S(1)}, u32[]{:S(2)}, u32[]{:S(2)}) collective-permute-start(bf16[64,2432]{1,0:T(8,128)(2,1)S(1)} %pad_maximum_fusion.1.refs_2_), channel_id=1, source_target_pairs={{0,1},{1,0},{2,3},{3,2},{4,5},{5,4},{6,7},{7,6},{8,9},{9,8},{10,11... | collective-permute-start | bytes 933896 | tf_op jit(solution)/shard_map/ppermute | solution.py:32
  69.9 2.4 %collective-permute-start.14 = (bf16[64,2432]{1,0:T(8,128)(2,1)S(1)}, bf16[64,2432]{1,0:T(8,128)(2,1)S(1)}, u32[]{:S(2)}, u32[]{:S(2)}) collective-permute-start(bf16[64,2432]{1,0:T(8,128)(2,1)S(1)} %pad_maximum_fusion.refs_0_), channel_id=1, source_target_pairs={{0,1},{1,0},{2,3},{3,2},{4,5},{5,4},{6,7},{7,6},{8,9},{9,8},{10,11... | collective-permute-start | bytes 933896 | tf_op jit(solution)/shard_map/ppermute | solution.py:32
  72.3 0.7 collective-permute-start.20
  73.0 0.8 collective-permute-start.22
  73.9 2.7 %gated_near.1 = (f32[256,1280]{1,0:T(8,128)S(1)}, f32[256,128]{1,0:T(8,128)S(1)}) custom-call(bf16[64,2432]{1,0:T(8,128)(2,1)S(1)} %pad_maximum_fusion.refs_0_, bf16[64,2432]{1,0:T(8,128)(2,1)S(1)} %collective-permute-done.14.refs_1_, bf16[64,2432]{1,0:T(8,128)(2,1)S(1)} %pad_maximum_fusion.1.refs_2_, bf16[64,2432]{1,0:T(8,128)(2,1)S(1)} %collective-permute-done.16.refs_3_, ...), custom_call_target="tpu_custom_call" | custom-call | flops 2348810240 | bytes 18350080 | tf_op jit(solution)/shard_map/gated_near/pallas_call | solution.py:284
  76.6 4.6 %collective-permute-done.13.refs_1_ = bf16[64,2432]{1,0:T(8,128)(2,1)S(1)} collective-permute-done((bf16[64,2432]{1,0:T(8,128)(2,1)S(1)}, bf16[64,2432]{1,0:T(8,128)(2,1)S(1)}, u32[]{:S(2)}, u32[]{:S(2)}) %collective-permute-start.13) | collective-permute-done | bytes 311328 | tf_op jit(solution)/shard_map/ppermute | solution.py:32
  81.2 0.9 collective-permute-done.20.refs_3_
  82.1 1.2 %collective-permute-start.23 = (bf16[64,2304]{1,0:T(8,128)(2,1)S(1)}, bf16[64,2304]{1,0:T(8,128)(2,1)S(1)}, u32[]{:S(2)}, u32[]{:S(2)}) collective-permute-start(bf16[64,2304]{1,0:T(8,128)(2,1)S(1)} %collective-permute-done.22.refs_5_), channel_id=1, source_target_pairs={{0,1},{1,0},{2,3},{3,2},{4,5},{5,4},{6,7},{7,6},{8,9},{9,8},{10,11... | collective-permute-start | bytes 884744 | tf_op jit(solution)/shard_map/ppermute | solution.py:32
  83.8 0.7 maximum_bitcast_fusion
  85.3 4.0 %gated_far.1 = bf16[2,128,640]{2,1,0:T(8,128)(2,1)} custom-call(s32[16]{0:T(128)S(1)} %stack.67.order_ref.refs_0_, bf16[64,2432]{1,0:T(8,128)(2,1)S(1)} %collective-permute-done.13.refs_1_, bf16[64,2432]{1,0:T(8,128)(2,1)S(1)} %collective-permute-done.19.refs_2_, bf16[64,2432]{1,0:T(8,128)(2,1)S(1)} %collective-permute-done.20.refs_3_, ...), custom_call_target="tpu_custom_call" | custom-call | flops 2348810240 | bytes 18350080 | tf_op jit(solution)/shard_map/gated_far/pallas_call | solution.py:284
  (80 shorter events, 4.8 us)
Async XLA Ops:
  7.2 23.0 %copy-start.1 = (bf16[4,512,128]{2,1,0:T(8,128)(2,1)S(1)}, bf16[4,512,128]{2,1,0:T(8,128)(2,1)}, u32[]{:S(2)}) copy-start(bf16[4,512,128]{2,1,0:T(8,128)(2,1)} %v_ref.1) | copy-start | bytes 1572868
  7.2 23.0 %all-to-all-start = ((bf16[16,4,16,512]{3,2,1,0:T(8,128)(2,1)}), bf16[16,4,16,512]{3,2,1,0:T(8,128)(2,1)S(1)}, u32[]{:S(2)}, u32[]{:S(2)}) async-start(bf16[16,4,16,512]{3,2,1,0:T(8,128)(2,1)} %bitcast.30), calls=%async_computation | async-start | bytes 2097152 | tf_op jit(solution)/shard_map/all_to_all | solution.py:337
  30.2 43.6 %slice-start.3 = ((s8[9175040]{0:T(1024)(128)(4,1)}), s8[4194304]{0:T(1024)(128)(4,1)S(1)}, s32[]{:S(2)}) async-start(s8[9175040]{0:T(1024)(128)(4,1)} %bitcast.27), calls=%async_computation.4 | async-start | bytes 8388608
  34.6 39.3 %slice-start = ((s8[9175040]{0:T(1024)(128)(4,1)}), s8[4194304]{0:T(1024)(128)(4,1)S(1)}, s32[]{:S(2)}) async-start(s8[9175040]{0:T(1024)(128)(4,1)} %bitcast.25), calls=%async_computation.1 | async-start | bytes 8388608
  34.6 39.3 %slice-start.4 = ((s8[9175040]{0:T(1024)(128)(4,1)}), s8[4194304]{0:T(1024)(128)(4,1)S(1)}, s32[]{:S(2)}) async-start(s8[9175040]{0:T(1024)(128)(4,1)} %bitcast.27), calls=%async_computation.5 | async-start | bytes 8388608
  36.7 2.6 %collective-permute-start.8 = (bf16[128,2304]{1,0:T(8,128)(2,1)S(1)}, bf16[128,2304]{1,0:T(8,128)(2,1)S(1)}, u32[]{:S(2)}, u32[]{:S(2)}) collective-permute-start(bf16[128,2304]{1,0:T(8,128)(2,1)S(1)} %get-tuple-element.24), channel_id=1, source_target_pairs={{0,1},{1,0},{2,3},{3,2},{4,5},{5,4},{6,7},{7,6},{8,9},{9,8},{10,11... | collective-permute-start | bytes 1769480 | tf_op jit(solution)/shard_map/ppermute | solution.py:32
  37.7 2.5 %collective-permute-start = (bf16[128,2432]{1,0:T(8,128)(2,1)S(1)}, bf16[128,2432]{1,0:T(8,128)(2,1)S(1)}, u32[]{:S(2)}, u32[]{:S(2)}) collective-permute-start(bf16[128,2432]{1,0:T(8,128)(2,1)S(1)} %get-tuple-element.20), channel_id=1, source_target_pairs={{0,1},{1,0},{2,3},{3,2},{4,5},{5,4},{6,7},{7,6},{8,9},{9,8},{10,11... | collective-permute-start | bytes 1867784 | tf_op jit(solution)/shard_map/ppermute | solution.py:32
  37.8 3.3 %collective-permute-start.4 = (bf16[128,2432]{1,0:T(8,128)(2,1)S(1)}, bf16[128,2432]{1,0:T(8,128)(2,1)S(1)}, u32[]{:S(2)}, u32[]{:S(2)}) collective-permute-start(bf16[128,2432]{1,0:T(8,128)(2,1)S(1)} %get-tuple-element.22), channel_id=1, source_target_pairs={{0,1},{1,0},{2,3},{3,2},{4,5},{5,4},{6,7},{7,6},{8,9},{9,8},{10,11... | collective-permute-start | bytes 1867784 | tf_op jit(solution)/shard_map/ppermute | solution.py:32
  39.3 34.5 %slice-start.1 = ((s8[9175040]{0:T(1024)(128)(4,1)}), s8[4194304]{0:T(1024)(128)(4,1)S(1)}, s32[]{:S(2)}) async-start(s8[9175040]{0:T(1024)(128)(4,1)} %bitcast.25), calls=%async_computation.2 | async-start | bytes 8388608
  39.5 8.3 %collective-permute-start.9 = (bf16[64,2304]{1,0:T(8,128)(2,1)S(1)}, bf16[64,2304]{1,0:T(8,128)(2,1)S(1)}, u32[]{:S(2)}, u32[]{:S(2)}) collective-permute-start(bf16[64,2304]{1,0:T(8,128)(2,1)S(1)} %slice.155), channel_id=1, source_target_pairs={{0,2},{1,3},{2,0},{3,1},{4,6},{5,7},{6,4},{7,5},{8,10},{9,11},{10,... | collective-permute-start | bytes 884744 | tf_op jit(solution)/shard_map/ppermute | solution.py:32
  40.4 8.7 %collective-permute-start.1 = (bf16[64,2432]{1,0:T(8,128)(2,1)S(1)}, bf16[64,2432]{1,0:T(8,128)(2,1)S(1)}, u32[]{:S(2)}, u32[]{:S(2)}) collective-permute-start(bf16[64,2432]{1,0:T(8,128)(2,1)S(1)} %slice.139), channel_id=1, source_target_pairs={{0,4},{1,5},{2,6},{3,7},{4,0},{5,1},{6,2},{7,3},{8,12},{9,13},{10,... | collective-permute-start | bytes 933896 | tf_op jit(solution)/shard_map/ppermute | solution.py:32
  41.3 32.6 %slice-start.5 = ((s8[9175040]{0:T(1024)(128)(4,1)}), s8[786432]{0:T(1024)(128)(4,1)S(1)}, s32[]{:S(2)}) async-start(s8[9175040]{0:T(1024)(128)(4,1)} %bitcast.27), calls=%async_computation.6 | async-start | bytes 1572864
  41.3 9.9 %collective-permute-start.5 = (bf16[64,2432]{1,0:T(8,128)(2,1)S(1)}, bf16[64,2432]{1,0:T(8,128)(2,1)S(1)}, u32[]{:S(2)}, u32[]{:S(2)}) collective-permute-start(bf16[64,2432]{1,0:T(8,128)(2,1)S(1)} %slice.147), channel_id=1, source_target_pairs={{0,12},{1,13},{2,14},{3,15},{4,8},{5,9},{6,10},{7,11},{8,4},{9,5},... | collective-permute-start | bytes 933896 | tf_op jit(solution)/shard_map/ppermute | solution.py:32
  47.9 4.1 %collective-permute-start.10 = (bf16[32,2304]{1,0:T(8,128)(2,1)S(1)}, bf16[32,2304]{1,0:T(8,128)(2,1)S(1)}, u32[]{:S(2)}, u32[]{:S(2)}) collective-permute-start(bf16[32,2304]{1,0:T(8,128)(2,1)S(1)} %slice.157), channel_id=1, source_target_pairs={{0,4},{1,5},{2,6},{3,7},{4,0},{5,1},{6,2},{7,3},{8,12},{9,13},{10,... | collective-permute-start | bytes 442376 | tf_op jit(solution)/shard_map/ppermute | solution.py:32
  49.2 24.7 %slice-start.2 = ((s8[9175040]{0:T(1024)(128)(4,1)}), s8[786432]{0:T(1024)(128)(4,1)S(1)}, s32[]{:S(2)}) async-start(s8[9175040]{0:T(1024)(128)(4,1)} %bitcast.25), calls=%async_computation.3 | async-start | bytes 1572864
  49.2 6.6 %collective-permute-start.2 = (bf16[32,2432]{1,0:T(8,128)(2,1)S(1)}, bf16[32,2432]{1,0:T(8,128)(2,1)S(1)}, u32[]{:S(2)}, u32[]{:S(2)}) collective-permute-start(bf16[32,2432]{1,0:T(8,128)(2,1)S(1)} %slice.141), channel_id=1, source_target_pairs={{0,12},{1,13},{2,14},{3,15},{4,8},{5,9},{6,10},{7,11},{8,4},{9,5},... | collective-permute-start | bytes 466952 | tf_op jit(solution)/shard_map/ppermute | solution.py:32
  51.3 4.5 %collective-permute-start.6 = (bf16[32,2432]{1,0:T(8,128)(2,1)S(1)}, bf16[32,2432]{1,0:T(8,128)(2,1)S(1)}, u32[]{:S(2)}, u32[]{:S(2)}) collective-permute-start(bf16[32,2432]{1,0:T(8,128)(2,1)S(1)} %slice.149), channel_id=1, source_target_pairs={{0,2},{1,3},{2,0},{3,1},{4,6},{5,7},{6,4},{7,5},{8,10},{9,11},{10,... | collective-permute-start | bytes 466952 | tf_op jit(solution)/shard_map/ppermute | solution.py:32
  52.1 5.7 %collective-permute-start.11 = (bf16[32,2304]{1,0:T(8,128)(2,1)S(1)}, bf16[32,2304]{1,0:T(8,128)(2,1)S(1)}, u32[]{:S(2)}, u32[]{:S(2)}) collective-permute-start(bf16[32,2304]{1,0:T(8,128)(2,1)S(1)} %pad_maximum_fusion.7), channel_id=1, source_target_pairs={{0,12},{1,13},{2,14},{3,15},{4,8},{5,9},{6,10},{7,11},{8,4},{9,5},... | collective-permute-start | bytes 442376 | tf_op jit(solution)/shard_map/ppermute | solution.py:32
  55.9 4.5 %collective-permute-start.7 = (bf16[32,2432]{1,0:T(8,128)(2,1)S(1)}, bf16[32,2432]{1,0:T(8,128)(2,1)S(1)}, u32[]{:S(2)}, u32[]{:S(2)}) collective-permute-start(bf16[32,2432]{1,0:T(8,128)(2,1)S(1)} %pad_maximum_fusion.4), channel_id=1, source_target_pairs={{0,4},{1,5},{2,6},{3,7},{4,0},{5,1},{6,2},{7,3},{8,12},{9,13},{10,... | collective-permute-start | bytes 466952 | tf_op jit(solution)/shard_map/ppermute | solution.py:32
  56.0 4.6 %collective-permute-start.3 = (bf16[32,2432]{1,0:T(8,128)(2,1)S(1)}, bf16[32,2432]{1,0:T(8,128)(2,1)S(1)}, u32[]{:S(2)}, u32[]{:S(2)}) collective-permute-start(bf16[32,2432]{1,0:T(8,128)(2,1)S(1)} %pad_maximum_fusion.3), channel_id=1, source_target_pairs={{0,2},{1,3},{2,0},{3,1},{4,6},{5,7},{6,4},{7,5},{8,10},{9,11},{10,... | collective-permute-start | bytes 466952 | tf_op jit(solution)/shard_map/ppermute | solution.py:32
  57.9 5.5 %collective-permute-start.17 = (bf16[32,2304]{1,0:T(8,128)(2,1)S(1)}, bf16[32,2304]{1,0:T(8,128)(2,1)S(1)}, u32[]{:S(2)}, u32[]{:S(2)}) collective-permute-start(bf16[32,2304]{1,0:T(8,128)(2,1)S(1)} %pad_maximum_fusion.8), channel_id=1, source_target_pairs={{0,4},{1,5},{2,6},{3,7},{4,0},{5,1},{6,2},{7,3},{8,12},{9,13},{10,... | collective-permute-start | bytes 442376 | tf_op jit(solution)/shard_map/ppermute | solution.py:32
  60.4 6.4 %collective-permute-start.15 = (bf16[32,2432]{1,0:T(8,128)(2,1)S(1)}, bf16[32,2432]{1,0:T(8,128)(2,1)S(1)}, u32[]{:S(2)}, u32[]{:S(2)}) collective-permute-start(bf16[32,2432]{1,0:T(8,128)(2,1)S(1)} %pad_maximum_fusion.6), channel_id=1, source_target_pairs={{0,2},{1,3},{2,0},{3,1},{4,6},{5,7},{6,4},{7,5},{8,10},{9,11},{10,... | collective-permute-start | bytes 466952 | tf_op jit(solution)/shard_map/ppermute | solution.py:32
  60.6 9.2 %collective-permute-start.12 = (bf16[32,2432]{1,0:T(8,128)(2,1)S(1)}, bf16[32,2432]{1,0:T(8,128)(2,1)S(1)}, u32[]{:S(2)}, u32[]{:S(2)}) collective-permute-start(bf16[32,2432]{1,0:T(8,128)(2,1)S(1)} %pad_maximum_fusion.5), channel_id=1, source_target_pairs={{0,12},{1,13},{2,14},{3,15},{4,8},{5,9},{6,10},{7,11},{8,4},{9,5},... | collective-permute-start | bytes 466952 | tf_op jit(solution)/shard_map/ppermute | solution.py:32
  63.4 9.6 %collective-permute-start.18 = (bf16[64,2304]{1,0:T(8,128)(2,1)S(1)}, bf16[64,2304]{1,0:T(8,128)(2,1)S(1)}, u32[]{:S(2)}, u32[]{:S(2)}) collective-permute-start(bf16[64,2304]{1,0:T(8,128)(2,1)S(1)} %pad_maximum_fusion.2.refs_4_), channel_id=1, source_target_pairs={{0,1},{1,0},{2,3},{3,2},{4,5},{5,4},{6,7},{7,6},{8,9},{9,8},{10,11... | collective-permute-start | bytes 884744 | tf_op jit(solution)/shard_map/ppermute | solution.py:32
  66.8 7.0 %collective-permute-start.16 = (bf16[64,2432]{1,0:T(8,128)(2,1)S(1)}, bf16[64,2432]{1,0:T(8,128)(2,1)S(1)}, u32[]{:S(2)}, u32[]{:S(2)}) collective-permute-start(bf16[64,2432]{1,0:T(8,128)(2,1)S(1)} %pad_maximum_fusion.1.refs_2_), channel_id=1, source_target_pairs={{0,1},{1,0},{2,3},{3,2},{4,5},{5,4},{6,7},{7,6},{8,9},{9,8},{10,11... | collective-permute-start | bytes 933896 | tf_op jit(solution)/shard_map/ppermute | solution.py:32
  69.9 4.0 %collective-permute-start.14 = (bf16[64,2432]{1,0:T(8,128)(2,1)S(1)}, bf16[64,2432]{1,0:T(8,128)(2,1)S(1)}, u32[]{:S(2)}, u32[]{:S(2)}) collective-permute-start(bf16[64,2432]{1,0:T(8,128)(2,1)S(1)} %pad_maximum_fusion.refs_0_), channel_id=1, source_target_pairs={{0,1},{1,0},{2,3},{3,2},{4,5},{5,4},{6,7},{7,6},{8,9},{9,8},{10,11... | collective-permute-start | bytes 933896 | tf_op jit(solution)/shard_map/ppermute | solution.py:32
  72.3 8.9 %collective-permute-start.13 = (bf16[64,2432]{1,0:T(8,128)(2,1)S(1)}, bf16[64,2432]{1,0:T(8,128)(2,1)S(1)}, u32[]{:S(2)}, u32[]{:S(2)}) collective-permute-start(bf16[64,2432]{1,0:T(8,128)(2,1)S(1)} %pad_maximum_fusion.refs_0_), channel_id=1, source_target_pairs={{0,4},{1,5},{2,6},{3,7},{4,0},{5,1},{6,2},{7,3},{8,12},{9,13},{10,... | collective-permute-start | bytes 933896 | tf_op jit(solution)/shard_map/ppermute | solution.py:32
  72.3 9.8 %collective-permute-start.20 = (bf16[64,2432]{1,0:T(8,128)(2,1)S(1)}, bf16[64,2432]{1,0:T(8,128)(2,1)S(1)}, u32[]{:S(2)}, u32[]{:S(2)}) collective-permute-start(bf16[64,2432]{1,0:T(8,128)(2,1)S(1)} %pad_maximum_fusion.1.refs_2_), channel_id=1, source_target_pairs={{0,12},{1,13},{2,14},{3,15},{4,8},{5,9},{6,10},{7,11},{8,4},{9,5},... | collective-permute-start | bytes 933896 | tf_op jit(solution)/shard_map/ppermute | solution.py:32
  73.0 9.1 %collective-permute-start.22 = (bf16[64,2304]{1,0:T(8,128)(2,1)S(1)}, bf16[64,2304]{1,0:T(8,128)(2,1)S(1)}, u32[]{:S(2)}, u32[]{:S(2)}) collective-permute-start(bf16[64,2304]{1,0:T(8,128)(2,1)S(1)} %pad_maximum_fusion.2.refs_4_), channel_id=1, source_target_pairs={{0,2},{1,3},{2,0},{3,1},{4,6},{5,7},{6,4},{7,5},{8,10},{9,11},{10,... | collective-permute-start | bytes 884744 | tf_op jit(solution)/shard_map/ppermute | solution.py:32
  82.1 2.4 %collective-permute-start.23 = (bf16[64,2304]{1,0:T(8,128)(2,1)S(1)}, bf16[64,2304]{1,0:T(8,128)(2,1)S(1)}, u32[]{:S(2)}, u32[]{:S(2)}) collective-permute-start(bf16[64,2304]{1,0:T(8,128)(2,1)S(1)} %collective-permute-done.22.refs_5_), channel_id=1, source_target_pairs={{0,1},{1,0},{2,3},{3,2},{4,5},{5,4},{6,7},{7,6},{8,9},{9,8},{10,11... | collective-permute-start | bytes 884744 | tf_op jit(solution)/shard_map/ppermute | solution.py:32
  83.2 1.7 %collective-permute-start.21 = (bf16[64,2432]{1,0:T(8,128)(2,1)S(1)}, bf16[64,2432]{1,0:T(8,128)(2,1)S(1)}, u32[]{:S(2)}, u32[]{:S(2)}) collective-permute-start(bf16[64,2432]{1,0:T(8,128)(2,1)S(1)} %collective-permute-done.20.refs_3_), channel_id=1, source_target_pairs={{0,1},{1,0},{2,3},{3,2},{4,5},{5,4},{6,7},{7,6},{8,9},{9,8},{10,11... | collective-permute-start | bytes 933896 | tf_op jit(solution)/shard_map/ppermute | solution.py:32
  83.3 2.1 %collective-permute-start.19 = (bf16[64,2432]{1,0:T(8,128)(2,1)S(1)}, bf16[64,2432]{1,0:T(8,128)(2,1)S(1)}, u32[]{:S(2)}, u32[]{:S(2)}) collective-permute-start(bf16[64,2432]{1,0:T(8,128)(2,1)S(1)} %collective-permute-done.13.refs_1_), channel_id=1, source_target_pairs={{0,1},{1,0},{2,3},{3,2},{4,5},{5,4},{6,7},{7,6},{8,9},{9,8},{10,11... | collective-permute-start | bytes 933896 | tf_op jit(solution)/shard_map/ppermute | solution.py:32
  (3 other events, 19.6 us)
